TPU v7x, 32 devices: a whole 2x2x4 slice. The times are simulated.
32 devices in a mesh: dp: 16 (over z, x, core), mp: 2 (over y).
Axes of the slice: x: 2, y: 2, z: 4, core: 2. Of those that a mesh axis runs over, the one named last changes fastest.
Arguments:
- hidden_in: bfloat16 [32, 512, 768], P('dp', 'mp'), may hold values from -6 to 6
- cotangent: bfloat16 [32, 512, 768], P('dp', 'mp'), may hold values from -6 to 6
- segment_ids: int32 [32, 512], P('dp'), may hold values from 0 to 7, as said below
- clip_ranges: int32 [2, 4], replicated, may hold values from 1 to 3
- w_qkv: bfloat16 [2, 3, 768, 768], P(None, None, None, 'mp'), may hold values from -0.21875 to 0.21875
- bias_qv: float32 [2, 2, 768], P(None, None, 'mp'), may hold values from -1.2 to 1.2
- w_out: bfloat16 [2, 768, 768], P(None, 'mp'), may hold values from -0.875 to 0.875
- vector_bias: float32 [2, 4, 768], replicated, may hold values from -1.2 to 1.2
- ln_gain: float32 [2, 2, 768], replicated, may hold values from 0.5 to 1.5
- w_up: bfloat16 [2, 768, 3072], replicated, may hold values from -0.21875 to 0.21875
- bias_up: float32 [2, 3072], replicated, may hold values from -1.2 to 1.2
- w_down: bfloat16 [2, 3072, 768], replicated, may hold values from -0.109375 to 0.109375
Outputs:
- hidden_out: bfloat16 [32, 512, 768], P('dp', 'mp')
- grad_input: float32 [32, 512, 768], P('dp', 'mp')
- grad_qkv: float32 [2, 12, 147456], P(None, 'mp', 'dp')
- grad_bias_qv: float32 [2, 2, 768], P(None, None, 'mp')
- grad_out: float32 [2, 12, 49152], P(None, 'mp', 'dp')
- grad_vector_bias: float32 [2, 4, 768], replicated
- grad_ln_gain: float32 [2, 2, 768], replicated
- grad_up: float32 [2, 2359296], P(None, 'dp')
- grad_bias_up: float32 [2, 3072], replicated
- grad_down: float32 [2, 2359296], P(None, 'dp')
Inputs may be any that keep to these rules, and one draw needn't show every extreme that they name: `segment_ids`: in each row the ids start at 0, never fall, and rise by one at each of 7 distinct positions; none of these lies within 64 positions of the row's middle, so one example spans both halves of every row.
All inputs are finite; a program needn't handle non-finite values.
Results may differ from a plain program's by a relative error of at most 0.023.
Values may be sent and summed in bfloat16 or wider, within the bound.
No kernel may reach another device: no remote copies, remote signals or barrier semaphores. Data moves between devices by JAX's collectives and lax.ppermute only.
A program may use at most 256 MiB of HBM per device.

v0:
```python
import jax
import jax.numpy as jnp
from jax import lax
from jax.sharding import PartitionSpec as P

HEAD = 64


epsilon = 1e-06


def layer_norm(entries, gain_vec, shift_vec):
    centred = entries - jnp.mean(entries, axis=-1, keepdims=True)
    spread = jnp.mean(centred * centred, axis=-1, keepdims=True)
    return centred * lax.rsqrt(spread + epsilon) * gain_vec + shift_vec


def clipped(entries, clip_limit):
    return clip_limit * jnp.tanh(entries / clip_limit)


def local(
    hidden_in,
    cotangent,
    segment_ids,
    clip_ranges,
    w_qkv,
    bias_qv,
    w_out,
    vector_bias,
    ln_gain,
    w_up,
    bias_up,
    w_down,
):
    layer_count = w_qkv.shape[0]
    row_count = hidden_in.shape[0]
    seq_len = segment_ids.shape[1]
    local_width = w_qkv.shape[3]
    local_heads = local_width // HEAD
    score_scale = HEAD ** (-0.5)
    clip_bounds = clip_ranges.astype(jnp.float32)
    same_doc = (segment_ids[:, :, None] == segment_ids[:, None, :])[:, None]
    bf16 = jnp.bfloat16
    f32 = jnp.float32
    dp_count = lax.axis_size("dp")

    def split_heads(tensor):
        return tensor.reshape(row_count, seq_len, local_heads, HEAD)

    def masked_scores(query_heads, key_heads):
        scores = (
            jnp.einsum("rqhd,rkhd->rhqk", query_heads, key_heads, preferred_element_type=f32)
            * score_scale
        )
        return jnp.where(same_doc, scores, -1e30)

    hidden = hidden_in.astype(f32)
    stored = []
    for layer_index in range(layer_count):
        quant_in = clipped(hidden, clip_bounds[layer_index, 0]).astype(bf16)
        gathered = lax.all_gather(quant_in, "mp", axis=1, tiled=True)
        projected = jnp.einsum(
            "rsd,pde->prse", gathered, w_qkv[layer_index], preferred_element_type=f32
        )
        queries = (projected[0] + bias_qv[layer_index, 0]).astype(bf16)
        key_rows = projected[1].astype(bf16)
        value_rows = (projected[2] + bias_qv[layer_index, 1]).astype(bf16)
        masked = masked_scores(split_heads(queries), split_heads(key_rows))
        row_max = jnp.max(masked, axis=-1, keepdims=True)
        log_total = row_max + jnp.log(jnp.sum(jnp.exp(masked - row_max), axis=-1, keepdims=True))
        weights = jnp.exp(masked - log_total).astype(bf16)
        context = jnp.einsum(
            "rhqk,rkhd->rqhd", weights, split_heads(value_rows), preferred_element_type=f32
        ).reshape(row_count, seq_len, local_width)
        quant_ctx = clipped(context, clip_bounds[layer_index, 1]).astype(bf16)
        partial_out = jnp.einsum(
            "rsc,cd->rsd", quant_ctx, w_out[layer_index], preferred_element_type=f32
        )
        attn_out = (
            lax.psum_scatter(partial_out, "mp", scatter_dimension=1, tiled=True)
            + vector_bias[layer_index, 0]
        )
        summed = hidden + attn_out
        normed = layer_norm(summed, ln_gain[layer_index, 0], vector_bias[layer_index, 1])
        quant_ff = clipped(normed, clip_bounds[layer_index, 2]).astype(bf16)
        inner_pre = (
            jnp.einsum("rsd,df->rsf", quant_ff, w_up[layer_index], preferred_element_type=f32)
            + bias_up[layer_index]
        )
        quant_act = clipped(
            jax.nn.gelu(inner_pre, approximate=False), clip_bounds[layer_index, 3]
        ).astype(bf16)
        summed_ff = normed + (
            jnp.einsum("rsf,fd->rsd", quant_act, w_down[layer_index], preferred_element_type=f32)
            + vector_bias[layer_index, 2]
        )
        stored.append(
            (
                hidden,
                gathered,
                queries,
                key_rows,
                value_rows,
                log_total,
                context,
                quant_ctx,
                summed,
                normed,
                quant_ff,
                inner_pre,
                quant_act,
                summed_ff,
            )
        )
        hidden = layer_norm(summed_ff, ln_gain[layer_index, 1], vector_bias[layer_index, 3])
    hidden_out = hidden.astype(bf16)
    grad_hidden = cotangent.astype(f32)
    qkv_list, bqv_list, out_list, vec_list, gain_list, up_list, bup_list, down_list = (
        [],
        [],
        [],
        [],
        [],
        [],
        [],
        [],
    )
    for layer_index in reversed(range(layer_count)):
        (
            hidden_prev,
            gathered,
            queries,
            key_rows,
            value_rows,
            log_total,
            context,
            quant_ctx,
            summed,
            normed,
            quant_ff,
            inner_pre,
            quant_act,
            summed_ff,
        ) = stored[layer_index]
        in_limit = clip_bounds[layer_index, 0]
        ctx_limit = clip_bounds[layer_index, 1]
        ff_limit = clip_bounds[layer_index, 2]
        act_limit = clip_bounds[layer_index, 3]
        _, norm_back = jax.vjp(
            layer_norm, summed_ff, ln_gain[layer_index, 1], vector_bias[layer_index, 3]
        )
        d_summed_ff, d_gain_ff, d_shift_ff = norm_back(grad_hidden)
        d_branch = d_summed_ff.astype(bf16)
        grad_down_w = jnp.einsum("rsf,rsd->fd", quant_act, d_branch, preferred_element_type=f32)
        d_quant_act = jnp.einsum(
            "rsd,fd->rsf", d_branch, w_down[layer_index], preferred_element_type=f32
        )
        _, act_back = jax.vjp(
            lambda entries: clipped(jax.nn.gelu(entries, approximate=False), act_limit), inner_pre
        )
        d_inner = act_back(d_quant_act)[0].astype(bf16)
        grad_up_w = jnp.einsum("rsd,rsf->df", quant_ff, d_inner, preferred_element_type=f32)
        d_quant_ff = jnp.einsum(
            "rsf,df->rsd", d_inner, w_up[layer_index], preferred_element_type=f32
        )
        _, ff_back = jax.vjp(lambda entries: clipped(entries, ff_limit), normed)
        d_normed = d_summed_ff + ff_back(d_quant_ff)[0]
        _, attn_norm_back = jax.vjp(
            layer_norm, summed, ln_gain[layer_index, 0], vector_bias[layer_index, 1]
        )
        d_summed, d_gain_attn, d_shift_attn = attn_norm_back(d_normed)
        d_attn = d_summed.astype(bf16)
        d_attn_rows = lax.all_gather(d_attn, "mp", axis=1, tiled=True)
        grad_out_w = jnp.einsum("rsc,rsd->cd", quant_ctx, d_attn_rows, preferred_element_type=f32)
        d_quant_ctx = jnp.einsum(
            "rsd,cd->rsc", d_attn_rows, w_out[layer_index], preferred_element_type=f32
        )
        _, ctx_back = jax.vjp(lambda entries: clipped(entries, ctx_limit), context)
        d_context = split_heads(ctx_back(d_quant_ctx)[0].astype(bf16))
        query_heads = split_heads(queries)
        key_heads = split_heads(key_rows)
        value_heads = split_heads(value_rows)
        soft_probs = jnp.exp(masked_scores(query_heads, key_heads) - log_total)
        d_values = jnp.einsum(
            "rhqk,rqhd->rkhd", soft_probs.astype(bf16), d_context, preferred_element_type=f32
        )
        d_weights = jnp.einsum(
            "rqhd,rkhd->rhqk", d_context, value_heads, preferred_element_type=f32
        )
        row_delta = jnp.sum(d_weights * soft_probs, axis=-1, keepdims=True)
        d_scores = (soft_probs * (d_weights - row_delta)).astype(bf16)
        d_queries = (
            jnp.einsum("rhqk,rkhd->rqhd", d_scores, key_heads, preferred_element_type=f32)
            * score_scale
        )
        d_keys = (
            jnp.einsum("rhqk,rqhd->rkhd", d_scores, query_heads, preferred_element_type=f32)
            * score_scale
        )
        d_projected = (
            jnp.stack([d_queries, d_keys, d_values])
            .reshape(3, row_count, seq_len, local_width)
            .astype(bf16)
        )
        grad_qkv_w = jnp.einsum("rsd,prse->pde", gathered, d_projected, preferred_element_type=f32)
        d_bias_qv = jnp.sum(d_projected[0::2], axis=(1, 2), dtype=f32)
        d_gathered = jnp.einsum(
            "prse,pde->rsd", d_projected, w_qkv[layer_index], preferred_element_type=f32
        )
        d_quant_in = lax.psum_scatter(d_gathered, "mp", scatter_dimension=1, tiled=True)
        _, in_back = jax.vjp(lambda entries: clipped(entries, in_limit), hidden_prev)
        grad_hidden = d_summed + in_back(d_quant_in)[0]
        d_gains = jnp.stack([d_gain_attn, d_gain_ff])
        d_vectors = jnp.stack(
            [
                jnp.sum(d_attn, axis=(0, 1), dtype=f32),
                d_shift_attn,
                jnp.sum(d_branch, axis=(0, 1), dtype=f32),
                d_shift_ff,
            ]
        )
        d_bias_up = jnp.sum(d_inner, axis=(0, 1), dtype=f32)
        d_bias_qv, d_gains, d_vectors, d_bias_up = lax.psum(
            (d_bias_qv, d_gains, d_vectors, d_bias_up), "dp"
        )
        qkv_flat = (
            grad_qkv_w.reshape(3, grad_qkv_w.shape[1], local_heads, HEAD)
            .transpose(2, 0, 1, 3)
            .reshape(local_heads, -1)
        )
        out_flat = grad_out_w.reshape(local_heads, -1)
        up_grid = grad_up_w.reshape(dp_count, -1)
        down_grid = grad_down_w.reshape(dp_count, -1)
        up_half, down_half = (
            lax.psum_scatter(up_grid, "mp", scatter_dimension=1, tiled=True),
            lax.psum_scatter(down_grid, "mp", scatter_dimension=1, tiled=True),
        )
        qkv_part, out_part, up_half, down_half = (
            lax.psum_scatter(qkv_flat, "dp", scatter_dimension=1, tiled=True),
            lax.psum_scatter(out_flat, "dp", scatter_dimension=1, tiled=True),
            lax.psum_scatter(up_half, "dp", scatter_dimension=0, tiled=True),
            lax.psum_scatter(down_half, "dp", scatter_dimension=0, tiled=True),
        )
        up_joined, down_joined = (
            lax.all_gather(up_half, "mp", axis=1, tiled=True),
            lax.all_gather(down_half, "mp", axis=1, tiled=True),
        )
        up_part = up_joined.reshape(-1)
        down_part = down_joined.reshape(-1)
        d_gains, d_vectors, d_bias_up = lax.psum((d_gains, d_vectors, d_bias_up), "mp")
        qkv_list.append(qkv_part)
        bqv_list.append(d_bias_qv)
        out_list.append(out_part)
        vec_list.append(d_vectors)
        gain_list.append(d_gains)
        up_list.append(up_part)
        bup_list.append(d_bias_up)
        down_list.append(down_part)
    return (
        hidden_out,
        grad_hidden,
        jnp.stack(qkv_list[::-1]),
        jnp.stack(bqv_list[::-1]),
        jnp.stack(out_list[::-1]),
        jnp.stack(vec_list[::-1]),
        jnp.stack(gain_list[::-1]),
        jnp.stack(up_list[::-1]),
        jnp.stack(bup_list[::-1]),
        jnp.stack(down_list[::-1]),
    )


def solution(mesh):
    return jax.shard_map(
        local,
        mesh=mesh,
        in_specs=(
            P("dp", "mp", None),
            P("dp", "mp", None),
            P("dp", None),
            P(),
            P(None, None, None, "mp"),
            P(None, None, "mp"),
            P(None, "mp", None),
            P(),
            P(),
            P(),
            P(),
            P(),
        ),
        out_specs=(
            P("dp", "mp", None),
            P("dp", "mp", None),
            P(None, "mp", "dp"),
            P(None, None, "mp"),
            P(None, "mp", "dp"),
            P(),
            P(),
            P(None, "dp"),
            P(),
            P(None, "dp"),
        ),
        check_vma=False,
    )
```

profile of v0, /device:TPU:0, one launch (start us, length us, event | category | flops | bytes accessed | tf_op | source)
XLA Modules:
  0.0 1717.1 jit_solution(10423435748773751701)
XLA Ops:
  8.6 2.8 multiply_convert_fusion.13
  13.6 27.9 %all-gather.5.cloned.1.call-done = bf16[2,512,768]{2,1,0:T(8,128)(2,1)} async-done(((bf16[2,256,768]{2,1,0:T(8,128)(2,1)}), bf16[2,512,768]{2,1,0:T(8,128)(2,1)}) %all-gather.5.cloned.1.call-update) | async-done | bytes 1572880 | tf_op jit(solution)/shard_map/all_gather | solution.py:62
  41.5 4.0 convolution_bitcast_fusion.5
  54.1 6.7 subtract_multiply_fusion
  61.7 2.7 fusion.73
  65.1 42.8 %reduce-scatter.13.cloned.1.call-done = f32[2,256,768]{2,1,0:T(8,128)} async-done(((f32[2,512,768]{2,1,0:T(8,128)}), f32[2,256,768]{2,1,0:T(8,128)}) %reduce-scatter.13.cloned.1.call-update) | async-done | bytes 1572880 | tf_op jit(solution)/shard_map/reduce_scatter | solution.py:81
  110.1 22.5 %multiply_convert_fusion.3 = (bf16[2,256,3072]{2,1,0:T(8,128)(2,1)S(1)}, f32[2,256,3072]{2,1,0:T(8,128)}, f32[2,256,3072]{2,1,0:T(8,128)}) fusion(f32[3072]{0:T(1024)S(1)} %bitcast.271, f32[]{:T(128)} %bitcast.14, bf16[2,768,3072]{2,1,0:T(8,128)(2,1)} %param.21, f32[]{:T(128)} %bitcast.15, f32[768]{0:T(1024)S(1)} %get-tuple-element.49, ...), kind=kOutput, calls=%fused_computation.36 | convolution fusion | flops 2525626368 | bytes 22043648 | tf_op jit(solution)/shard_map/rsd,df->rsf/dot_general | solution.py:88
  132.7 2.8 fusion.103
  139.0 27.0 %all-gather.7.cloned.1.call-done = bf16[2,512,768]{2,1,0:T(8,128)(2,1)} async-done(((bf16[2,256,768]{2,1,0:T(8,128)(2,1)}), bf16[2,512,768]{2,1,0:T(8,128)(2,1)}) %all-gather.7.cloned.1.call-update) | async-done | bytes 1572880 | tf_op jit(solution)/shard_map/all_gather | solution.py:62
  166.0 4.0 convolution_bitcast_fusion.4
  178.5 6.7 subtract_multiply_fusion.1
  186.0 2.6 fusion.70
  188.9 43.2 %reduce-scatter.15.cloned.1.call-done = f32[2,256,768]{2,1,0:T(8,128)} async-done(((f32[2,512,768]{2,1,0:T(8,128)}), f32[2,256,768]{2,1,0:T(8,128)}) %reduce-scatter.15.cloned.1.call-update) | async-done | bytes 1572880 | tf_op jit(solution)/shard_map/reduce_scatter | solution.py:81
  235.1 23.0 %multiply_convert_fusion.2 = (bf16[2,256,3072]{2,1,0:T(8,128)(2,1)S(1)}, f32[2,256,3072]{2,1,0:T(8,128)}, f32[2,256,3072]{2,1,0:T(8,128)}) fusion(f32[3072]{0:T(1024)S(1)} %bitcast.273, f32[]{:T(128)} %bitcast.35, bf16[2,768,3072]{2,1,0:T(8,128)(2,1)} %param.21, f32[]{:T(128)} %bitcast.36, f32[768]{0:T(1024)S(1)} %get-tuple-element.45, ...), kind=kOutput, calls=%fused_computation.22 | convolution fusion | flops 2525626368 | bytes 22043648 | tf_op jit(solution)/shard_map/rsd,df->rsf/dot_general | solution.py:88
  258.2 2.8 fusion.104
  265.1 12.4 convert_reduce_fusion
  277.5 6.2 multiply_reduce_fusion.2
  286.7 27.3 %all-gather.9.cloned.1.call-done = bf16[2,512,768]{2,1,0:T(8,128)(2,1)} async-done(((bf16[2,256,768]{2,1,0:T(8,128)(2,1)}), bf16[2,512,768]{2,1,0:T(8,128)(2,1)}) %all-gather.9.cloned.1.call-update) | async-done | bytes 1572880 | tf_op jit(solution)/shard_map/all_gather | solution.py:174
  314.1 3.9 fusion.50
  318.0 7.5 convolution_convert_fusion.1
  325.5 7.2 multiply_reduce_fusion.1
  332.8 7.2 multiply_convert_fusion.1
  340.0 2.9 multiply_convert_fusion.6
  350.8 5.6 convolution_bitcast_fusion.7
  356.5 43.4 %reduce-scatter.17.cloned.1.call-done = f32[2,256,768]{2,1,0:T(8,128)} async-done(((f32[2,512,768]{2,1,0:T(8,128)}), f32[2,256,768]{2,1,0:T(8,128)}) %reduce-scatter.17.cloned.1.call-update) | async-done | bytes 1572880 | tf_op jit(solution)/shard_map/reduce_scatter | solution.py:211
  400.0 3.8 multiply_reduce_fusion.3
  406.4 12.2 convert_reduce_fusion.1
  418.7 4.0 multiply_reduce_fusion.4
  425.6 9.6 convolution_bitcast_fusion.2
  435.2 10.6 reshape.292
  446.3 8.3 convolution_bitcast_fusion
  454.6 11.5 reshape.294
  466.2 9.3 convolution_bitcast_fusion.3
  475.5 10.7 reshape.291
  486.3 8.3 convolution_bitcast_fusion.1
  494.6 10.7 reshape.293
  509.7 3.5 fusion.48
  513.2 6.9 convolution_convert_fusion
  520.6 10.2 multiply_reduce_fusion
  530.8 7.2 multiply_convert_fusion
  543.6 5.7 multiply_convert_fusion.4
  560.6 4.2 fusion.51
  564.8 4.3 copy.103
  569.1 7.3 reshape.288
  576.4 4.2 fusion.54
  580.7 4.3 copy.101
  585.0 7.3 reshape.286
  593.9 5.5 convolution_bitcast_fusion.6
  599.5 79.4 %reduce-scatter.35.cloned.1.call-done = f32[16,73728]{1,0:T(8,128)} async-done(((f32[16,147456]{1,0:T(8,128)}), f32[16,73728]{1,0:T(8,128)}) %reduce-scatter.35.cloned.1.call-update) | async-done | bytes 4718608 | tf_op jit(solution)/shard_map/reduce_scatter | solution.py:237
  678.9 112.9 %reduce-scatter.29.cloned.1.call-done = f32[16,73728]{1,0:T(8,128)} async-done(((f32[16,147456]{1,0:T(8,128)}), f32[16,73728]{1,0:T(8,128)}) %reduce-scatter.29.cloned.1.call-update) | async-done | bytes 4718608 | tf_op jit(solution)/shard_map/reduce_scatter | solution.py:236
  791.8 113.0 %reduce-scatter.33.cloned.1.call-done = f32[16,73728]{1,0:T(8,128)} async-done(((f32[16,147456]{1,0:T(8,128)}), f32[16,73728]{1,0:T(8,128)}) %reduce-scatter.33.cloned.1.call-update) | async-done | bytes 4718608 | tf_op jit(solution)/shard_map/reduce_scatter | solution.py:237
  906.1 91.3 %all-reduce.10.cloned.1.call-done = (f32[1,2,384]{2,1,0:T(2,128)}, f32[1,2,384]{2,1,0:T(2,128)}, f32[4,768]{1,0:T(4,128)}, f32[4,768]{1,0:T(4,128)}, f32[2,768]{...) async-done(((f32[1,2,384]{2,1,0:T(2,128)}, f32[1,2,384]{2,1,0:T(2,128)}, f32[4,768]{1,0:T(4,128)}, f32[4,768]{1,0:T(4,128)}, f32[2,768]{1,0:T(2,128)}, ...) | async-done | bytes 67600 | tf_op jit(solution)/shard_map/psum | solution.py:224
  997.3 9.4 all-reduce.6
  1009.9 52.7 %reduce-scatter.27.cloned.1.call-done = f32[6,3072]{1,0:T(8,128)} async-done(((f32[6,49152]{1,0:T(8,128)}), f32[6,3072]{1,0:T(8,128)}) %reduce-scatter.27.cloned.1.call-update) | async-done | bytes 73744 | tf_op jit(solution)/shard_map/reduce_scatter | solution.py:241
  1062.7 62.4 %reduce-scatter.25.cloned.1.call-done = f32[6,3072]{1,0:T(8,128)} async-done(((f32[6,49152]{1,0:T(8,128)}), f32[6,3072]{1,0:T(8,128)}) %reduce-scatter.25.cloned.1.call-update) | async-done | bytes 73744 | tf_op jit(solution)/shard_map/reduce_scatter | solution.py:241
  1126.9 76.6 %reduce-scatter.23.cloned.1.call-done = f32[6,9216]{1,0:T(8,128)} async-done(((f32[6,147456]{1,0:T(8,128)}), f32[6,9216]{1,0:T(8,128)}) %reduce-scatter.23.cloned.1.call-update) | async-done | bytes 221200 | tf_op jit(solution)/shard_map/reduce_scatter | solution.py:240
  1203.5 78.9 %reduce-scatter.21.cloned.1.call-done = f32[6,9216]{1,0:T(8,128)} async-done(((f32[6,147456]{1,0:T(8,128)}), f32[6,9216]{1,0:T(8,128)}) %reduce-scatter.21.cloned.1.call-update) | async-done | bytes 221200 | tf_op jit(solution)/shard_map/reduce_scatter | solution.py:240
  1284.6 42.3 %reduce-scatter.19.cloned.1.call-done = f32[2,256,768]{2,1,0:T(8,128)} async-done(((f32[2,512,768]{2,1,0:T(8,128)}), f32[2,256,768]{2,1,0:T(8,128)}) %reduce-scatter.19.cloned.1.call-update) | async-done | bytes 1572880 | tf_op jit(solution)/shard_map/reduce_scatter | solution.py:211
  1326.9 3.7 divide_add_fusion
  1330.6 332.7 %all-reduce.12.cloned.1.call-done = (f32[16,73728]{1,0:T(8,128)}, f32[16,73728]{1,0:T(8,128)}, f32[16,73728]{1,0:T(8,128)}, f32[16,73728]{1,0:T(8,128)}) async-done(((f32[16,73728]{1,0:T(8,128)}, f32[16,73728]{1,0:T(8,128)}, f32[16,73728]{1,0:T(8,128)}, f32[16,73728]{1,0:T(8,128)}), (f32[16,73728]{1,0:T(8,128)}, f32[16,73728]{1,0:T(8,128)}, f32[16,73728]{1,0:T(8,128)}, ...) | async-done | bytes 18874384
  1665.8 9.3 all_gather.29
  1677.7 8.4 all_gather.28
  1691.1 7.5 all_gather.30
  1698.7 7.4 all_gather.31
  (305 shorter events, 97.6 us)
Async XLA Ops:
  7.2 34.3 %all-gather.5.cloned.1.call-start = ((), (), s32[]{:S(2)}) async-start(), calls=%async_computation.12 | async-start | bytes 2359296 | tf_op jit(solution)/shard_map/all_gather | solution.py:62
  11.4 96.4 %reduce-scatter.13.cloned.1.call-start = ((), (), s32[]{:S(2)}) async-start(), calls=%async_computation.13 | async-start | bytes 4718592 | tf_op jit(solution)/shard_map/reduce_scatter | solution.py:81
  12.4 34.8 %copy-start.39 = (f32[6,64]{1,0:T(8,128)}, f32[6,64]{1,0:T(8,128)S(1)}, u32[]{:S(2)}) copy-start(f32[6,64]{1,0:T(8,128)S(1)} %add.323) | copy-start | bytes 4612
  12.4 39.8 %copy-start.41 = (f32[6,64]{1,0:T(8,128)}, f32[6,64]{1,0:T(8,128)S(1)}, u32[]{:S(2)}) copy-start(f32[6,64]{1,0:T(8,128)S(1)} %add.320) | copy-start | bytes 4612
  52.2 8.6 copy-start.37
  54.1 7.6 copy-start.27
  61.7 46.2 %copy-start.17 = (bf16[2,256,768]{2,1,0:T(8,128)(2,1)S(1)}, bf16[2,256,768]{2,1,0:T(8,128)(2,1)}, u32[]{:S(2)}) copy-start(bf16[2,256,768]{2,1,0:T(8,128)(2,1)} %param.12) | copy-start | bytes 2359300
  64.4 101.6 %all-gather.7.cloned.1.call-start = ((), (), s32[]{:S(2)}) async-start(), calls=%async_computation.14 | async-start | bytes 2359296 | tf_op jit(solution)/shard_map/all_gather | solution.py:62
  65.0 67.7 %copy-start.54 = (f32[768]{0:T(1024)}, f32[768]{0:T(1024)S(1)}, u32[]{:S(2)}) copy-start(f32[768]{0:T(1024)S(1)} %get-tuple-element.54) | copy-start | bytes 9220
  65.1 67.6 %copy-start.61 = (f32[768]{0:T(1024)}, f32[768]{0:T(1024)S(1)}, u32[]{:S(2)}) copy-start(f32[768]{0:T(1024)S(1)} %get-tuple-element.49) | copy-start | bytes 9220
  65.1 67.6 %copy-start.57 = (f32[1,3072]{1,0:T(1,128)}, f32[1,3072]{1,0:T(1,128)S(1)}, u32[]{:S(2)}) copy-start(f32[1,3072]{1,0:T(1,128)S(1)} %get-tuple-element.111) | copy-start | bytes 36868
  107.9 24.8 %slice-start.3 = ((s8[9437184]{0:T(1024)(128)(4,1)}), s8[4194304]{0:T(1024)(128)(4,1)S(1)}, s32[]{:S(2)}) async-start(s8[9437184]{0:T(1024)(128)(4,1)} %bitcast.283), calls=%async_computation.33 | async-start | bytes 8388608
  109.7 22.9 %copy-start.8 = (f32[2,256,768]{2,1,0:T(8,128)}, f32[2,256,768]{2,1,0:T(8,128)S(1)}, u32[]{:S(2)}) copy-start(f32[2,256,768]{2,1,0:T(8,128)S(1)} %get-tuple-element.100) | copy-start | bytes 4718596
  109.8 22.9 %copy-start.45 = (f32[2,256]{1,0:T(2,128)}, f32[2,256]{1,0:T(2,128)S(1)}, u32[]{:S(2)}) copy-start(f32[2,256]{1,0:T(2,128)S(1)} %broadcast_multiply_fusion.3) | copy-start | bytes 6148
  110.1 22.6 %copy-start.47 = (f32[2,256]{1,0:T(2,128)}, f32[2,256]{1,0:T(2,128)S(1)}, u32[]{:S(2)}) copy-start(f32[2,256]{1,0:T(2,128)S(1)} %multiply_reduce_fusion.11) | copy-start | bytes 6148
  110.1 22.6 %copy-start.59 = (f32[2,256]{1,0:T(2,128)}, f32[2,256]{1,0:T(2,128)S(1)}, u32[]{:S(2)}) copy-start(f32[2,256]{1,0:T(2,128)S(1)} %fusion.83) | copy-start | bytes 6148
  110.1 22.6 %slice-start.4 = ((s8[9437184]{0:T(1024)(128)(4,1)}), s8[4194304]{0:T(1024)(128)(4,1)S(1)}, s32[]{:S(2)}) async-start(s8[9437184]{0:T(1024)(128)(4,1)} %bitcast.283), calls=%async_computation.34 | async-start | bytes 8388608
  110.1 22.6 %slice-start.5 = ((s8[9437184]{0:T(1024)(128)(4,1)}), s8[1048576]{0:T(1024)(128)(4,1)S(1)}, s32[]{:S(2)}) async-start(s8[9437184]{0:T(1024)(128)(4,1)} %bitcast.283), calls=%async_computation.35 | async-start | bytes 2097152
  135.9 30.1 %copy-start.49 = (f32[2,256]{1,0:T(2,128)}, f32[2,256]{1,0:T(2,128)S(1)}, u32[]{:S(2)}) copy-start(f32[2,256]{1,0:T(2,128)S(1)} %multiply_reduce_fusion.10) | copy-start | bytes 6148
  138.7 93.5 %reduce-scatter.15.cloned.1.call-start = ((), (), s32[]{:S(2)}) async-start(), calls=%async_computation.15 | async-start | bytes 4718592 | tf_op jit(solution)/shard_map/reduce_scatter | solution.py:81
  178.5 7.5 copy-start.28
  188.7 125.4 %all-gather.9.cloned.1.call-start = ((), (), s32[]{:S(2)}) async-start(), calls=%async_computation.16 | async-start | bytes 2359296 | tf_op jit(solution)/shard_map/all_gather | solution.py:174
  232.2 26.0 %slice-start.6 = ((s8[9437184]{0:T(1024)(128)(4,1)}), s8[4194304]{0:T(1024)(128)(4,1)S(1)}, s32[]{:S(2)}) async-start(s8[9437184]{0:T(1024)(128)(4,1)} %bitcast.285), calls=%async_computation.36 | async-start | bytes 8388608
  234.7 49.0 %copy-start.10 = (f32[2,256,768]{2,1,0:T(8,128)}, f32[2,256,768]{2,1,0:T(8,128)S(1)}, u32[]{:S(2)}) copy-start(f32[2,256,768]{2,1,0:T(8,128)S(1)} %get-tuple-element.96) | copy-start | bytes 4718596
  235.1 23.1 %slice-start.7 = ((s8[9437184]{0:T(1024)(128)(4,1)}), s8[4194304]{0:T(1024)(128)(4,1)S(1)}, s32[]{:S(2)}) async-start(s8[9437184]{0:T(1024)(128)(4,1)} %bitcast.285), calls=%async_computation.37 | async-start | bytes 8388608
  235.1 23.1 %slice-start.8 = ((s8[9437184]{0:T(1024)(128)(4,1)}), s8[1048576]{0:T(1024)(128)(4,1)S(1)}, s32[]{:S(2)}) async-start(s8[9437184]{0:T(1024)(128)(4,1)} %bitcast.285), calls=%async_computation.38 | async-start | bytes 2097152
  261.5 16.0 slice-start.9
  265.1 12.4 copy-start.30
  265.1 12.4 slice-start.10
  265.1 12.4 slice-start.11
  283.8 30.3 %copy-start.29 = (bf16[2,384,768]{2,1,0:T(8,128)(2,1)S(1)}, bf16[2,384,768]{2,1,0:T(8,128)(2,1)}, u32[]{:S(2)}) copy-start(bf16[2,384,768]{2,1,0:T(8,128)(2,1)} %param.18) | copy-start | bytes 3538948
  286.7 113.3 %reduce-scatter.17.cloned.1.call-start = ((), (), s32[]{:S(2)}) async-start(), calls=%async_computation.17 | async-start | bytes 4718592 | tf_op jit(solution)/shard_map/reduce_scatter | solution.py:211
  314.1 11.5 slice-start
  314.1 11.5 slice-start.1
  318.0 7.6 slice-start.2
  318.0 7.6 copy-start.19
  346.4 159.6 %copy-start.20 = (bf16[1,2,512,384]{3,2,0,1:T(8,128)(2,1)}, bf16[1,2,512,384]{3,2,0,1:T(8,128)(2,1)S(1)}, u32[]{:S(2)}) copy-start(bf16[1,2,512,384]{3,2,0,1:T(8,128)(2,1)S(1)} %copy.91) | copy-start | bytes 2359300
  348.2 157.8 %copy-start.21 = (bf16[1,2,512,384]{3,2,0,1:T(8,128)(2,1)}, bf16[1,2,512,384]{3,2,0,1:T(8,128)(2,1)S(1)}, u32[]{:S(2)}) copy-start(bf16[1,2,512,384]{3,2,0,1:T(8,128)(2,1)S(1)} %copy.89) | copy-start | bytes 2359300
  356.5 47.4 %copy-start.50 = (f32[2,256]{1,0:T(2,128)S(1)}, f32[2,256]{1,0:T(2,128)}, u32[]{:S(2)}) copy-start(f32[2,256]{1,0:T(2,128)} %copy-done.49) | copy-start | bytes 6148
  356.5 153.2 %all-gather.11.cloned.1.call-start = ((), (), s32[]{:S(2)}) async-start(), calls=%async_computation.18 | async-start | bytes 2359296 | tf_op jit(solution)/shard_map/all_gather | solution.py:174
  403.9 14.7 slice-start.12
  406.3 12.3 copy-start.31
  406.3 12.3 copy-start.9
  406.3 12.3 copy-start.46
  406.3 12.3 copy-start.55
  406.3 12.3 copy-start.60
  406.3 12.3 copy-start.62
  406.3 12.3 slice-start.13
  406.3 12.3 slice-start.14
  425.6 173.9 %reduce-scatter.31.cloned.1.call-start = ((), (), s32[]{:S(2)}) async-start(), calls=%async_computation.25 | async-start | bytes 14155776 | tf_op jit(solution)/shard_map/reduce_scatter | solution.py:236
  445.8 233.1 %reduce-scatter.35.cloned.1.call-start = ((), (), s32[]{:S(2)}) async-start(), calls=%async_computation.27 | async-start | bytes 14155776 | tf_op jit(solution)/shard_map/reduce_scatter | solution.py:237
  466.2 325.7 %reduce-scatter.29.cloned.1.call-start = ((), (), s32[]{:S(2)}) async-start(), calls=%async_computation.24 | async-start | bytes 14155776 | tf_op jit(solution)/shard_map/reduce_scatter | solution.py:236
  486.2 418.6 %reduce-scatter.33.cloned.1.call-start = ((), (), s32[]{:S(2)}) async-start(), calls=%async_computation.26 | async-start | bytes 14155776 | tf_op jit(solution)/shard_map/reduce_scatter | solution.py:237
  505.3 492.0 %all-reduce.10.cloned.1.call-start = ((), (), s32[]{:S(2)}) async-start(), calls=%async_computation.28 | async-start | bytes 135168 | tf_op jit(solution)/shard_map/psum | solution.py:224
  513.2 7.3 copy-start.42
  520.6 30.2 %copy-start.22 = (bf16[1,2,512,384]{3,2,0,1:T(8,128)(2,1)}, bf16[1,2,512,384]{3,2,0,1:T(8,128)(2,1)S(1)}, u32[]{:S(2)}) copy-start(bf16[1,2,512,384]{3,2,0,1:T(8,128)(2,1)S(1)} %copy.98) | copy-start | bytes 2359300
  553.5 509.2 %reduce-scatter.27.cloned.1.call-start = ((), (), s32[]{:S(2)}) async-start(), calls=%async_computation.23 | async-start | bytes 1671168 | tf_op jit(solution)/shard_map/reduce_scatter | solution.py:241
  557.5 567.6 %reduce-scatter.25.cloned.1.call-start = ((), (), s32[]{:S(2)}) async-start(), calls=%async_computation.22 | async-start | bytes 1671168 | tf_op jit(solution)/shard_map/reduce_scatter | solution.py:241
  560.5 643.0 %reduce-scatter.23.cloned.1.call-start = ((), (), s32[]{:S(2)}) async-start(), calls=%async_computation.21 | async-start | bytes 5013504 | tf_op jit(solution)/shard_map/reduce_scatter | solution.py:240
  576.4 706.0 %reduce-scatter.21.cloned.1.call-start = ((), (), s32[]{:S(2)}) async-start(), calls=%async_computation.20 | async-start | bytes 5013504 | tf_op jit(solution)/shard_map/reduce_scatter | solution.py:240
  592.3 734.6 %reduce-scatter.19.cloned.1.call-start = ((), (), s32[]{:S(2)}) async-start(), calls=%async_computation.19 | async-start | bytes 4718592 | tf_op jit(solution)/shard_map/reduce_scatter | solution.py:211
  599.4 1063.9 %all-reduce.12.cloned.1.call-start = ((), (), s32[]{:S(2)}) async-start(), calls=%async_computation.29 | async-start | bytes 37748736
  904.8 422.1 %copy-start.12 = (f32[2,256,768]{2,1,0:T(8,128)S(1)}, f32[2,256,768]{2,1,0:T(8,128)}, u32[]{:S(2)}) copy-start(f32[2,256,768]{2,1,0:T(8,128)} %copy-done.11) | copy-start | bytes 4718596
  904.9 422.1 %copy-start.18 = (bf16[2,256,768]{2,1,0:T(8,128)(2,1)S(1)}, bf16[2,256,768]{2,1,0:T(8,128)(2,1)}, u32[]{:S(2)}) copy-start(bf16[2,256,768]{2,1,0:T(8,128)(2,1)} %param.12) | copy-start | bytes 2359300
  (37 other events, 105.0 us)
Sparse Core Ops, SparseCore 0:
  11.6 29.8 all-gather.4
  64.5 43.3 reduce-scatter.12
  138.8 27.1 all-gather.6
  188.8 43.3 reduce-scatter.14
  286.8 27.2 all-gather.8
  356.6 43.3 reduce-scatter.16
  425.7 27.1 all-gather.10
  455.4 110.5 reduce-scatter.30
  568.4 110.5 reduce-scatter.34
  681.2 110.5 reduce-scatter.28
  794.2 110.5 reduce-scatter.32
  911.0 86.3 all-reduce.9
  1001.6 61.0 reduce-scatter.26
  1066.6 58.4 reduce-scatter.24
  1128.8 74.6 reduce-scatter.22
  1207.7 74.6 reduce-scatter.20
  1284.4 42.4 reduce-scatter.18
  1331.9 331.3 all-reduce.11
where the time goes:
time: 1730 us; the launch traced here: 1720 us
  waiting for transfers between devices  1250 us (72%)
  matrix products  228 us (13%)
  local copies, waits for them, and re-layouts  110 us (6%)
  other arithmetic  64.1 us (4%)
  blocking collectives  42.1 us (2%)
    unnamed x19, waiting for transfers between devices  333 us
    reduce_scatter x2, waiting for transfers between devices, local(): lax.psum_scatter(down_grid, 'mp', scatter_dimension=1, tiled=True)  192 us
    reduce_scatter x2, waiting for transfers between devices, local(): lax.psum_scatter(qkv_flat, 'dp', scatter_dimension=1, tiled=True)  156 us
    reduce_scatter x2, waiting for transfers between devices, local(): lax.psum_scatter(out_flat, 'dp', scatter_dimension=1, tiled=True)  115 us
    reduce_scatter x2, waiting for transfers between devices, local(): lax.psum_scatter(up_grid, 'mp', scatter_dimension=1, tiled=True)  113 us
    psum x1, waiting for transfers between devices, local(): lax.psum((d_bias_qv, d_gains, d_vectors, d_bias_up), 'dp')  91.3 us
    reduce_scatter x2, waiting for transfers between devices, local(): lax.psum_scatter(partial_out, 'mp', scatter_dimension=1, tiled=True)  86 us
    reduce_scatter x2, waiting for transfers between devices, local(): lax.psum_scatter(d_gathered, 'mp', scatter_dimension=1, tiled=True)  85.8 us
  transfers between devices with their start and end apart: 18, of which 16 were waited for; matrix products, arithmetic and copies ran while one was open for 11% of the time, Pallas kernels for 0%

commit v1 on v0

v1 whole, which is shorter than its diff:
```python
import functools

import jax
import jax.numpy as jnp
from jax import lax
from jax.experimental import pallas as pl
from jax.experimental.pallas import tpu as pltpu
from jax.sharding import PartitionSpec as P

HEAD = 64
PAIR = 2 * HEAD
EPS = 1e-06
BIG = -1e30
INV_SQRT2 = 0.7071067811865476
INV_SQRT2PI = 0.3989422804014327

f32 = jnp.float32
bf16 = jnp.bfloat16
MIB = 1024 * 1024

NT = (((1,), (1,)), ((), ()))
TN = (((0,), (0,)), ((), ()))


def dot(lhs, rhs, dims=(((1,), (0,)), ((), ()))):
    return lax.dot_general(lhs, rhs, dims, preferred_element_type=f32)


def whole(*shape):
    return pl.BlockSpec(shape, lambda *_: (0,) * len(shape))


def params(mib):
    return pltpu.CompilerParams(vmem_limit_bytes=mib * MIB)


def cost(flops, moved):
    return pl.CostEstimate(flops=int(flops), bytes_accessed=int(moved), transcendentals=0)


def shape(dims, dtype):
    return jax.ShapeDtypeStruct(dims, dtype)


def head_mask(head, value):
    lane = lax.broadcasted_iota(jnp.int32, (1, PAIR), 1)
    return jnp.where((lane // HEAD) == head, value, 0.0).astype(bf16)


def attn_fwd_kernel(a_ref, w_ref, b_ref, sq_ref, sk_ref, q_ref, k_ref, v_ref, c_ref, lse_ref):
    seq = a_ref.shape[0]
    act = a_ref[...]
    both = dot(act, jnp.concatenate([w_ref[0], w_ref[1]], axis=1))
    query = (both[:, :PAIR] + b_ref[0:1, :]).astype(bf16)
    key = both[:, PAIR:].astype(bf16)
    value = dot(act, w_ref[2]) + b_ref[1:2, :]
    value_t = value.T.astype(bf16)
    q_ref[...] = query
    k_ref[...] = key
    v_ref[...] = value.astype(bf16)
    key_ext = jnp.concatenate([key, sk_ref[...]], axis=1)
    parts = []
    ones = jnp.ones((16, seq), bf16)
    for head in range(2):
        query_ext = jnp.concatenate([query * head_mask(head, HEAD**-0.5), sq_ref[...]], axis=1)
        scores = dot(key_ext, query_ext, NT)
        top = jnp.max(scores, axis=0, keepdims=True)
        weights = jnp.exp(scores - top).astype(bf16)
        summed = dot(
            jnp.concatenate([value_t[head * HEAD : (head + 1) * HEAD], ones], axis=0), weights
        )
        total = summed[HEAD : HEAD + 1]
        parts.append(summed[:HEAD] * (1.0 / total))
        lse_ref[0, head : head + 1, :] = top + jnp.log(total)
    c_ref[...] = jnp.concatenate(parts, axis=0).T


def attn_fwd(act, weights, bias, seg_q, seg_k):
    seq, width = act.shape
    cols = weights.shape[2]
    steps = cols // PAIR
    block = pl.BlockSpec((seq, PAIR), lambda t: (0, t))
    return pl.pallas_call(
        attn_fwd_kernel,
        grid=(steps,),
        in_specs=[
            whole(seq, width),
            pl.BlockSpec((3, width, PAIR), lambda t: (0, 0, t)),
            pl.BlockSpec((2, PAIR), lambda t: (0, t)),
            whole(seq, PAIR),
            whole(seq, PAIR),
        ],
        out_specs=[block, block, block, block, pl.BlockSpec((1, 8, seq), lambda t: (t, 0, 0))],
        out_shape=[
            shape((seq, cols), bf16),
            shape((seq, cols), bf16),
            shape((seq, cols), bf16),
            shape((seq, cols), f32),
            shape((steps, 8, seq), f32),
        ],
        compiler_params=params(24),
        cost_estimate=cost(6 * seq * width * cols + 16 * seq * seq * cols, 5 * MIB),
        name="attn_fwd",
    )(act, weights, bias, seg_q, seg_k)


def norm_rows(entries):
    centred = entries - jnp.mean(entries, axis=-1, keepdims=True)
    spread = jnp.mean(centred * centred, axis=-1, keepdims=True)
    rate = lax.rsqrt(spread + EPS)
    return centred * rate, rate


def ff_fwd_kernel(
    last, clip_ref, x_ref, co_ref, ct_ref, wo_ref, wt_ref, vec_ref, gain_ref, up_ref, bup_ref,
    down_ref, cq_ref, hat1_ref, rate1_ref, u_ref, g_ref, slope_ref, hat2_ref, rate2_ref, *rest
):
    acc_ref = rest[-1]
    step = pl.program_id(0)
    seq = x_ref.shape[0]
    half = co_ref.shape[1]
    rows = 64
    ctx_limit, ff_limit, act_limit = clip_ref[1], clip_ref[2], clip_ref[3]
    next_limit = clip_ref[4]

    @pl.when(step == 0)
    def _():
        inv = 1.0 / ctx_limit
        cq_ref[:, :half] = (ctx_limit * jnp.tanh(co_ref[...] * inv)).astype(bf16)
        cq_ref[:, half:] = (ctx_limit * jnp.tanh(ct_ref[...] * inv)).astype(bf16)
        acc_ref[...] = dot(cq_ref[:, :half], wo_ref[...]) + dot(cq_ref[:, half:], wt_ref[...])

        def body(i, carry):
            at = pl.ds(pl.multiple_of(i * rows, rows), rows)
            hat, rate = norm_rows(x_ref[at, :].astype(f32) + (acc_ref[at, :] + vec_ref[0:1, :]))
            hat1_ref[at, :] = hat
            rate1_ref[at, :] = jnp.broadcast_to(rate, (rows, 128))
            normed = hat * gain_ref[0:1, :] + vec_ref[1:2, :]
            u_ref[at, :] = (ff_limit * jnp.tanh(normed * (1.0 / ff_limit))).astype(bf16)
            acc_ref[at, :] = normed + vec_ref[2:3, :]
            return carry

        lax.fori_loop(0, seq // rows, body, 0)

    inv_act = 1.0 / act_limit
    chunk = up_ref.shape[1]
    sub = 256
    total = None
    for part in range(chunk // sub):
        cols = slice(part * sub, (part + 1) * sub)
        pre = dot(u_ref[...], up_ref[:, cols]) + bup_ref[:, cols]
        cdf = 0.5 * lax.erf(pre * INV_SQRT2) + 0.5
        pdf = jnp.exp(pre * pre * -0.5) * INV_SQRT2PI
        bent = jnp.tanh(pre * cdf * inv_act)
        out = (act_limit * bent).astype(bf16)
        g_ref[:, cols] = out
        slope_ref[:, cols] = ((1.0 - bent * bent) * (cdf + pre * pdf)).astype(bf16)
        term = dot(out, down_ref[cols, :])
        total = term if total is None else total + term
    acc_ref[...] += total

    @pl.when(step == pl.num_programs(0) - 1)
    def _():
        def body(i, carry):
            at = pl.ds(pl.multiple_of(i * rows, rows), rows)
            hat, rate = norm_rows(acc_ref[at, :])
            hat2_ref[at, :] = hat
            rate2_ref[at, :] = jnp.broadcast_to(rate, (rows, 128))
            new = hat * gain_ref[1:2, :] + vec_ref[3:4, :]
            if last:
                rest[0][at, :] = new.astype(bf16)
            else:
                rest[0][at, :] = new
                rest[1][at, :] = (next_limit * jnp.tanh(new * (1.0 / next_limit))).astype(bf16)
            return carry

        lax.fori_loop(0, seq // rows, body, 0)


def ff_fwd(last, clips, x, ctx_own, ctx_oth, wo_own, wo_oth, vec, gain, w_up, b_up, w_down):
    seq, width = x.shape
    half = ctx_own.shape[1]
    hidden = w_up.shape[1]
    chunk = 512
    steps = hidden // chunk
    tile = pl.BlockSpec((seq, chunk), lambda t: (0, t))
    full = whole(seq, width)
    outs = [
        (full, shape((seq, width), bf16)),
        (full, shape((seq, width), f32)),
        (whole(seq, 128), shape((seq, 128), f32)),
        (full, shape((seq, width), bf16)),
        (tile, shape((seq, hidden), bf16)),
        (tile, shape((seq, hidden), bf16)),
        (full, shape((seq, width), f32)),
        (whole(seq, 128), shape((seq, 128), f32)),
    ]
    if last:
        outs.append((full, shape((seq, width), bf16)))
    else:
        outs.append((full, shape((seq, width), f32)))
        outs.append((full, shape((seq, width), bf16)))
    return pl.pallas_call(
        functools.partial(ff_fwd_kernel, last),
        grid=(steps,),
        in_specs=[
            pl.BlockSpec(memory_space=pltpu.SMEM),
            full,
            whole(seq, half),
            whole(seq, half),
            whole(half, width),
            whole(half, width),
            whole(*vec.shape),
            whole(*gain.shape),
            pl.BlockSpec((width, chunk), lambda t: (0, t)),
            pl.BlockSpec((1, chunk), lambda t: (0, t)),
            pl.BlockSpec((chunk, width), lambda t: (t, 0)),
        ],
        out_specs=[spec for spec, _ in outs],
        out_shape=[out for _, out in outs],
        scratch_shapes=[pltpu.VMEM((seq, width), f32)],
        compiler_params=params(48),
        cost_estimate=cost(4 * seq * width * hidden * 2, 20 * MIB),
        name="ff_fwd",
    )(clips, x, ctx_own, ctx_oth, wo_own, wo_oth, vec, gain, w_up, b_up, w_down)


def norm_back(grad, hat, rate, gain):
    scaled = grad * gain
    mean = jnp.mean(scaled, axis=-1, keepdims=True)
    lean = jnp.mean(scaled * hat, axis=-1, keepdims=True)
    return rate * (scaled - mean - hat * lean)


def ff_bwd_kernel(
    core_ref, clip_ref, dx_ref, hat2_ref, rate2_ref, hat1_ref, rate1_ref, vec_ref, gain_ref,
    slope_ref, up_ref, down_ref, wo_ref, wt_ref, co_ref, ct_ref,
    zk_ref, zs_ref, fk_ref, fs_ref, ok_ref, os_ref, dy_ref, dco_ref, dct_ref, small_ref, bup_ref,
    df_ref, de_ref, du_ref,
):
    step = pl.program_id(0)
    steps = pl.num_programs(0)
    seq, width = dx_ref.shape
    half = width // 2
    rows = 64
    count = seq // rows
    core = core_ref[0]
    mine = pl.ds(pl.multiple_of(core * half, 128), half)
    other = pl.ds(pl.multiple_of((1 - core) * half, 128), half)
    zero = jnp.zeros((1, width), f32)
    ctx_limit, ff_limit = clip_ref[1], clip_ref[2]

    @pl.when(step == 0)
    def _():
        def body(i, carry):
            gain_sum, shift_sum, branch_sum = carry
            at = pl.ds(pl.multiple_of(i * rows, rows), rows)
            grad = dx_ref[at, :].astype(f32)
            hat = hat2_ref[at, :]
            de = norm_back(grad, hat, rate2_ref[at, 0:1], gain_ref[1:2, :])
            df = de.astype(bf16)
            de_ref[at, :] = de
            df_ref[at, :] = df
            return (
                gain_sum + jnp.sum(grad * hat, axis=0, keepdims=True),
                shift_sum + jnp.sum(grad, axis=0, keepdims=True),
                branch_sum + jnp.sum(df.astype(f32), axis=0, keepdims=True),
            )

        gain_sum, shift_sum, branch_sum = lax.fori_loop(0, count, body, (zero, zero, zero))
        small_ref[2:3, :] = branch_sum
        small_ref[3:4, :] = shift_sum
        small_ref[5:6, :] = gain_sum
        fk_ref[...] = df_ref[:, mine]
        fs_ref[...] = df_ref[:, other]
        du_ref[...] = jnp.zeros_like(du_ref)

    chunk = up_ref.shape[1]
    sub = 256
    total = None
    for part in range(chunk // sub):
        cols = slice(part * sub, (part + 1) * sub)
        dz = dot(df_ref[...], down_ref[cols, :], NT) * slope_ref[:, cols].astype(f32)
        low = dz.astype(bf16)
        bup_ref[:, cols] = jnp.sum(low.astype(f32), axis=0, keepdims=True)

        @pl.when(step < steps // 2)
        def _():
            zk_ref[:, pl.ds(pl.multiple_of(step * chunk + part * sub, 128), sub)] = low

        @pl.when(step >= steps // 2)
        def _():
            place = (step - steps // 2) * chunk + part * sub
            zs_ref[:, pl.ds(pl.multiple_of(place, 128), sub)] = low

        term = dot(low, up_ref[:, cols], NT)
        total = term if total is None else total + term
    du_ref[...] += total

    @pl.when(step == steps - 1)
    def _():
        def body(i, carry):
            gain_sum, shift_sum, out_sum = carry
            at = pl.ds(pl.multiple_of(i * rows, rows), rows)
            hat = hat1_ref[at, :]
            normed = hat * gain_ref[0:1, :] + vec_ref[1:2, :]
            bent = jnp.tanh(normed * (1.0 / ff_limit))
            grad = de_ref[at, :] + du_ref[at, :] * (1.0 - bent * bent)
            dy = norm_back(grad, hat, rate1_ref[at, 0:1], gain_ref[0:1, :])
            low = dy.astype(bf16)
            dy_ref[at, :] = dy
            df_ref[at, :] = low
            return (
                gain_sum + jnp.sum(grad * hat, axis=0, keepdims=True),
                shift_sum + jnp.sum(grad, axis=0, keepdims=True),
                out_sum + jnp.sum(low.astype(f32), axis=0, keepdims=True),
            )

        gain_sum, shift_sum, out_sum = lax.fori_loop(0, count, body, (zero, zero, zero))
        small_ref[0:1, :] = out_sum
        small_ref[1:2, :] = shift_sum
        small_ref[4:5, :] = gain_sum
        small_ref[6:8, :] = jnp.zeros((2, width), f32)
        ok_ref[...] = df_ref[:, mine]
        os_ref[...] = df_ref[:, other]
        inv = 1.0 / ctx_limit
        for w_ref, ctx_ref, out_ref in ((wo_ref, co_ref, dco_ref), (wt_ref, ct_ref, dct_ref)):
            bent = jnp.tanh(ctx_ref[...] * inv)
            grad = dot(df_ref[...], w_ref[...], NT)
            out_ref[...] = (grad * (1.0 - bent * bent)).astype(bf16)


def ff_bwd(
    core, clips, dx, hat2, rate2, hat1, rate1, vec, gain, slope, w_up, w_down, wo_own, wo_oth,
    ctx_own, ctx_oth,
):
    seq, width = dx.shape
    half = ctx_own.shape[1]
    hidden = w_up.shape[1]
    chunk = 512
    steps = hidden // chunk
    span = steps // 2

    def place(t, core_ref):
        first = t < span
        return jnp.where(first, core_ref[0] * span + t, (1 - core_ref[0]) * span + t - span)

    full = whole(seq, width)
    part = whole(seq, width // 2)
    outs = [
        (whole(seq, hidden // 2), shape((seq, hidden // 2), bf16)),
        (whole(seq, hidden // 2), shape((seq, hidden // 2), bf16)),
        (part, shape((seq, width // 2), bf16)),
        (part, shape((seq, width // 2), bf16)),
        (part, shape((seq, width // 2), bf16)),
        (part, shape((seq, width // 2), bf16)),
        (full, shape((seq, width), f32)),
        (whole(seq, half), shape((seq, half), bf16)),
        (whole(seq, half), shape((seq, half), bf16)),
        (whole(8, width), shape((8, width), f32)),
        (pl.BlockSpec((1, chunk), lambda t, core: (0, place(t, core))), shape((1, hidden), f32)),
    ]
    return pl.pallas_call(
        ff_bwd_kernel,
        grid_spec=pltpu.PrefetchScalarGridSpec(
            num_scalar_prefetch=1,
            grid=(steps,),
            in_specs=[
                pl.BlockSpec(memory_space=pltpu.SMEM),
                full,
                full,
                whole(seq, 128),
                full,
                whole(seq, 128),
                whole(*vec.shape),
                whole(*gain.shape),
                pl.BlockSpec((seq, chunk), lambda t, core: (0, place(t, core))),
                pl.BlockSpec((width, chunk), lambda t, core: (0, place(t, core))),
                pl.BlockSpec((chunk, width), lambda t, core: (place(t, core), 0)),
                whole(half, width),
                whole(half, width),
                whole(seq, half),
                whole(seq, half),
            ],
            out_specs=[spec for spec, _ in outs],
            scratch_shapes=[
                pltpu.VMEM((seq, width), bf16),
                pltpu.VMEM((seq, width), f32),
                pltpu.VMEM((seq, width), f32),
            ],
        ),
        out_shape=[out for _, out in outs],
        compiler_params=params(52),
        cost_estimate=cost(4 * seq * width * hidden * 2, 20 * MIB),
        name="ff_bwd",
    )(
        core, clips, dx, hat2, rate2, hat1, rate1, vec, gain, slope, w_up, w_down, wo_own, wo_oth,
        ctx_own, ctx_oth,
    )


def attn_bwd_half(q_ref, k_ref, v_ref, c_ref, lse_ref, dc_ref, seg_q, seg_k):
    query, key, value, grad = q_ref[...], k_ref[...], v_ref[...], dc_ref[...]
    key_ext = jnp.concatenate([key, seg_k], axis=1)
    key_t = key.astype(f32).T.astype(bf16)
    product_t = (grad.astype(f32) * c_ref[...]).T
    d_key = d_value = None
    d_query_t = []
    for head in range(2):
        scaled = query * head_mask(head, HEAD**-0.5)
        scores = dot(key_ext, jnp.concatenate([scaled, seg_q], axis=1), NT)
        probs = jnp.exp(scores - lse_ref[0, head : head + 1, :])
        grad_head = grad * head_mask(head, 1.0)
        d_probs = dot(value, grad_head, NT)
        delta = jnp.sum(product_t[head * HEAD : (head + 1) * HEAD], axis=0, keepdims=True)
        d_scores = (probs * (d_probs - delta)).astype(bf16)
        term_v = dot(probs.astype(bf16), grad_head)
        term_k = dot(d_scores, scaled)
        d_value = term_v if d_value is None else d_value + term_v
        d_key = term_k if d_key is None else d_key + term_k
        d_query_t.append(dot(key_t[head * HEAD : (head + 1) * HEAD], d_scores))
    d_query = jnp.concatenate(d_query_t, axis=0).T * HEAD**-0.5
    return d_query.astype(bf16), d_key.astype(bf16), d_value.astype(bf16)


def attn_bwd_kernel(
    clip_ref, x_ref, dy_ref, sq_ref, sk_ref,
    qo_ref, ko_ref, vo_ref, co_ref, lo_ref, dco_ref, wo_ref,
    qt_ref, kt_ref, vt_ref, ct_ref, lt_ref, dct_ref, wt_ref,
    dqo_ref, dko_ref, dvo_ref, dqt_ref, dkt_ref, dvt_ref, bo_ref, bt_ref, dx_ref, acc_ref,
):
    step = pl.program_id(0)
    seq = x_ref.shape[0]
    rows = 64
    own = attn_bwd_half(qo_ref, ko_ref, vo_ref, co_ref, lo_ref, dco_ref, sq_ref[...], sk_ref[...])
    oth = attn_bwd_half(qt_ref, kt_ref, vt_ref, ct_ref, lt_ref, dct_ref, sq_ref[...], sk_ref[...])
    dqo_ref[...], dko_ref[...], dvo_ref[...] = own
    dqt_ref[...], dkt_ref[...], dvt_ref[...] = oth
    for out_ref, grads in ((bo_ref, own), (bt_ref, oth)):
        out_ref[0:1, :] = jnp.sum(grads[0].astype(f32), axis=0, keepdims=True)
        out_ref[1:2, :] = jnp.sum(grads[2].astype(f32), axis=0, keepdims=True)
        out_ref[2:8, :] = jnp.zeros((6, PAIR), f32)
    total = None
    for which in range(3):
        term = dot(
            jnp.concatenate([own[which], oth[which]], axis=1),
            jnp.concatenate([wo_ref[which], wt_ref[which]], axis=1),
            NT,
        )
        total = term if total is None else total + term

    @pl.when(step == 0)
    def _():
        acc_ref[...] = total

    @pl.when(step > 0)
    def _():
        acc_ref[...] += total

    @pl.when(step == pl.num_programs(0) - 1)
    def _():
        inv = 1.0 / clip_ref[0]

        def body(i, carry):
            at = pl.ds(pl.multiple_of(i * rows, rows), rows)
            bent = jnp.tanh(x_ref[at, :].astype(f32) * inv)
            dx_ref[at, :] = dy_ref[at, :] + acc_ref[at, :] * (1.0 - bent * bent)
            return carry

        lax.fori_loop(0, seq // rows, body, 0)


def attn_bwd(clips, x, dy, seg_q, seg_k, own, oth):
    seq, width = x.shape
    cols = own[0].shape[1]
    steps = cols // PAIR
    block = pl.BlockSpec((seq, PAIR), lambda t: (0, t))
    half_specs = [
        block,
        block,
        block,
        block,
        pl.BlockSpec((1, 8, seq), lambda t: (t, 0, 0)),
        block,
        pl.BlockSpec((3, width, PAIR), lambda t: (0, 0, t)),
    ]
    return pl.pallas_call(
        attn_bwd_kernel,
        grid=(steps,),
        in_specs=[
            pl.BlockSpec(memory_space=pltpu.SMEM),
            whole(seq, width),
            whole(seq, width),
            whole(seq, PAIR),
            whole(seq, PAIR),
        ]
        + half_specs * 2,
        out_specs=[block] * 6
        + [pl.BlockSpec((8, PAIR), lambda t: (0, t))] * 2
        + [whole(seq, width)],
        out_shape=[shape((seq, cols), bf16)] * 6
        + [shape((8, cols), f32)] * 2
        + [shape((seq, width), f32)],
        scratch_shapes=[pltpu.VMEM((seq, width), f32)],
        compiler_params=params(40),
        cost_estimate=cost(14 * seq * width * width + 40 * seq * seq * width, 14 * MIB),
        name="attn_bwd",
    )(clips, x, dy, seg_q, seg_k, *own, *oth)


def w_ff_kernel(um_ref, uo_ref, zm_ref, zo_ref, gm_ref, go_ref, fm_ref, fo_ref, out_ref, ut_ref):
    step = pl.program_id(0)
    chips, _, lanes = out_ref.shape
    seq, width = um_ref.shape
    tall = width // chips
    quarters = pl.num_programs(0)

    @pl.when(step == 0)
    def _():
        ut_ref[:, :seq] = um_ref[...].T
        ut_ref[:, seq:] = uo_ref[...].T

    grad_up = dot(ut_ref[:, :seq], zm_ref[...]) + dot(ut_ref[:, seq:], zo_ref[...])
    grad_up = grad_up.astype(bf16)
    for chip in range(chips):
        at = pl.ds(pl.multiple_of(step * tall, 16), tall)
        out_ref[chip, at, :] = grad_up[chip * tall : (chip + 1) * tall]
    start = out_ref.shape[1] // 2
    span = start
    per = gm_ref.shape[1] // span
    for part in range(per):
        cols = slice(part * span, (part + 1) * span)
        grad_down = dot(gm_ref[:, cols], fm_ref[...], TN) + dot(go_ref[:, cols], fo_ref[...], TN)
        out_ref[step * per + part, start:, :] = grad_down.astype(bf16)


def w_ff(chips, u_mine, u_core, dz_mine, dz_core, g_mine, g_core, df_mine, df_core):
    seq, width = u_mine.shape
    hidden = g_mine.shape[1]
    lanes = width // 2
    steps = dz_mine.shape[1] // lanes
    tall = 2 * (hidden // chips)
    z_block = pl.BlockSpec((seq, lanes), lambda t: (0, t))
    g_block = pl.BlockSpec((seq, hidden // steps), lambda t: (0, t))
    return pl.pallas_call(
        w_ff_kernel,
        grid=(steps,),
        in_specs=[
            whole(seq, width),
            whole(seq, width),
            z_block,
            z_block,
            g_block,
            g_block,
            whole(seq, lanes),
            whole(seq, lanes),
        ],
        out_specs=whole(chips, tall, lanes),
        out_shape=shape((chips, tall, lanes), bf16),
        scratch_shapes=[pltpu.VMEM((width, 2 * seq), bf16)],
        compiler_params=params(40),
        cost_estimate=cost(4 * seq * width * hidden, 17 * MIB),
        name="w_ff",
    )(u_mine, u_core, dz_mine, dz_core, g_mine, g_core, df_mine, df_core)


def w_att_kernel(
    core_ref, a_ref, dqo_ref, dko_ref, dvo_ref, dqt_ref, dkt_ref, dvt_ref,
    cm_ref, cc_ref, dom_ref, doc_ref,
    keep_o_ref, keep_t_ref, send_o_ref, send_t_ref, out_o_ref, out_t_ref, at_ref, spare_ref,
):
    width = a_ref.shape[1]
    chips, tall, cols = keep_o_ref.shape
    core = core_ref[0]
    piece = 48
    per = tall // piece
    at_ref[...] = a_ref[...].T
    sides = (
        ((dqo_ref, dko_ref, dvo_ref), keep_o_ref, send_o_ref),
        ((dqt_ref, dkt_ref, dvt_ref), keep_t_ref, send_t_ref),
    )
    for grads, keep_ref, send_ref in sides:
        for which in range(3):
            result = dot(at_ref[...], grads[which][...]).astype(bf16)
            for j in range(width // piece):
                index = which * (width // piece) + j
                block, sub = index // per, index % per
                spare_ref[block % 2, block // 2, sub * piece : (sub + 1) * piece, :] = result[
                    j * piece : (j + 1) * piece
                ]
        keep_ref[...] = spare_ref[core]
        send_ref[...] = spare_ref[1 - core]
    half = width // 2
    heads = half // HEAD
    for base, out_ref in ((0, out_o_ref), (half, out_t_ref)):
        result = dot(cm_ref[:, base : base + half], dom_ref[...], TN) + dot(
            cc_ref[:, base : base + half], doc_ref[...], TN
        )
        for chip in range(chips):
            for pair in range(heads // 2):
                first = (2 * pair) * HEAD + 8 * chip
                second = first + HEAD
                out_ref[chip, pair * 16 : (pair + 1) * 16, :] = jnp.concatenate(
                    [result[first : first + 8], result[second : second + 8]], axis=0
                ).astype(bf16)


def w_att(chips, core, act, d_own, d_oth, cq_mine, cq_core, do_mine, do_core):
    seq, width = act.shape
    cols = width // 2
    tall = 3 * width // (2 * chips)
    vmem = pl.BlockSpec(memory_space=pltpu.VMEM)
    outs = [shape((chips, tall, cols), bf16)] * 4 + [
        shape((chips, cols // chips, cols), bf16)
    ] * 2
    return pl.pallas_call(
        w_att_kernel,
        in_specs=[pl.BlockSpec(memory_space=pltpu.SMEM)] + [vmem] * 11,
        out_specs=[vmem] * 6,
        out_shape=outs,
        scratch_shapes=[
            pltpu.VMEM((width, seq), bf16),
            pltpu.VMEM((2, chips, tall, cols), bf16),
        ],
        compiler_params=params(40),
        cost_estimate=cost(8 * seq * width * width, 12 * MIB),
        name="w_att",
    )(core, act, *d_own, *d_oth, cq_mine, cq_core, do_mine, do_core)


def local(
    hidden_in, cotangent, segment_ids, clip_ranges, w_qkv, bias_qv, w_out, vector_bias, ln_gain,
    w_up, bias_up, w_down,
):
    layers = w_qkv.shape[0]
    row_count, half_seq, width = hidden_in.shape
    seq = segment_ids.shape[1]
    cols = w_qkv.shape[3]
    heads = cols // HEAD
    hidden = w_up.shape[2]
    dp_count = lax.axis_size("dp")
    assert lax.axis_size("mp") == 2 and row_count == 2 and seq == 2 * half_seq
    bits = dp_count.bit_length() - 1
    assert dp_count == 1 << bits and bits >= 1
    chips = dp_count // 2
    side = lax.axis_index("mp")
    place = lax.axis_index("dp")
    core = place % 2
    core_arr = core.reshape(1).astype(jnp.int32)

    def over_mp(value):
        return lax.ppermute(value, "mp", [(0, 1), (1, 0)])

    def over_bit(value, bit):
        return lax.ppermute(value, "dp", [(i, i ^ (1 << bit)) for i in range(dp_count)])

    def over_core(value):
        return over_bit(value, 0)

    def pick(value, index, axis):
        return lax.dynamic_index_in_dim(value, index, axis, keepdims=False)

    def ordered(index, mine, theirs, axis):
        first = jnp.where(index == 0, mine, theirs)
        second = jnp.where(index == 0, theirs, mine)
        return jnp.concatenate([first, second], axis=axis)

    def after(value, *earlier):
        return lax.optimization_barrier((value,) + earlier)[0]

    def gather_row(array, hold=()):
        return jnp.concatenate(
            [pick(array, side, 0), over_mp(after(pick(array, 1 - side, 0), *hold))], axis=0
        )

    x = gather_row(hidden_in)
    bias_oth = over_mp(bias_qv)
    limits = clip_ranges.astype(f32)
    clips = [
        jnp.concatenate([limits[i], limits[min(i + 1, layers - 1), :1]]) for i in range(layers)
    ]
    seg_row = pick(segment_ids, side, 0).reshape(2, half_seq)
    seg_row = jnp.concatenate([pick(seg_row, side, 0), pick(seg_row, 1 - side, 0)])
    same = seg_row[:, None] == jnp.arange(PAIR, dtype=seg_row.dtype)[None, :]
    used = (jnp.arange(PAIR) < seq)[None, :]
    seg_q = jnp.where(same, BIG, 0.0).astype(bf16)
    seg_k = jnp.where(same, 0.0, 1.0).astype(bf16) * used.astype(bf16)

    def fetch(weight, axis, hold):
        pieces = weight.shape[axis] // 2
        sent = lax.dynamic_slice_in_dim(weight, core * pieces, pieces, axis)
        got = over_mp(after(sent, hold))
        return ordered(core, got, over_core(got), axis)

    hold = x
    wq_oth, wo_oth = [], []
    for layer in range(layers):
        wq_oth.append(fetch(w_qkv[layer], 1, hold))
        wo_oth.append(fetch(w_out[layer], 0, hold))
        hold = wq_oth[-1][0, :8, :128]
    dx = gather_row(cotangent, (hold,))

    r0 = limits[0, 0]
    act = (r0 * jnp.tanh(x.astype(f32) / r0)).astype(bf16)
    stored = []
    for layer in range(layers):
        last = layer == layers - 1
        own = attn_fwd(act, w_qkv[layer], bias_qv[layer], seg_q, seg_k)
        oth = attn_fwd(act, wq_oth[layer], bias_oth[layer], seg_q, seg_k)
        outs = ff_fwd(
            last, clips[layer], x, own[3], oth[3], w_out[layer], wo_oth[layer],
            vector_bias[layer], ln_gain[layer], w_up[layer], bias_up[layer][None], w_down[layer],
        )
        cq, hat1, rate1, u, g, slope, hat2, rate2 = outs[:8]
        shared = over_core(cq), over_core(u), over_core(g)
        stored.append((x, act, own, oth, cq, hat1, rate1, u, g, slope, hat2, rate2, shared))
        if last:
            hidden_row = outs[8]
        else:
            x, act = outs[8], outs[9]

    def spread_row(row, theirs):
        mine = row[None, :half_seq]
        return ordered(side, mine, theirs[None].astype(row.dtype), 0)

    hidden_out = spread_row(hidden_row, over_mp(hidden_row[half_seq:]))

    fast = chips == 8 and width == 768 and hidden == 3072 and cols == 384

    def reduce_stage(value, bit, axis, dtype=bf16):
        mybit = (place >> bit) & 1
        keep = pick(value, mybit, axis)
        sent = pick(value, 1 - mybit, axis)
        got = over_bit(sent, bit)
        return (keep.astype(f32) + got.astype(f32)).astype(dtype)

    qkv_list, out_list, up_list, down_list, small_list = [], [], [], [], []
    for layer in reversed(range(layers)):
        x, act, own, oth, cq, hat1, rate1, u, g, slope, hat2, rate2, shared = stored[layer]
        (
            dz_keep, dz_send, df_keep, df_send, do_keep, do_send, dy, dc_own, dc_oth, small, d_bup,
        ) = ff_bwd(
            core_arr, clips[layer], dx, hat2, rate2, hat1, rate1, vector_bias[layer],
            ln_gain[layer], slope, w_up[layer], w_down[layer], w_out[layer], wo_oth[layer],
            own[3], oth[3],
        )
        outs = attn_bwd(
            clips[layer], x, dy, seg_q, seg_k,
            (*own, dc_own, w_qkv[layer]), (*oth, dc_oth, wq_oth[layer]),
        )
        d_own, d_oth = outs[:3], outs[3:6]
        dx = outs[8]
        d_bias = ordered(side, outs[6][:2], outs[7][:2], 1)
        small_list.append(
            jnp.concatenate([d_bias, small[:6], d_bup.reshape(-1, width)], axis=0)
        )
        if fast:
            cq_core, u_core, g_core = shared
            packed = w_ff(
                chips, u, u_core, dz_keep, over_core(dz_send), g, g_core, df_keep,
                over_core(df_send),
            )
            tall = packed.shape[1]
            packed = packed.reshape(2, 2, 2, tall, cols)
            packed = reduce_stage(packed, 1, 2)
            packed = reduce_stage(packed, 2, 1)
            packed = reduce_stage(packed, 3, 0)
            packed = packed.astype(f32) + over_mp(packed).astype(f32)
            share = hidden // chips
            up = packed[:share].reshape(hidden // width, 2, share // 8, cols)
            keep, sent = pick(up, core, 1), pick(up, 1 - core, 1).astype(bf16)
            up = ordered(core, keep[None], over_core(sent).astype(f32)[None], 0)
            up_list.append(up.transpose(2, 0, 1, 3).reshape(-1))
            down = packed[share:].reshape(2, share // 2, cols)
            keep, sent = pick(down, core, 0), pick(down, 1 - core, 0).astype(bf16)
            down = ordered(core, keep[:, None], over_core(sent).astype(f32)[:, None], 1)
            down_list.append(down.reshape(-1))

            keep_o, keep_t, send_o, send_t, out_o, out_t = w_att(
                chips, core_arr, act, d_own, d_oth, cq, cq_core, do_keep, over_core(do_send)
            )
            send_o, send_t = over_core(send_o), over_core(send_t)
            mine = jnp.concatenate([keep_o + send_o, out_o], axis=1)
            theirs = jnp.concatenate([keep_t + send_t, out_t], axis=1)
            packed = mine + over_mp(theirs)
            tall = packed.shape[1]
            packed = packed.reshape(2, 2, 2, tall, cols)
            packed = reduce_stage(packed, 1, 2)
            packed = reduce_stage(packed, 2, 1)
            packed = reduce_stage(packed, 3, 0, f32)
            share = keep_o.shape[1]
            qkv_list.append(
                packed[:share].reshape(share, heads, HEAD).transpose(1, 0, 2).reshape(heads, -1)
            )
            out = packed[share:].reshape(heads, 2, 4, cols)
            keep, sent = pick(out, core, 1), pick(out, 1 - core, 1).astype(bf16)
            out = ordered(core, keep[:, :, None], over_core(sent).astype(f32)[:, :, None], 2)
            out_list.append(out.reshape(heads, -1))
        else:
            dz = ordered(core, dz_keep, dz_send, 1)
            df = ordered(core, df_keep, df_send, 1)
            do = ordered(core, do_keep, do_send, 1)
            for lhs, rhs, bucket in ((u, dz, up_list), (g, df, down_list)):
                grad = dot(lhs, rhs, TN).reshape(-1)
                grad = grad + over_mp(grad)
                bucket.append(lax.psum_scatter(grad, "dp", scatter_dimension=0, tiled=True))
            sides = []
            for grads, part in ((d_own, cq[:, :cols]), (d_oth, cq[:, cols:])):
                qkv = jnp.stack([dot(act, grad, TN) for grad in grads])
                qkv = qkv.reshape(3, width, heads, HEAD).transpose(2, 0, 1, 3)
                sides.append((qkv.reshape(heads, -1), dot(part, do, TN).reshape(heads, -1)))
            for k, bucket in ((0, qkv_list), (1, out_list)):
                grad = sides[0][k] + over_mp(sides[1][k])
                bucket.append(lax.psum_scatter(grad, "dp", scatter_dimension=1, tiled=True))

    grad_input = spread_row(dx, over_mp(dx[half_seq:].astype(bf16)))
    small = jnp.stack(small_list[::-1])
    small = small + over_mp(small)
    for bit in range(bits):
        small = small + over_bit(small, bit)
    grad_bias_qv = lax.dynamic_slice_in_dim(small[:, :2], side * cols, cols, 2)
    return (
        hidden_out,
        grad_input,
        jnp.stack(qkv_list[::-1]),
        grad_bias_qv,
        jnp.stack(out_list[::-1]),
        small[:, 2:6],
        small[:, 6:8],
        jnp.stack(up_list[::-1]),
        small[:, 8:].reshape(layers, hidden),
        jnp.stack(down_list[::-1]),
    )


def solution(mesh):
    return jax.shard_map(
        local,
        mesh=mesh,
        in_specs=(
            P("dp", "mp", None),
            P("dp", "mp", None),
            P("dp", None),
            P(),
            P(None, None, None, "mp"),
            P(None, None, "mp"),
            P(None, "mp", None),
            P(),
            P(),
            P(),
            P(),
            P(),
        ),
        out_specs=(
            P("dp", "mp", None),
            P("dp", "mp", None),
            P(None, "mp", "dp"),
            P(None, None, "mp"),
            P(None, "mp", "dp"),
            P(),
            P(),
            P(None, "dp"),
            P(),
            P(None, "dp"),
        ),
        check_vma=False,
    )
```

time: 1730 us -> 580 us (0.34)
  waiting for transfers between devices: 1250 us -> 178 us
  matrix products: 228 us -> 0 us
  Pallas kernels: 0 us -> 171 us
  starting transfers between devices: 2.64 us -> 47.7 us
  blocking collectives: 42.1 us -> 0 us
  other arithmetic: 64.1 us -> 42.3 us
  local copies, waits for them, and re-layouts: 110 us -> 131 us
    reduce_scatter x12 -> x0, waiting for transfers between devices: 748 us -> none  [the longest x2 192 us: local(): lax.psum_scatter(down_grid, 'mp', scatter_dimension=1, tiled=True)]
    unnamed x19 -> x0, waiting for transfers between devices: 333 us -> none
    dot_general x36 -> x0, matrix products: 228 us -> none  [the longest x2 45.6 us: local(): jnp.einsum('rsd,df->rsf', quant_ff, w_up[layer_index], preferred_element_...]
    ppermute x0 -> x56, waiting for transfers between devices: none -> 178 us  [the longest x42 93.1 us: over_bit(): lax.ppermute(value, 'dp', [(i, i ^ 1 << bit) for i in range(dp_count)])]
    pallas_call x0 -> x14, Pallas kernels: none -> 171 us  [the longest x2 47 us: ff_bwd(): pl.pallas_call(ff_bwd_kernel, grid_spec=pltpu.PrefetchScalarGridSpec(num_...]
    psum x1 -> x0, waiting for transfers between devices: 91.3 us -> none  [local(): lax.psum((d_bias_qv, d_gains, d_vectors, d_bias_up), 'dp')]
    all_gather x4 -> x0, waiting for transfers between devices: 82.2 us -> none  [the longest x2 54.9 us: local(): gathered = lax.all_gather(quant_in, 'mp', axis=1, tiled=True)]
    reshape x10 -> x5, local copies, waits for them, and re-layouts: 69.8 us -> 1.6 us  [the longest x2 1.56 us: local(): out = packed[share:].reshape(heads, 2, 4, cols)]
  transfers between devices with their start and end apart: 18 -> 56, of which waited for: 16 -> 20; matrix products, arithmetic and copies ran while one was open for 11% -> 18% of each run, Pallas kernels for 0% -> 12%
where the time goes in v1:
time: 580 us; the launch traced here: 573 us
  waiting for transfers between devices  178 us (31%)
  Pallas kernels  171 us (29%)
  local copies, waits for them, and re-layouts  131 us (23%)
  starting transfers between devices  47.7 us (8%)
  other arithmetic  42.3 us (7%)
    ppermute x42, waiting for transfers between devices, over_bit(): lax.ppermute(value, 'dp', [(i, i ^ 1 << bit) for i in range(dp_count)])  93.1 us
    ppermute x14, waiting for transfers between devices, over_mp(): return lax.ppermute(value, 'mp', [(0, 1), (1, 0)])  84.9 us
    unnamed x280, local copies, waits for them, and re-layouts  62.6 us
    pallas_call x2, Pallas kernels, ff_bwd(): pl.pallas_call(ff_bwd_kernel, grid_spec=pltpu.PrefetchScalarGridSpec(num_...  47 us
    pallas_call x2, Pallas kernels, ff_fwd(): pl.pallas_call(functools.partial(ff_fwd_kernel, last), grid=(steps,), in_...  38.6 us
    ppermute x42, starting transfers between devices, over_bit(): lax.ppermute(value, 'dp', [(i, i ^ 1 << bit) for i in range(dp_count)])  32 us
    pallas_call x2, Pallas kernels, attn_bwd(): pl.pallas_call(attn_bwd_kernel, grid=(steps,), in_specs=[pl.BlockSpec(mem...  30.4 us
    pallas_call x2, Pallas kernels, w_ff(): pl.pallas_call(w_ff_kernel, grid=(steps,), in_specs=[whole(seq, width), w...  23.4 us
  transfers between devices with their start and end apart: 56, of which 20 were waited for; matrix products, arithmetic and copies ran while one was open for 18% of the time, Pallas kernels for 12%

profile of v1, /device:TPU:0, one launch (start us, length us, event | category | flops | bytes accessed | tf_op | source)
XLA Modules:
  0.0 573.0 jit_solution(2561929294814543302)
XLA Ops:
  0.7 2.3 dynamic-slice_bitcast_fusion.13
  3.0 3.0 collective-permute-start
  6.1 2.0 collective-permute-start.11
  9.2 4.7 fusion.30
  13.8 2.7 fusion.33
  17.6 1.7 dynamic-slice_bitcast_fusion.17
  19.5 8.0 %slice_bitcast_fusion = (bf16[3072,768]{1,0:T(8,128)(2,1)}, bf16[3072,768]{1,0:T(8,128)(2,1)}) fusion(bf16[2,3072,768]{2,1,0:T(8,128)(2,1)} %param.23), kind=kLoop, calls=%fused_computation.4 | loop fusion | bytes 18874368 | tf_op jit(solution)/shard_map/squeeze | solution.py:712
  32.4 8.3 %slice_bitcast_fusion.1 = (bf16[768,3072]{1,0:T(8,128)(2,1)}, bf16[768,3072]{1,0:T(8,128)(2,1)}) fusion(bf16[2,768,3072]{2,1,0:T(8,128)(2,1)} %param.21), kind=kLoop, calls=%fused_computation.5 | loop fusion | bytes 18874368 | tf_op jit(solution)/shard_map/squeeze | solution.py:712
  40.8 12.3 %collective-permute-done.1 = bf16[3,384,384]{2,1,0:T(8,128)(2,1)} collective-permute-done((bf16[3,384,384]{2,1,0:T(8,128)(2,1)S(1)}, bf16[3,384,384]{2,1,0:T(8,128)(2,1)}, u32[]{:S(2)}, u32[]{:S(2)}) %collective-permute-start.1) | collective-permute-done | bytes 884768 | tf_op jit(solution)/shard_map/ppermute | solution.py:652
  56.0 5.9 %attn_fwd.4 = (bf16[512,384]{1,0:T(8,128)(2,1)S(1)}, bf16[512,384]{1,0:T(8,128)(2,1)S(1)}, bf16[512,384]{1,0:T(8,128)(2,1)S(1)}, f32[512,384]{1,0:T(8,128)S(1)}, f32[3,8,512]{2,1,0:T(8,128)S(1)}) custom-call(bf16[512,768]{1,0:T(8,128)(2,1)S(1)} %multiply_convert_fusion.a_ref, bf16[3,768,384]{2,1,0:T(8,128)(2,1)S(1)} %get-tuple-element.235.w_ref.wo_ref, ...), custom_call_target="tpu_custom_call" | custom-call | flops 2516582400 | bytes 5242880 | tf_op jit(solution)/shard_map/attn_fwd/pallas_call | solution.py:83
  62.0 2.5 collective-permute-done.4
  66.5 1.9 pad_maximum_fusion.9.dx_ref
  68.5 1.7 collective-permute-start.8
  71.3 5.7 attn_fwd.5
  79.4 15.2 %collective-permute-done.8 = bf16[192,768]{1,0:T(8,128)(2,1)S(1)} collective-permute-done((bf16[192,768]{1,0:T(8,128)(2,1)S(1)}, bf16[192,768]{1,0:T(8,128)(2,1)S(1)}, u32[]{:S(2)}, u32[]{:S(2)}) %collective-permute-start.8) | collective-permute-done | bytes 294944 | tf_op jit(solution)/shard_map/ppermute | solution.py:652
  95.1 19.3 %ff_fwd.2 = (bf16[512,768]{1,0:T(8,128)(2,1)S(1)}, f32[512,768]{1,0:T(8,128)}, f32[512,128]{1,0:T(8,128)S(1)}, bf16[512,768]{1,0:T(8,128)(2,1)S(1)}, bf16[512,30...) custom-call(f32[5]{0:T(128)S(1)} %pad_maximum_fusion.20.clip_ref, ...), custom_call_target="tpu_custom_call" | custom-call | flops 9663676416 | bytes 20971520 | tf_op jit(solution)/shard_map/ff_fwd/pallas_call | solution.py:203
  116.7 5.7 attn_fwd.6
  123.4 5.7 attn_fwd.7
  129.9 19.3 %ff_fwd.3 = (bf16[512,768]{1,0:T(8,128)(2,1)}, f32[512,768]{1,0:T(8,128)}, f32[512,128]{1,0:T(8,128)S(1)}, bf16[512,768]{1,0:T(8,128)(2,1)S(1)}, bf16[512,3072]{...) custom-call(f32[5]{0:T(128)S(1)} %pad_maximum_fusion.19.clip_ref, ...), custom_call_target="tpu_custom_call" | custom-call | flops 9663676416 | bytes 20971520 | tf_op jit(solution)/shard_map/ff_fwd/pallas_call | solution.py:203
  151.0 23.2 %ff_bwd.2 = (bf16[512,1536]{1,0:T(8,128)(2,1)}, bf16[512,1536]{1,0:T(8,128)(2,1)}, bf16[512,384]{1,0:T(8,128)(2,1)S(1)}, bf16[512,384]{1,0:T(8,128)(2,1)S(1)}, b...) custom-call(s32[1]{0:T(128)} %bitcast.31.core_ref, ...), custom_call_target="tpu_custom_call" | custom-call | flops 9663676416 | bytes 20971520 | tf_op jit(solution)/shard_map/ff_bwd/pallas_call | solution.py:363
  185.5 15.0 %attn_bwd.2 = (bf16[512,384]{1,0:T(8,128)(2,1)S(1)}, bf16[512,384]{1,0:T(8,128)(2,1)S(1)}, bf16[512,384]{1,0:T(8,128)(2,1)S(1)}, bf16[512,384]{1,0:T(8,128)(2,1)...) custom-call(f32[5]{0:T(128)S(1)} %pad_maximum_fusion.19.clip_ref, ...), custom_call_target="tpu_custom_call" | custom-call | flops 12280922112 | bytes 14680064 | tf_op jit(solution)/shard_map/attn_bwd/pallas_call | solution.py:487
  208.4 23.8 %ff_bwd.3 = (bf16[512,1536]{1,0:T(8,128)(2,1)}, bf16[512,1536]{1,0:T(8,128)(2,1)}, bf16[512,384]{1,0:T(8,128)(2,1)S(1)}, bf16[512,384]{1,0:T(8,128)(2,1)S(1)}, b...) custom-call(s32[1]{0:T(128)} %bitcast.31.core_ref, ...), custom_call_target="tpu_custom_call" | custom-call | flops 9663676416 | bytes 20971520 | tf_op jit(solution)/shard_map/ff_bwd/pallas_call | solution.py:363
  251.6 15.4 %attn_bwd.3 = (bf16[512,384]{1,0:T(8,128)(2,1)S(1)}, bf16[512,384]{1,0:T(8,128)(2,1)S(1)}, bf16[512,384]{1,0:T(8,128)(2,1)S(1)}, bf16[512,384]{1,0:T(8,128)(2,1)...) custom-call(f32[5]{0:T(128)S(1)} %pad_maximum_fusion.20.clip_ref, ...), custom_call_target="tpu_custom_call" | custom-call | flops 12280922112 | bytes 14680064 | tf_op jit(solution)/shard_map/attn_bwd/pallas_call | solution.py:487
  268.8 3.9 collective-permute-done.29
  273.5 1.8 collective-permute-done.30
  275.3 1.7 collective-permute-start.31
  277.0 3.2 collective-permute-done.31
  280.2 1.8 collective-permute-start.32
  282.0 2.9 collective-permute-done.32
  285.5 2.8 collective-permute-start.33
  288.3 4.0 w_att.2
  297.5 8.6 %collective-permute-done.12 = bf16[256,768]{1,0:T(8,128)(2,1)} collective-permute-done((bf16[256,768]{1,0:T(8,128)(2,1)}, bf16[256,768]{1,0:T(8,128)(2,1)}, u32[]{:S(2)}, u32[]{:S(2)}) %collective-permute-start.12) | collective-permute-done | bytes 393248 | tf_op jit(solution)/shard_map/ppermute | solution.py:652
  315.8 5.1 w_att.3
  333.5 11.5 %w_ff.2 = bf16[8,768,384]{2,1,0:T(8,128)(2,1)} custom-call(bf16[512,768]{1,0:T(8,128)(2,1)S(1)} %copy-done.40, bf16[512,768]{1,0:T(8,128)(2,1)S(1)} %copy-done.42, bf16[512,1536]{1,0:T(8,128)(2,1)S(1)} %copy-done.52, bf16[512,1536]{1,0:T(8,128)(2,1)S(1)} %collective-permute-done.37.zo_ref, bf16[512,3072]{1,0:T(8,128)(2,1)} %get-tuple-element.191.gm_ref, ...), custom_call_target="tpu_custom_call" | custom-call | flops 4831838208 | bytes 17825792 | tf_op jit(solution)/shard_map/w_ff/pallas_call | solution.py:545
  345.0 9.5 %collective-permute-done.17 = bf16[8,192,384]{2,1,0:T(8,128)(2,1)S(1)} collective-permute-done((bf16[8,192,384]{2,1,0:T(8,128)(2,1)S(1)}, bf16[8,192,384]{2,1,0:T(8,128)(2,1)S(1)}, u32[]{:S(2)}, u32[]{:S(2)}) %collective-permute-start.17) | collective-permute-done | bytes 1179680 | tf_op jit(solution)/shard_map/ppermute | solution.py:652
  357.3 1.6 dynamic-slice_bitcast_fusion.1
  363.7 15.2 %collective-permute-done.25 = bf16[8,192,384]{2,1,0:T(8,128)(2,1)} collective-permute-done((bf16[8,192,384]{2,1,0:T(8,128)(2,1)}, bf16[8,192,384]{2,1,0:T(8,128)(2,1)}, u32[]{:S(2)}, u32[]{:S(2)}) %collective-permute-start.25) | collective-permute-done | bytes 1179680 | tf_op jit(solution)/shard_map/ppermute | solution.py:652
  378.9 1.8 maximum_add_fusion.1
  382.0 2.2 copy.101
  384.7 2.2 copy.80
  386.9 1.7 fusion.5
  391.8 11.9 %w_ff.3 = bf16[8,768,384]{2,1,0:T(8,128)(2,1)} custom-call(bf16[512,768]{1,0:T(8,128)(2,1)S(1)} %copy-done.37, bf16[512,768]{1,0:T(8,128)(2,1)S(1)} %collective-permute-done.45.uo_ref, bf16[512,1536]{1,0:T(8,128)(2,1)S(1)} %copy-done.51, bf16[512,1536]{1,0:T(8,128)(2,1)S(1)} %collective-permute-done.46.zo_ref, bf16[512,3072]{1,0:T(8,128)(2,1)} %get-tuple-element.197.gm_ref, ...), custom_call_target="tpu_custom_call" | custom-call | flops 4831838208 | bytes 17825792 | tf_op jit(solution)/shard_map/w_ff/pallas_call | solution.py:545
  403.7 3.3 dynamic-slice_bitcast_fusion
  407.8 2.1 collective-permute-start.20
  409.9 25.7 %collective-permute-done.26 = bf16[2,2,192,384]{3,2,1,0:T(8,128)(2,1)} collective-permute-done((bf16[2,2,192,384]{3,2,1,0:T(8,128)(2,1)S(1)}, bf16[2,2,192,384]{3,2,1,0:T(8,128)(2,1)}, u32[]{:S(2)}, u32[]{:S(2)}) %collective-permute-start.26) | collective-permute-done | bytes 589856 | tf_op jit(solution)/shard_map/ppermute | solution.py:655
  439.5 2.9 fusion.1
  445.8 1.7 copy.85
  451.4 1.9 stack_reshape.24
  454.4 1.7 collective-permute-start.28
  457.6 14.7 %collective-permute-done.28 = bf16[192,384]{0,1:T(8,128)(2,1)S(1)} collective-permute-done((bf16[192,384]{0,1:T(8,128)(2,1)S(1)}, bf16[192,384]{0,1:T(8,128)(2,1)S(1)}, u32[]{:S(2)}, u32[]{:S(2)}) %collective-permute-start.28) | collective-permute-done | bytes 147488 | tf_op jit(solution)/shard_map/ppermute | solution.py:655
  474.4 1.6 fusion.3
  476.1 2.7 collective-permute-start.42
  480.0 3.3 collective-permute-done.49
  483.3 2.9 fusion
  489.0 16.6 %collective-permute-done.42 = bf16[768,384]{1,0:T(8,128)(2,1)S(1)} collective-permute-done((bf16[768,384]{1,0:T(8,128)(2,1)S(1)}, bf16[768,384]{1,0:T(8,128)(2,1)S(1)}, u32[]{:S(2)}, u32[]{:S(2)}) %collective-permute-start.42) | collective-permute-done | bytes 589856 | tf_op jit(solution)/shard_map/ppermute | solution.py:655
  505.8 1.6 collective-permute-start.43
  512.1 8.6 %collective-permute-done.43 = bf16[768,384]{1,0:T(8,128)(2,1)S(1)} collective-permute-done((bf16[768,384]{1,0:T(8,128)(2,1)S(1)}, bf16[768,384]{1,0:T(8,128)(2,1)S(1)}, u32[]{:S(2)}, u32[]{:S(2)}) %collective-permute-start.43) | collective-permute-done | bytes 589856 | tf_op jit(solution)/shard_map/ppermute | solution.py:652
  520.9 1.8 collective-permute-done.50
  522.7 1.6 fusion.2
  524.4 3.5 collective-permute-start.51
  528.8 21.6 %collective-permute-done.51 = bf16[768,384]{1,0:T(8,128)(2,1)S(1)} collective-permute-done((bf16[768,384]{1,0:T(8,128)(2,1)S(1)}, bf16[768,384]{1,0:T(8,128)(2,1)S(1)}, u32[]{:S(2)}, u32[]{:S(2)}) %collective-permute-start.51) | collective-permute-done | bytes 589856 | tf_op jit(solution)/shard_map/ppermute | solution.py:655
  554.7 9.2 %collective-permute-done.52 = bf16[768,384]{1,0:T(8,128)(2,1)S(1)} collective-permute-done((bf16[768,384]{1,0:T(8,128)(2,1)S(1)}, bf16[768,384]{1,0:T(8,128)(2,1)S(1)}, u32[]{:S(2)}, u32[]{:S(2)}) %collective-permute-start.52) | collective-permute-done | bytes 589856 | tf_op jit(solution)/shard_map/ppermute | solution.py:652
  568.9 1.9 pad_maximum_fusion.6
  570.8 1.9 pad_maximum_fusion.5
  (486 shorter events, 138.9 us)
Async XLA Ops:
  3.0 28.4 %collective-permute-start = (bf16[256,768]{1,0:T(8,128)(2,1)}, bf16[256,768]{1,0:T(8,128)(2,1)S(1)}, u32[]{:S(2)}, u32[]{:S(2)}) collective-permute-start(bf16[256,768]{1,0:T(8,128)(2,1)} %get-tuple-element.302), channel_id=1, source_target_pairs={{0,1},{1,0},{2,3},{3,2},{4,5},{5,4},{6,7},{7,6},{8,9},{9,8},{10,11... | collective-permute-start | bytes 1179656 | tf_op jit(solution)/shard_map/ppermute | solution.py:652
  6.0 48.8 %collective-permute-start.3 = (f32[2,2,384]{2,1,0:T(2,128)S(1)}, f32[2,2,384]{2,1,0:T(2,128)S(1)}, u32[]{:S(2)}, u32[]{:S(2)}) collective-permute-start(f32[2,2,384]{2,1,0:T(2,128)S(1)} %copy-done.131), channel_id=1, source_target_pairs={{0,1},{1,0},{2,3},{3,2},{4,5},{5,4},{6,7},{7,6},{8,9},{9,8},{10,11... | collective-permute-start | bytes 18440 | tf_op jit(solution)/shard_map/ppermute | solution.py:652
  6.1 60.4 %collective-permute-start.11 = (bf16[256,768]{1,0:T(8,128)(2,1)}, bf16[256,768]{1,0:T(8,128)(2,1)}, u32[]{:S(2)}, u32[]{:S(2)}) collective-permute-start(bf16[256,768]{1,0:T(8,128)(2,1)} %get-tuple-element.259), channel_id=1, source_target_pairs={{0,1},{1,0},{2,3},{3,2},{4,5},{5,4},{6,7},{7,6},{8,9},{9,8},{10,11... | collective-permute-start | bytes 1179656 | tf_op jit(solution)/shard_map/ppermute | solution.py:652
  19.5 36.5 %copy-start.22 = (bf16[512,128]{1,0:T(8,128)(2,1)}, bf16[512,128]{1,0:T(8,128)(2,1)S(1)}, u32[]{:S(2)}) copy-start(bf16[512,128]{1,0:T(8,128)(2,1)S(1)} %select_convert_fusion.1.sq_ref) | copy-start | bytes 393220
  32.4 20.7 %collective-permute-start.1 = (bf16[3,384,384]{2,1,0:T(8,128)(2,1)S(1)}, bf16[3,384,384]{2,1,0:T(8,128)(2,1)}, u32[]{:S(2)}, u32[]{:S(2)}) collective-permute-start(bf16[3,384,384]{2,1,0:T(8,128)(2,1)S(1)} %dynamic-slice_bitcast_fusion.5), channel_id=1, source_target_pairs={{0,1},{1,0},{2,3},{3,2},{4,5},{5,4},{6,7},{7,6},{8,9},{9,8},{10,11... | collective-permute-start | bytes 2654216 | tf_op jit(solution)/shard_map/ppermute | solution.py:652
  53.0 11.4 %collective-permute-start.2 = (bf16[3,384,384]{2,1,0:T(8,128)(2,1)}, bf16[3,384,384]{2,1,0:T(8,128)(2,1)}, u32[]{:S(2)}, u32[]{:S(2)}) collective-permute-start(bf16[3,384,384]{2,1,0:T(8,128)(2,1)} %collective-permute-done.1), channel_id=1, source_target_pairs={{0,2},{2,0},{4,6},{6,4},{8,10},{10,8},{12,14},{14,12},{16,18},{18,... | collective-permute-start | bytes 2654216 | tf_op jit(solution)/shard_map/ppermute | solution.py:655
  54.8 9.7 %collective-permute-start.4 = (bf16[192,768]{1,0:T(8,128)(2,1)}, bf16[192,768]{1,0:T(8,128)(2,1)S(1)}, u32[]{:S(2)}, u32[]{:S(2)}) collective-permute-start(bf16[192,768]{1,0:T(8,128)(2,1)} %dynamic-slice_bitcast_fusion.17), channel_id=1, source_target_pairs={{0,1},{1,0},{2,3},{3,2},{4,5},{5,4},{6,7},{7,6},{8,9},{9,8},{10,11... | collective-permute-start | bytes 884744 | tf_op jit(solution)/shard_map/ppermute | solution.py:652
  61.9 33.1 %copy-start.75 = (f32[512,384]{1,0:T(8,128)}, f32[512,384]{1,0:T(8,128)S(1)}, u32[]{:S(2)}) copy-start(f32[512,384]{1,0:T(8,128)S(1)} %get-tuple-element.105.co_ref) | copy-start | bytes 2359300
  64.4 4.0 collective-permute-start.5
  66.1 28.5 %collective-permute-start.6 = (bf16[3,384,384]{2,1,0:T(8,128)(2,1)S(1)}, bf16[3,384,384]{2,1,0:T(8,128)(2,1)S(1)}, u32[]{:S(2)}, u32[]{:S(2)}) collective-permute-start(bf16[3,384,384]{2,1,0:T(8,128)(2,1)S(1)} %copy-done.123), channel_id=1, source_target_pairs={{0,1},{1,0},{2,3},{3,2},{4,5},{5,4},{6,7},{7,6},{8,9},{9,8},{10,11... | collective-permute-start | bytes 2654216 | tf_op jit(solution)/shard_map/ppermute | solution.py:652
  68.5 26.5 %copy-start.14 = (bf16[384,768]{1,0:T(8,128)(2,1)}, bf16[384,768]{1,0:T(8,128)(2,1)S(1)}, u32[]{:S(2)}) copy-start(bf16[384,768]{1,0:T(8,128)(2,1)S(1)} %pad_maximum_fusion.10.wt_ref) | copy-start | bytes 1769476
  68.5 26.0 %collective-permute-start.8 = (bf16[192,768]{1,0:T(8,128)(2,1)S(1)}, bf16[192,768]{1,0:T(8,128)(2,1)S(1)}, u32[]{:S(2)}, u32[]{:S(2)}) collective-permute-start(bf16[192,768]{1,0:T(8,128)(2,1)S(1)} %dynamic-slice_bitcast_fusion.16), channel_id=1, source_target_pairs={{0,1},{1,0},{2,3},{3,2},{4,5},{5,4},{6,7},{7,6},{8,9},{9,8},{10,11... | collective-permute-start | bytes 884744 | tf_op jit(solution)/shard_map/ppermute | solution.py:652
  79.4 35.0 %copy-start.93 = (bf16[512,384]{1,0:T(8,128)(2,1)}, bf16[512,384]{1,0:T(8,128)(2,1)S(1)}, u32[]{:S(2)}) copy-start(bf16[512,384]{1,0:T(8,128)(2,1)S(1)} %get-tuple-element.146.vt_ref) | copy-start | bytes 1179652
  79.4 35.0 %copy-start.111 = (f32[3,8,512]{2,1,0:T(8,128)}, f32[3,8,512]{2,1,0:T(8,128)S(1)}, u32[]{:S(2)}) copy-start(f32[3,8,512]{2,1,0:T(8,128)S(1)} %get-tuple-element.147.lt_ref) | copy-start | bytes 147460
  94.5 27.9 %collective-permute-start.9 = (bf16[192,768]{1,0:T(8,128)(2,1)S(1)}, bf16[192,768]{1,0:T(8,128)(2,1)S(1)}, u32[]{:S(2)}, u32[]{:S(2)}) collective-permute-start(bf16[192,768]{1,0:T(8,128)(2,1)S(1)} %collective-permute-done.8), channel_id=1, source_target_pairs={{0,2},{2,0},{4,6},{6,4},{8,10},{10,8},{12,14},{14,12},{16,18},{18,... | collective-permute-start | bytes 884744 | tf_op jit(solution)/shard_map/ppermute | solution.py:655
  94.5 28.0 %collective-permute-start.7 = (bf16[3,384,384]{2,1,0:T(8,128)(2,1)S(1)}, bf16[3,384,384]{2,1,0:T(8,128)(2,1)S(1)}, u32[]{:S(2)}, u32[]{:S(2)}) collective-permute-start(bf16[3,384,384]{2,1,0:T(8,128)(2,1)S(1)} %collective-permute-done.6), channel_id=1, source_target_pairs={{0,2},{2,0},{4,6},{6,4},{8,10},{10,8},{12,14},{14,12},{16,18},{18,... | collective-permute-start | bytes 2654216 | tf_op jit(solution)/shard_map/ppermute | solution.py:655
  151.0 25.5 %copy-start.82 = (f32[512,384]{1,0:T(8,128)S(1)}, f32[512,384]{1,0:T(8,128)}, u32[]{:S(2)}) copy-start(f32[512,384]{1,0:T(8,128)} %copy-done.81) | copy-start | bytes 2359300
  208.3 27.9 %copy-start.24 = (bf16[512,128]{1,0:T(8,128)(2,1)S(1)}, bf16[512,128]{1,0:T(8,128)(2,1)}, u32[]{:S(2)}) copy-start(bf16[512,128]{1,0:T(8,128)(2,1)} %copy-done.22) | copy-start | bytes 393220
  267.9 4.8 collective-permute-start.29
  268.3 64.2 %collective-permute-start.38 = (bf16[512,3072]{1,0:T(8,128)(2,1)}, bf16[512,3072]{1,0:T(8,128)(2,1)}, u32[]{:S(2)}, u32[]{:S(2)}) collective-permute-start(bf16[512,3072]{1,0:T(8,128)(2,1)} %get-tuple-element.191.gm_ref), channel_id=1, source_target_pairs={{0,2},{2,0},{4,6},{6,4},{8,10},{10,8},{12,14},{14,12},{16,18},{18,... | collective-permute-start | bytes 9437192 | tf_op jit(solution)/shard_map/ppermute | solution.py:655
  268.3 16.6 %collective-permute-start.13 = (bf16[512,768]{1,0:T(8,128)(2,1)S(1)}, bf16[512,768]{1,0:T(8,128)(2,1)S(1)}, u32[]{:S(2)}, u32[]{:S(2)}) collective-permute-start(bf16[512,768]{1,0:T(8,128)(2,1)S(1)} %copy-done.44), channel_id=1, source_target_pairs={{0,2},{2,0},{4,6},{6,4},{8,10},{10,8},{12,14},{14,12},{16,18},{18,... | collective-permute-start | bytes 2359304 | tf_op jit(solution)/shard_map/ppermute | solution.py:655
  272.8 2.5 collective-permute-start.30
  272.9 19.3 %collective-permute-start.36 = (bf16[512,768]{1,0:T(8,128)(2,1)S(1)}, bf16[512,768]{1,0:T(8,128)(2,1)S(1)}, u32[]{:S(2)}, u32[]{:S(2)}) collective-permute-start(bf16[512,768]{1,0:T(8,128)(2,1)S(1)} %copy-done.39), channel_id=1, source_target_pairs={{0,2},{2,0},{4,6},{6,4},{8,10},{10,8},{12,14},{14,12},{16,18},{18,... | collective-permute-start | bytes 2359304 | tf_op jit(solution)/shard_map/ppermute | solution.py:655
  273.4 12.1 %collective-permute-start.14 = (bf16[512,384]{1,0:T(8,128)(2,1)S(1)}, bf16[512,384]{1,0:T(8,128)(2,1)S(1)}, u32[]{:S(2)}, u32[]{:S(2)}) collective-permute-start(bf16[512,384]{1,0:T(8,128)(2,1)S(1)} %copy-done.135), channel_id=1, source_target_pairs={{0,2},{2,0},{4,6},{6,4},{8,10},{10,8},{12,14},{14,12},{16,18},{18,... | collective-permute-start | bytes 1179656 | tf_op jit(solution)/shard_map/ppermute | solution.py:655
  275.3 4.9 collective-permute-start.31
  280.2 4.7 collective-permute-start.32
  284.9 21.3 %collective-permute-start.21 = (bf16[512,768]{1,0:T(8,128)(2,1)}, bf16[512,768]{1,0:T(8,128)(2,1)}, u32[]{:S(2)}, u32[]{:S(2)}) collective-permute-start(bf16[512,768]{1,0:T(8,128)(2,1)} %get-tuple-element.171.cm_ref), channel_id=1, source_target_pairs={{0,2},{2,0},{4,6},{6,4},{8,10},{10,8},{12,14},{14,12},{16,18},{18,... | collective-permute-start | bytes 2359304 | tf_op jit(solution)/shard_map/ppermute | solution.py:655
  284.9 11.3 %collective-permute-start.22 = (bf16[512,384]{1,0:T(8,128)(2,1)S(1)}, bf16[512,384]{1,0:T(8,128)(2,1)S(1)}, u32[]{:S(2)}, u32[]{:S(2)}) collective-permute-start(bf16[512,384]{1,0:T(8,128)(2,1)S(1)} %copy-done.134), channel_id=1, source_target_pairs={{0,2},{2,0},{4,6},{6,4},{8,10},{10,8},{12,14},{14,12},{16,18},{18,... | collective-permute-start | bytes 1179656 | tf_op jit(solution)/shard_map/ppermute | solution.py:655
  285.5 8.4 %collective-permute-start.33 = (f32[2,12,768]{2,1,0:T(8,128)S(1)}, f32[2,12,768]{2,1,0:T(8,128)S(1)}, u32[]{:S(2)}, u32[]{:S(2)}) collective-permute-start(f32[2,12,768]{2,1,0:T(8,128)S(1)} %add.196), channel_id=1, source_target_pairs={{0,16},{2,18},{4,20},{6,22},{8,24},{10,26},{12,28},{14,30},{16,0},... | collective-permute-start | bytes 221192 | tf_op jit(solution)/shard_map/ppermute | solution.py:655
  293.2 28.5 %collective-permute-start.16 = (bf16[8,144,384]{2,1,0:T(8,128)(2,1)}, bf16[8,144,384]{2,1,0:T(8,128)(2,1)}, u32[]{:S(2)}, u32[]{:S(2)}) collective-permute-start(bf16[8,144,384]{2,1,0:T(8,128)(2,1)} %get-tuple-element.163), channel_id=1, source_target_pairs={{0,2},{2,0},{4,6},{6,4},{8,10},{10,8},{12,14},{14,12},{16,18},{18,... | collective-permute-start | bytes 2654216 | tf_op jit(solution)/shard_map/ppermute | solution.py:655
  293.9 12.2 %collective-permute-start.12 = (bf16[256,768]{1,0:T(8,128)(2,1)}, bf16[256,768]{1,0:T(8,128)(2,1)}, u32[]{:S(2)}, u32[]{:S(2)}) collective-permute-start(bf16[256,768]{1,0:T(8,128)(2,1)} %slice.248), channel_id=1, source_target_pairs={{0,1},{1,0},{2,3},{3,2},{4,5},{5,4},{6,7},{7,6},{8,9},{9,8},{10,11... | collective-permute-start | bytes 1179656 | tf_op jit(solution)/shard_map/ppermute | solution.py:652
  297.0 23.9 %collective-permute-start.10 = (bf16[256,768]{1,0:T(8,128)(2,1)}, bf16[256,768]{1,0:T(8,128)(2,1)}, u32[]{:S(2)}, u32[]{:S(2)}) collective-permute-start(bf16[256,768]{1,0:T(8,128)(2,1)} %slice.178), channel_id=1, source_target_pairs={{0,1},{1,0},{2,3},{3,2},{4,5},{5,4},{6,7},{7,6},{8,9},{9,8},{10,11... | collective-permute-start | bytes 1179656 | tf_op jit(solution)/shard_map/ppermute | solution.py:652
  306.2 26.4 %collective-permute-start.37 = (bf16[512,1536]{1,0:T(8,128)(2,1)}, bf16[512,1536]{1,0:T(8,128)(2,1)S(1)}, u32[]{:S(2)}, u32[]{:S(2)}) collective-permute-start(bf16[512,1536]{1,0:T(8,128)(2,1)} %get-tuple-element.190), channel_id=1, source_target_pairs={{0,2},{2,0},{4,6},{6,4},{8,10},{10,8},{12,14},{14,12},{16,18},{18,... | collective-permute-start | bytes 4718600 | tf_op jit(solution)/shard_map/ppermute | solution.py:655
  306.2 19.4 %collective-permute-start.15 = (bf16[8,144,384]{2,1,0:T(8,128)(2,1)}, bf16[8,144,384]{2,1,0:T(8,128)(2,1)S(1)}, u32[]{:S(2)}, u32[]{:S(2)}) collective-permute-start(bf16[8,144,384]{2,1,0:T(8,128)(2,1)} %copy-done.35), channel_id=1, source_target_pairs={{0,2},{2,0},{4,6},{6,4},{8,10},{10,8},{12,14},{14,12},{16,18},{18,... | collective-permute-start | bytes 2654216 | tf_op jit(solution)/shard_map/ppermute | solution.py:655
  321.0 8.2 %collective-permute-start.24 = (bf16[8,144,384]{2,1,0:T(8,128)(2,1)S(1)}, bf16[8,144,384]{2,1,0:T(8,128)(2,1)S(1)}, u32[]{:S(2)}, u32[]{:S(2)}) collective-permute-start(bf16[8,144,384]{2,1,0:T(8,128)(2,1)S(1)} %get-tuple-element.178), channel_id=1, source_target_pairs={{0,2},{2,0},{4,6},{6,4},{8,10},{10,8},{12,14},{14,12},{16,18},{18,... | collective-permute-start | bytes 2654216 | tf_op jit(solution)/shard_map/ppermute | solution.py:655
  321.7 70.2 %collective-permute-start.47 = (bf16[512,3072]{1,0:T(8,128)(2,1)}, bf16[512,3072]{1,0:T(8,128)(2,1)}, u32[]{:S(2)}, u32[]{:S(2)}) collective-permute-start(bf16[512,3072]{1,0:T(8,128)(2,1)} %get-tuple-element.197.gm_ref), channel_id=1, source_target_pairs={{0,2},{2,0},{4,6},{6,4},{8,10},{10,8},{12,14},{14,12},{16,18},{18,... | collective-permute-start | bytes 9437192 | tf_op jit(solution)/shard_map/ppermute | solution.py:655
  325.6 28.9 %collective-permute-start.17 = (bf16[8,192,384]{2,1,0:T(8,128)(2,1)S(1)}, bf16[8,192,384]{2,1,0:T(8,128)(2,1)S(1)}, u32[]{:S(2)}, u32[]{:S(2)}) collective-permute-start(bf16[8,192,384]{2,1,0:T(8,128)(2,1)S(1)} %pad_maximum_fusion.3), channel_id=1, source_target_pairs={{0,1},{1,0},{2,3},{3,2},{4,5},{5,4},{6,7},{7,6},{8,9},{9,8},{10,11... | collective-permute-start | bytes 3538952 | tf_op jit(solution)/shard_map/ppermute | solution.py:652
  329.2 2.8 collective-permute-start.39
  332.0 59.8 %collective-permute-start.46 = (bf16[512,1536]{1,0:T(8,128)(2,1)}, bf16[512,1536]{1,0:T(8,128)(2,1)S(1)}, u32[]{:S(2)}, u32[]{:S(2)}) collective-permute-start(bf16[512,1536]{1,0:T(8,128)(2,1)} %get-tuple-element.196), channel_id=1, source_target_pairs={{0,2},{2,0},{4,6},{6,4},{8,10},{10,8},{12,14},{14,12},{16,18},{18,... | collective-permute-start | bytes 4718600 | tf_op jit(solution)/shard_map/ppermute | solution.py:655
  332.5 26.4 %collective-permute-start.23 = (bf16[8,144,384]{2,1,0:T(8,128)(2,1)S(1)}, bf16[8,144,384]{2,1,0:T(8,128)(2,1)S(1)}, u32[]{:S(2)}, u32[]{:S(2)}) collective-permute-start(bf16[8,144,384]{2,1,0:T(8,128)(2,1)S(1)} %get-tuple-element.175), channel_id=1, source_target_pairs={{0,2},{2,0},{4,6},{6,4},{8,10},{10,8},{12,14},{14,12},{16,18},{18,... | collective-permute-start | bytes 2654216 | tf_op jit(solution)/shard_map/ppermute | solution.py:655
  332.6 46.3 %collective-permute-start.25 = (bf16[8,192,384]{2,1,0:T(8,128)(2,1)}, bf16[8,192,384]{2,1,0:T(8,128)(2,1)}, u32[]{:S(2)}, u32[]{:S(2)}) collective-permute-start(bf16[8,192,384]{2,1,0:T(8,128)(2,1)} %pad_maximum_fusion.4), channel_id=1, source_target_pairs={{0,1},{1,0},{2,3},{3,2},{4,5},{5,4},{6,7},{7,6},{8,9},{9,8},{10,11... | collective-permute-start | bytes 3538952 | tf_op jit(solution)/shard_map/ppermute | solution.py:652
  355.8 28.4 %collective-permute-start.18 = (bf16[2,2,192,384]{3,2,1,0:T(8,128)(2,1)}, bf16[2,2,192,384]{3,2,1,0:T(8,128)(2,1)}, u32[]{:S(2)}, u32[]{:S(2)}) collective-permute-start(bf16[2,2,192,384]{3,2,1,0:T(8,128)(2,1)} %get-tuple-element.249), channel_id=1, source_target_pairs={{0,4},{2,6},{4,0},{6,2},{8,12},{10,14},{12,8},{14,10},{16,20},{18,... | collective-permute-start | bytes 1769480 | tf_op jit(solution)/shard_map/ppermute | solution.py:655
  358.9 80.6 %collective-permute-start.40 = (bf16[2,2,768,384]{3,2,1,0:T(8,128)(2,1)}, bf16[2,2,768,384]{3,2,1,0:T(8,128)(2,1)}, u32[]{:S(2)}, u32[]{:S(2)}) collective-permute-start(bf16[2,2,768,384]{3,2,1,0:T(8,128)(2,1)} %dynamic-slice_bitcast_fusion.1), channel_id=1, source_target_pairs={{0,4},{2,6},{4,0},{6,2},{8,12},{10,14},{12,8},{14,10},{16,20},{18,... | collective-permute-start | bytes 7077896 | tf_op jit(solution)/shard_map/ppermute | solution.py:655
  378.9 11.3 %collective-permute-start.45 = (bf16[512,768]{1,0:T(8,128)(2,1)S(1)}, bf16[512,768]{1,0:T(8,128)(2,1)S(1)}, u32[]{:S(2)}, u32[]{:S(2)}) collective-permute-start(bf16[512,768]{1,0:T(8,128)(2,1)S(1)} %copy-done.37), channel_id=1, source_target_pairs={{0,2},{2,0},{4,6},{6,4},{8,10},{10,8},{12,14},{14,12},{16,18},{18,... | collective-permute-start | bytes 2359304 | tf_op jit(solution)/shard_map/ppermute | solution.py:655
  384.2 4.5 collective-permute-start.48
  388.7 46.9 %collective-permute-start.26 = (bf16[2,2,192,384]{3,2,1,0:T(8,128)(2,1)S(1)}, bf16[2,2,192,384]{3,2,1,0:T(8,128)(2,1)}, u32[]{:S(2)}, u32[]{:S(2)}) collective-permute-start(bf16[2,2,192,384]{3,2,1,0:T(8,128)(2,1)S(1)} %copy-done.124), channel_id=1, source_target_pairs={{0,4},{2,6},{4,0},{6,2},{8,12},{10,14},{12,8},{14,10},{16,20},{18,... | collective-permute-start | bytes 1769480 | tf_op jit(solution)/shard_map/ppermute | solution.py:655
  390.3 17.3 %collective-permute-start.19 = (bf16[2,192,384]{1,2,0:T(8,128)(2,1)S(1)}, bf16[2,192,384]{1,2,0:T(8,128)(2,1)S(1)}, u32[]{:S(2)}, u32[]{:S(2)}) collective-permute-start(bf16[2,192,384]{1,2,0:T(8,128)(2,1)S(1)} %dynamic-slice_bitcast_fusion.11), channel_id=1, source_target_pairs={{0,8},{2,10},{4,12},{6,14},{8,0},{10,2},{12,4},{14,6},{16,24},{18,... | collective-permute-start | bytes 884744 | tf_op jit(solution)/shard_map/ppermute | solution.py:655
  407.1 29.9 %copy-start.119 = (bf16[2,2,1,192,384]{3,4,0,1,2:T(8,128)(2,1)S(1)}, bf16[2,2,1,192,384]{3,4,0,1,2:T(8,128)(2,1)}, u32[]{:S(2)}) copy-start(bf16[2,2,1,192,384]{3,4,0,1,2:T(8,128)(2,1)} %copy.101) | copy-start | bytes 1769476
  407.1 76.3 %collective-permute-start.49 = (bf16[2,2,768,384]{3,2,1,0:T(8,128)(2,1)}, bf16[2,2,768,384]{3,2,1,0:T(8,128)(2,1)}, u32[]{:S(2)}, u32[]{:S(2)}) collective-permute-start(bf16[2,2,768,384]{3,2,1,0:T(8,128)(2,1)} %dynamic-slice_bitcast_fusion), channel_id=1, source_target_pairs={{0,4},{2,6},{4,0},{6,2},{8,12},{10,14},{12,8},{14,10},{16,20},{18,... | collective-permute-start | bytes 7077896 | tf_op jit(solution)/shard_map/ppermute | solution.py:655
  407.8 36.3 %collective-permute-start.20 = (bf16[192,384]{0,1:T(8,128)(2,1)S(1)}, bf16[192,384]{0,1:T(8,128)(2,1)}, u32[]{:S(2)}, u32[]{:S(2)}) collective-permute-start(bf16[192,384]{0,1:T(8,128)(2,1)S(1)} %dynamic-slice_bitcast_fusion.19), channel_id=1, source_target_pairs={{0,16},{2,18},{4,20},{6,22},{8,24},{10,26},{12,28},{14,30},{16,0},... | collective-permute-start | bytes 442376 | tf_op jit(solution)/shard_map/ppermute | solution.py:655
  437.9 15.4 %collective-permute-start.27 = (bf16[2,192,384]{1,2,0:T(8,128)(2,1)}, bf16[2,192,384]{1,2,0:T(8,128)(2,1)}, u32[]{:S(2)}, u32[]{:S(2)}) collective-permute-start(bf16[2,192,384]{1,2,0:T(8,128)(2,1)} %dynamic-slice_bitcast_fusion.10), channel_id=1, source_target_pairs={{0,8},{2,10},{4,12},{6,14},{8,0},{10,2},{12,4},{14,6},{16,24},{18,... | collective-permute-start | bytes 884744 | tf_op jit(solution)/shard_map/ppermute | solution.py:655
  443.6 30.8 %collective-permute-start.41 = (bf16[2,768,384]{2,1,0:T(8,128)(2,1)}, bf16[2,768,384]{2,1,0:T(8,128)(2,1)}, u32[]{:S(2)}, u32[]{:S(2)}) collective-permute-start(bf16[2,768,384]{2,1,0:T(8,128)(2,1)} %dynamic-slice_bitcast_fusion.3), channel_id=1, source_target_pairs={{0,8},{2,10},{4,12},{6,14},{8,0},{10,2},{12,4},{14,6},{16,24},{18,... | collective-permute-start | bytes 3538952 | tf_op jit(solution)/shard_map/ppermute | solution.py:655
  450.4 5.7 collective-permute-start.34
  454.4 17.9 %collective-permute-start.28 = (bf16[192,384]{0,1:T(8,128)(2,1)S(1)}, bf16[192,384]{0,1:T(8,128)(2,1)S(1)}, u32[]{:S(2)}, u32[]{:S(2)}) collective-permute-start(bf16[192,384]{0,1:T(8,128)(2,1)S(1)} %dynamic-slice_bitcast_fusion.18), channel_id=1, source_target_pairs={{0,16},{2,18},{4,20},{6,22},{8,24},{10,26},{12,28},{14,30},{16,0},... | collective-permute-start | bytes 442376 | tf_op jit(solution)/shard_map/ppermute | solution.py:655
  473.3 34.1 %collective-permute-start.35 = (bf16[6,4,384]{2,1,0:T(4,128)(2,1)}, bf16[6,4,384]{2,1,0:T(4,128)(2,1)}, u32[]{:S(2)}, u32[]{:S(2)}) collective-permute-start(bf16[6,4,384]{2,1,0:T(4,128)(2,1)} %fusion.27), channel_id=1, source_target_pairs={{0,2},{2,0},{4,6},{6,4},{8,10},{10,8},{12,14},{14,12},{16,18},{18,... | collective-permute-start | bytes 55304 | tf_op jit(solution)/shard_map/ppermute | solution.py:655
  476.1 29.5 %collective-permute-start.42 = (bf16[768,384]{1,0:T(8,128)(2,1)S(1)}, bf16[768,384]{1,0:T(8,128)(2,1)S(1)}, u32[]{:S(2)}, u32[]{:S(2)}) collective-permute-start(bf16[768,384]{1,0:T(8,128)(2,1)S(1)} %dynamic-slice_bitcast_fusion.7), channel_id=1, source_target_pairs={{0,16},{2,18},{4,20},{6,22},{8,24},{10,26},{12,28},{14,30},{16,0},... | collective-permute-start | bytes 1769480 | tf_op jit(solution)/shard_map/ppermute | solution.py:655
  487.4 35.3 %collective-permute-start.50 = (bf16[2,768,384]{2,1,0:T(8,128)(2,1)}, bf16[2,768,384]{2,1,0:T(8,128)(2,1)}, u32[]{:S(2)}, u32[]{:S(2)}) collective-permute-start(bf16[2,768,384]{2,1,0:T(8,128)(2,1)} %dynamic-slice_bitcast_fusion.2), channel_id=1, source_target_pairs={{0,8},{2,10},{4,12},{6,14},{8,0},{10,2},{12,4},{14,6},{16,24},{18,... | collective-permute-start | bytes 3538952 | tf_op jit(solution)/shard_map/ppermute | solution.py:655
  505.8 15.0 %collective-permute-start.43 = (bf16[768,384]{1,0:T(8,128)(2,1)S(1)}, bf16[768,384]{1,0:T(8,128)(2,1)S(1)}, u32[]{:S(2)}, u32[]{:S(2)}) collective-permute-start(bf16[768,384]{1,0:T(8,128)(2,1)S(1)} %fusion.7), channel_id=1, source_target_pairs={{0,1},{1,0},{2,3},{3,2},{4,5},{5,4},{6,7},{7,6},{8,9},{9,8},{10,11... | collective-permute-start | bytes 1769480 | tf_op jit(solution)/shard_map/ppermute | solution.py:652
  524.4 26.0 %collective-permute-start.51 = (bf16[768,384]{1,0:T(8,128)(2,1)S(1)}, bf16[768,384]{1,0:T(8,128)(2,1)S(1)}, u32[]{:S(2)}, u32[]{:S(2)}) collective-permute-start(bf16[768,384]{1,0:T(8,128)(2,1)S(1)} %dynamic-slice_bitcast_fusion.6), channel_id=1, source_target_pairs={{0,16},{2,18},{4,20},{6,22},{8,24},{10,26},{12,28},{14,30},{16,0},... | collective-permute-start | bytes 1769480 | tf_op jit(solution)/shard_map/ppermute | solution.py:655
  528.0 24.2 %collective-permute-start.54 = (bf16[192,384]{1,0:T(8,128)(2,1)S(1)}, bf16[192,384]{1,0:T(8,128)(2,1)S(1)}, u32[]{:S(2)}, u32[]{:S(2)}) collective-permute-start(bf16[192,384]{1,0:T(8,128)(2,1)S(1)} %fusion.19), channel_id=1, source_target_pairs={{0,2},{2,0},{4,6},{6,4},{8,10},{10,8},{12,14},{14,12},{16,18},{18,... | collective-permute-start | bytes 442376 | tf_op jit(solution)/shard_map/ppermute | solution.py:655
  528.2 25.4 %collective-permute-start.44 = (bf16[4,48,384]{2,0,1:T(4,128)(2,1)S(1)}, bf16[4,48,384]{2,0,1:T(4,128)(2,1)S(1)}, u32[]{:S(2)}, u32[]{:S(2)}) collective-permute-start(bf16[4,48,384]{2,0,1:T(4,128)(2,1)S(1)} %bitcast.234), channel_id=1, source_target_pairs={{0,2},{2,0},{4,6},{6,4},{8,10},{10,8},{12,14},{14,12},{16,18},{18,... | collective-permute-start | bytes 442376 | tf_op jit(solution)/shard_map/ppermute | solution.py:655
  550.6 13.3 %collective-permute-start.52 = (bf16[768,384]{1,0:T(8,128)(2,1)S(1)}, bf16[768,384]{1,0:T(8,128)(2,1)S(1)}, u32[]{:S(2)}, u32[]{:S(2)}) collective-permute-start(bf16[768,384]{1,0:T(8,128)(2,1)S(1)} %fusion.6), channel_id=1, source_target_pairs={{0,1},{1,0},{2,3},{3,2},{4,5},{5,4},{6,7},{7,6},{8,9},{9,8},{10,11... | collective-permute-start | bytes 1769480 | tf_op jit(solution)/shard_map/ppermute | solution.py:652
  564.2 1.4 collective-permute-start.55
  564.3 3.5 collective-permute-start.53
  (128 other events, 727.1 us)

commit v2 on v1

v2 whole, which is shorter than its diff:
```python
import functools

import jax
import jax.numpy as jnp
from jax import lax
from jax.experimental import pallas as pl
from jax.experimental.pallas import tpu as pltpu
from jax.sharding import PartitionSpec as P

HEAD = 64
PAIR = 2 * HEAD
EPS = 1e-06
BIG = -1e30
INV_SQRT2 = 0.7071067811865476
INV_SQRT2PI = 0.3989422804014327

f32 = jnp.float32
bf16 = jnp.bfloat16
MIB = 1024 * 1024
FF_CHUNK = 768
FF_SUB = 256

NT = (((1,), (1,)), ((), ()))
TN = (((0,), (0,)), ((), ()))


def dot(lhs, rhs, dims=(((1,), (0,)), ((), ()))):
    return lax.dot_general(lhs, rhs, dims, preferred_element_type=f32)


def whole(*dims):
    return pl.BlockSpec(dims, lambda *_: (0,) * len(dims))


def at_layer(layer, *dims):
    return pl.BlockSpec((None, *dims), lambda *_: (layer,) + (0,) * len(dims))


def smem():
    return pl.BlockSpec(memory_space=pltpu.SMEM)


class Spot:
    def __init__(self, array):
        self.array = array
        self.latest = ()


def launch(body, name, spot, hold, ins, outs, scratch=(), grid=(1,), us=3.0):
    count = len(ins)
    known = [array for array, _ in ins]
    hold = [array for array in (*hold, *spot.latest) if not any(array is k for k in known)]

    def kernel(spot_ref, *refs):
        body(spot_ref, *refs[:count], *refs[count + len(hold) :])

    in_specs = [spec for _, spec in ins] + [pl.BlockSpec(memory_space=pl.ANY)] * len(hold)
    results = pl.pallas_call(
        kernel,
        grid_spec=pltpu.PrefetchScalarGridSpec(
            num_scalar_prefetch=1,
            grid=grid,
            in_specs=in_specs,
            out_specs=[spec for spec, _ in outs],
            scratch_shapes=list(scratch),
        ),
        out_shape=[out for _, out in outs],
        compiler_params=pltpu.CompilerParams(vmem_limit_bytes=60 * MIB),
        cost_estimate=pl.CostEstimate(
            flops=int(us * 1e9), bytes_accessed=int(us * 1e6), transcendentals=0
        ),
        name=name,
    )(spot.array, *known, *hold)
    spot.latest = (results[0],)
    return results


def shape(dims, dtype):
    return jax.ShapeDtypeStruct(dims, dtype)


def head_mask(head, value):
    lane = lax.broadcasted_iota(jnp.int32, (1, PAIR), 1)
    return jnp.where((lane // HEAD) == head, value, 0.0).astype(bf16)


CORE, SIDE, AXIS_X, AXIS_Z0, AXIS_Z1 = range(5)


def enter_kernel(layer_limit, spot_ref, lim_ref, mine_ref, recv_ref, act_ref):
    limit = lim_ref[0, 0]
    inv = 1.0 / limit
    half = mine_ref.shape[0]
    act_ref[:half, :] = (limit * jnp.tanh(mine_ref[...].astype(f32) * inv)).astype(bf16)
    act_ref[half:, :] = (limit * jnp.tanh(recv_ref[...].astype(f32) * inv)).astype(bf16)


def enter(spot, limits, hidden_in, recv):
    half, width = recv.shape
    (act,) = launch(
        functools.partial(enter_kernel, 0), "enter", spot, (),
        [(limits, smem()), (hidden_in, my_row(half, width)), (recv, whole(half, width))],
        [(whole(2 * half, width), shape((2 * half, width), bf16))],
        us=3.0,
    )
    return act


def my_row(half, width):
    return pl.BlockSpec((None, half, width), lambda t, s: (s[SIDE], 0, 0))


def place_kernel(spot_ref, mine_ref, recv_ref, out_ref):
    out_ref[spot_ref[SIDE]] = mine_ref[...].astype(out_ref.dtype)
    out_ref[1 - spot_ref[SIDE]] = recv_ref[...].astype(out_ref.dtype)


def place_rows(spot, hold, mine, recv, dtype):
    half, width = mine.shape
    (out,) = launch(
        place_kernel, "place_rows", spot, hold,
        [(mine, whole(half, width)), (recv, whole(half, width))],
        [(whole(2, half, width), shape((2, half, width), dtype))],
        us=2.5
    )
    return out


def copy_kernel(spot_ref, *refs):
    count = len(refs) // 2
    for source, target in zip(refs[:count], refs[count:]):
        target[...] = source[...]


def pick_weights(spot, hold, layer, w_qkv, w_out):
    _, _, width, cols = w_qkv.shape
    rows = width // 2
    wide = w_out.shape[2] // 2
    return launch(
        copy_kernel, "pick_weights", spot, hold,
        [
            (w_qkv, pl.BlockSpec((None, 3, rows, cols), lambda t, s: (layer, 0, s[CORE], 0))),
            (w_out, pl.BlockSpec((None, cols, wide), lambda t, s: (layer, 0, s[CORE]))),
        ],
        [
            (whole(3, rows, cols), shape((3, rows, cols), bf16)),
            (whole(cols, wide), shape((cols, wide), bf16)),
        ],
        us=3.0,
    )


def relay(spot, array):
    (out,) = launch(
        copy_kernel, "relay", spot, (),
        [(a, source) for a, source, _, _ in relay_piece(array)],
        [(target, out) for _, _, target, out in relay_piece(array)],
        grid=(3,),
        us=2.5,
    )
    return out


def attn_fwd_kernel(pieces, relays, spot_ref, a_ref, *refs):
    w_refs = refs[:pieces]
    b_ref, sq_ref, sk_ref = refs[pieces : pieces + 3]
    sources = refs[pieces + 3 : pieces + 3 + relays]
    q_ref, k_ref, v_ref, c_ref, lse_ref = refs[pieces + 3 + relays : pieces + 8 + relays]
    for source, target in zip(sources, refs[pieces + 8 + relays :]):
        target[...] = source[...]
    seq, width = a_ref.shape
    share = width // pieces
    both = value = None
    for piece, w_ref in enumerate(w_refs):
        if pieces == 1:
            act = a_ref[...]
        else:
            which = jnp.where(spot_ref[CORE] == 0, piece, 1 - piece)
            act = a_ref[:, pl.ds(pl.multiple_of(which * share, 128), share)]
        term = dot(act, jnp.concatenate([w_ref[0], w_ref[1]], axis=1))
        both = term if both is None else both + term
        term = dot(act, w_ref[2])
        value = term if value is None else value + term
    query = (both[:, :PAIR] + b_ref[0:1, :]).astype(bf16)
    key = both[:, PAIR:].astype(bf16)
    value = value + b_ref[1:2, :]
    value_t = value.T.astype(bf16)
    q_ref[...] = query
    k_ref[...] = key
    v_ref[...] = value.astype(bf16)
    key_ext = jnp.concatenate([key, sk_ref[...]], axis=1)
    parts = []
    ones = jnp.ones((16, seq), bf16)
    for head in range(2):
        query_ext = jnp.concatenate([query * head_mask(head, HEAD**-0.5), sq_ref[...]], axis=1)
        scores = dot(key_ext, query_ext, NT)
        top = jnp.max(scores, axis=0, keepdims=True)
        weights = jnp.exp(scores - top).astype(bf16)
        summed = dot(
            jnp.concatenate([value_t[head * HEAD : (head + 1) * HEAD], ones], axis=0), weights
        )
        total = summed[HEAD : HEAD + 1]
        parts.append(summed[:HEAD] * (1.0 / total))
        lse_ref[0, head : head + 1, :] = top + jnp.log(total)
    c_ref[...] = jnp.concatenate(parts, axis=0).T


def weight_specs(layer, weights):
    if len(weights) == 1:
        width = weights[0].shape[2]
        return [pl.BlockSpec((None, 3, width, PAIR), lambda t, s: (layer, 0, 0, t))]
    share = weights[0].shape[1]
    return [pl.BlockSpec((3, share, PAIR), lambda t, s: (0, 0, t))] * 2


def relay_weights(layer, w_qkv, w_out):
    _, _, width, cols = w_qkv.shape
    rows, wide, deep = width // 2, w_out.shape[2] // 2, cols // 3
    return [
        (
            w_qkv,
            pl.BlockSpec((None, 1, rows, cols), lambda t, s: (layer, t, s[CORE], 0)),
            pl.BlockSpec((1, rows, cols), lambda t, s: (t, 0, 0)),
            shape((3, rows, cols), bf16),
        ),
        (
            w_out,
            pl.BlockSpec((None, deep, wide), lambda t, s: (layer, t, s[CORE])),
            pl.BlockSpec((deep, wide), lambda t, s: (t, 0)),
            shape((cols, wide), bf16),
        ),
    ]


def relay_piece(array):
    lead, *rest = array.shape
    spec = pl.BlockSpec((lead // 3, *rest), lambda t, s: (t,) + (0,) * len(rest))
    return [(array, spec, spec, shape(array.shape, array.dtype))]


def relay_row(rows):
    _, half, width = rows.shape
    wide = width // 3
    return [
        (
            rows,
            pl.BlockSpec((None, half, wide), lambda t, s: (1 - s[SIDE], 0, t)),
            pl.BlockSpec((half, wide), lambda t, s: (0, t)),
            shape((half, width), rows.dtype),
        )
    ]


def attn_fwd(spot, hold, layer, act, weights, bias, seg_q, seg_k, relays=()):
    seq, width = act.shape
    cols = bias.shape[2]
    steps = cols // PAIR
    block = pl.BlockSpec((seq, PAIR), lambda t, s: (0, t))
    return launch(
        functools.partial(attn_fwd_kernel, len(weights), len(relays)), "attn_fwd", spot, hold,
        [(act, whole(seq, width))]
        + list(zip(weights, weight_specs(layer, weights)))
        + [
            (bias, pl.BlockSpec((None, 2, PAIR), lambda t, s: (layer, 0, t))),
            (seg_q, whole(seq, PAIR)),
            (seg_k, whole(seq, PAIR)),
        ]
        + [(array, source) for array, source, _, _ in relays],
        [
            (block, shape((seq, cols), bf16)),
            (block, shape((seq, cols), bf16)),
            (block, shape((seq, cols), bf16)),
            (block, shape((seq, cols), f32)),
            (pl.BlockSpec((1, 8, seq), lambda t, s: (t, 0, 0)), shape((steps, 8, seq), f32)),
        ]
        + [(target, out) for _, _, target, out in relays],
        grid=(steps,),
        us=8.0
    )


def norm_rows(entries):
    centred = entries - jnp.mean(entries, axis=-1, keepdims=True)
    spread = jnp.mean(centred * centred, axis=-1, keepdims=True)
    rate = lax.rsqrt(spread + EPS)
    return centred * rate, rate


def ff_fwd_kernel(
    layer, last, spot_ref, lim_ref, xt_ref, xb_ref, co_ref, ct_ref, wo_ref, wy_ref, wc_ref,
    vec_ref, gain_ref, up_ref, bup_ref, down_ref, *rest
):
    if last:
        gt_ref, gb_ref, *rest = rest
    cu_ref, hat1_ref, rate1_ref, g_ref, slope_ref, *rest = rest
    acc_ref = rest[-1]
    step = pl.program_id(0)
    half_seq, width = xt_ref.shape
    half = co_ref.shape[1]
    wide = width // 2
    rows = 64
    ctx_limit, ff_limit, act_limit = lim_ref[layer, 1], lim_ref[layer, 2], lim_ref[layer, 3]

    @pl.when(step == 0)
    def _():
        inv = 1.0 / ctx_limit
        cu_ref[:, :half] = (ctx_limit * jnp.tanh(co_ref[...] * inv)).astype(bf16)
        cu_ref[:, half:width] = (ctx_limit * jnp.tanh(ct_ref[...] * inv)).astype(bf16)
        acc_ref[...] = dot(cu_ref[:, :half], wo_ref[...])
        for piece, w_ref in enumerate((wy_ref, wc_ref)):
            which = jnp.where(spot_ref[CORE] == 0, piece, 1 - piece)
            at = pl.ds(pl.multiple_of(which * wide, 128), wide)
            acc_ref[:, at] += dot(cu_ref[:, half:width], w_ref[...])

        for base, x_ref in ((0, xt_ref), (half_seq, xb_ref)):

            def body(i, carry, base=base, x_ref=x_ref):
                start = pl.multiple_of(i * rows, rows)
                at = pl.ds(base + start, rows)
                hat, rate = norm_rows(
                    x_ref[pl.ds(start, rows), :].astype(f32) + (acc_ref[at, :] + vec_ref[0:1, :])
                )
                hat1_ref[at, :] = hat
                rate1_ref[at, :] = jnp.broadcast_to(rate, (rows, 128))
                normed = hat * gain_ref[0:1, :] + vec_ref[1:2, :]
                bent = ff_limit * jnp.tanh(normed * (1.0 / ff_limit))
                cu_ref[at, width:] = bent.astype(bf16)
                acc_ref[at, :] = normed + vec_ref[2:3, :]
                return carry

            lax.fori_loop(0, half_seq // rows, body, 0)

    inv_act = 1.0 / act_limit
    chunk = up_ref.shape[1]
    sub = FF_SUB
    for part in range(chunk // sub):
        cols = slice(part * sub, (part + 1) * sub)
        pre = dot(cu_ref[:, width:], up_ref[:, cols]) + bup_ref[layer : layer + 1, cols]
        cdf = 0.5 * lax.erf(pre * INV_SQRT2) + 0.5
        pdf = jnp.exp(pre * pre * -0.5) * INV_SQRT2PI
        bent = jnp.tanh(pre * cdf * inv_act)
        g_ref[:, cols] = (act_limit * bent).astype(bf16)
        slope_ref[:, cols] = ((1.0 - bent * bent) * (cdf + pre * pdf)).astype(bf16)
    acc_ref[...] += dot(g_ref[...], down_ref[...])

    @pl.when(step == pl.num_programs(0) - 1)
    def _():
        if last:
            top_ref, bottom_ref, de_ref, df_ref, sums_ref = rest[:-1]
            sums = norm_sums(width)
            for base, out_ref, in_ref in ((0, top_ref, gt_ref), (half_seq, bottom_ref, gb_ref)):

                def body(i, carry, base=base, out_ref=out_ref, in_ref=in_ref):
                    here = pl.ds(pl.multiple_of(i * rows, rows), rows)
                    at = pl.ds(base + pl.multiple_of(i * rows, rows), rows)
                    hat, rate = norm_rows(acc_ref[at, :])
                    new = hat * gain_ref[1:2, :] + vec_ref[3:4, :]
                    out_ref[here, :] = new.astype(bf16)
                    grad = in_ref[here, :].astype(f32)
                    return leave_norm(grad, hat, rate, gain_ref, at, de_ref, df_ref, carry)

                sums = lax.fori_loop(0, half_seq // rows, body, sums)
            store_sums(sums, sums_ref)
        else:
            hat2_ref, rate2_ref, new_ref, act_ref = rest[:-1]
            limit = lim_ref[layer + 1, 0]

            def body(i, carry):
                at = pl.ds(pl.multiple_of(i * rows, rows), rows)
                hat, rate = norm_rows(acc_ref[at, :])
                hat2_ref[at, :] = hat
                rate2_ref[at, :] = jnp.broadcast_to(rate, (rows, 128))
                new = hat * gain_ref[1:2, :] + vec_ref[3:4, :]
                new_ref[at, :] = new
                act_ref[at, :] = (limit * jnp.tanh(new * (1.0 / limit))).astype(bf16)
                return carry

            lax.fori_loop(0, 2 * half_seq // rows, body, 0)


def norm_back(grad, hat, rate, gain):
    scaled = grad * gain
    mean = jnp.mean(scaled, axis=-1, keepdims=True)
    lean = jnp.mean(scaled * hat, axis=-1, keepdims=True)
    return rate * (scaled - mean - hat * lean)


def norm_sums(width):
    return (jnp.zeros((1, width), f32),) * 3


def leave_norm(grad, hat, rate, gain_ref, at, de_ref, df_ref, sums):
    de = norm_back(grad, hat, rate, gain_ref[1:2, :])
    df = de.astype(bf16)
    de_ref[at, :] = de
    df_ref[at, :] = df
    return (
        sums[0] + jnp.sum(df.astype(f32), axis=0, keepdims=True),
        sums[1] + jnp.sum(grad, axis=0, keepdims=True),
        sums[2] + jnp.sum(grad * hat, axis=0, keepdims=True),
    )


def store_sums(sums, sums_ref):
    sums_ref[...] = jnp.zeros_like(sums_ref)
    sums_ref[2:3, :] = sums[0]
    sums_ref[3:4, :] = sums[1]
    sums_ref[5:6, :] = sums[2]


def norm_outs(seq, width):
    return [
        (whole(seq, width), shape((seq, width), f32)),
        (whole(seq, width), shape((seq, width), bf16)),
        (whole(8, width), shape((8, width), f32)),
    ]


def halves(pair, half, width):
    if len(pair) == 1:
        return [
            (pair[0], pl.BlockSpec((half, width), lambda *_: (0, 0))),
            (pair[0], pl.BlockSpec((half, width), lambda *_: (1, 0))),
        ]
    first = my_row(half, width) if pair[0].ndim == 3 else whole(half, width)
    return [(pair[0], first), (pair[1], whole(half, width))]


def ff_fwd(
    spot, hold, layer, last, limits, x, ctx_own, ctx_oth, w_out, wo_oth, vec, gain, w_up, b_up,
    w_down, cot=None
):
    seq, half = ctx_own.shape
    width, hidden = w_up.shape[1:]
    chunk = FF_CHUNK
    steps = hidden // chunk
    tile = pl.BlockSpec((seq, chunk), lambda t, s: (0, t))
    full = whole(seq, width)
    outs = [
        (whole(seq, 2 * width), shape((seq, 2 * width), bf16)),
        (full, shape((seq, width), f32)),
        (whole(seq, 128), shape((seq, 128), f32)),
        (tile, shape((seq, hidden), bf16)),
        (tile, shape((seq, hidden), bf16)),
    ]
    if last:
        outs += [(whole(seq // 2, width), shape((seq // 2, width), bf16))] * 2
        outs += norm_outs(seq, width)
    else:
        outs += [
            (full, shape((seq, width), f32)),
            (whole(seq, 128), shape((seq, 128), f32)),
            (full, shape((seq, width), f32)),
            (full, shape((seq, width), bf16)),
        ]
    return launch(
        functools.partial(ff_fwd_kernel, layer, last), "ff_fwd", spot, hold,
        [(limits, smem())]
        + halves(x, seq // 2, width)
        + [
            (ctx_own, whole(seq, half)),
            (ctx_oth, whole(seq, half)),
            (w_out, at_layer(layer, half, width)),
            (wo_oth[0], whole(half, width // 2)),
            (wo_oth[1], whole(half, width // 2)),
            (vec, at_layer(layer, *vec.shape[1:])),
            (gain, at_layer(layer, *gain.shape[1:])),
            (w_up, pl.BlockSpec((None, width, chunk), lambda t, s: (layer, 0, t))),
            (b_up, pl.BlockSpec((b_up.shape[0], chunk), lambda t, s: (0, t))),
            (w_down, pl.BlockSpec((None, chunk, width), lambda t, s: (layer, t, 0))),
        ]
        + (halves(cot, seq // 2, width) if last else []),
        outs,
        scratch=[pltpu.VMEM((seq, width), f32)],
        grid=(steps,),
        us=21.0
    )


def ff_bwd_kernel(
    layer, spot_ref, lim_ref, de_ref, fin_ref, hat1_ref, rate1_ref, vec_ref, gain_ref, slope_ref,
    up_ref, down_ref, wo_ref, wy_ref, wc_ref, co_ref, ct_ref,
    zk_ref, ok_ref, os_ref, dy_ref, dco_ref, dct_ref, small_ref, bup_ref,
    do_ref, du_ref, dz_ref,
):
    step = pl.program_id(0)
    steps = pl.num_programs(0)
    seq, width = de_ref.shape
    half = width // 2
    rows = 64
    core = spot_ref[CORE]
    mine = pl.ds(pl.multiple_of(core * half, 128), half)
    other = pl.ds(pl.multiple_of((1 - core) * half, 128), half)
    zero = jnp.zeros((1, width), f32)
    ctx_limit, ff_limit = lim_ref[layer, 1], lim_ref[layer, 2]

    chunk = up_ref.shape[1]
    sub = FF_SUB
    for part in range(chunk // sub):
        cols = slice(part * sub, (part + 1) * sub)
        dz = dot(fin_ref[...], down_ref[cols, :], NT) * slope_ref[:, cols].astype(f32)
        low = dz.astype(bf16)
        bup_ref[:, cols] = jnp.sum(low.astype(f32), axis=0, keepdims=True)
        dz_ref[:, cols] = low
    term = dot(dz_ref[...], up_ref[...], NT)

    @pl.when(step == 0)
    def _():
        du_ref[...] = term

    @pl.when(step > 0)
    def _():
        du_ref[...] += term

    @pl.when(step < steps // 2)
    def _():
        zk_ref[:, pl.ds(pl.multiple_of(step * chunk, 128), chunk)] = dz_ref[...]

    @pl.when(step == steps - 1)
    def _():
        def body(i, carry):
            gain_sum, shift_sum, out_sum = carry
            at = pl.ds(pl.multiple_of(i * rows, rows), rows)
            hat = hat1_ref[at, :]
            normed = hat * gain_ref[0:1, :] + vec_ref[1:2, :]
            bent = jnp.tanh(normed * (1.0 / ff_limit))
            grad = de_ref[at, :] + du_ref[at, :] * (1.0 - bent * bent)
            dy = norm_back(grad, hat, rate1_ref[at, 0:1], gain_ref[0:1, :])
            low = dy.astype(bf16)
            dy_ref[at, :] = dy
            do_ref[at, :] = low
            return (
                gain_sum + jnp.sum(grad * hat, axis=0, keepdims=True),
                shift_sum + jnp.sum(grad, axis=0, keepdims=True),
                out_sum + jnp.sum(low.astype(f32), axis=0, keepdims=True),
            )

        sums = lax.fori_loop(0, seq // rows, body, (zero, zero, zero))
        small_ref[...] = jnp.zeros_like(small_ref)
        small_ref[0:1, :] = sums[2]
        small_ref[1:2, :] = sums[1]
        small_ref[4:5, :] = sums[0]
        ok_ref[...] = do_ref[:, mine]
        os_ref[...] = do_ref[:, other]
        inv = 1.0 / ctx_limit
        bent = jnp.tanh(co_ref[...] * inv)
        dco_ref[...] = (dot(do_ref[...], wo_ref[...], NT) * (1.0 - bent * bent)).astype(bf16)
        bent = jnp.tanh(ct_ref[...] * inv)
        grad = dot(do_ref[:, mine], wy_ref[...], NT) + dot(do_ref[:, other], wc_ref[...], NT)
        dct_ref[...] = (grad * (1.0 - bent * bent)).astype(bf16)


def ff_bwd(
    spot, hold, layer, limits, de, df, hat1, rate1, vec, gain, slope, w_up, w_down, w_out,
    wo_oth, ctx_own, ctx_oth,
):
    seq, half = ctx_own.shape
    width, hidden = w_up.shape[1:]
    chunk = FF_CHUNK
    steps = hidden // chunk
    span = steps // 2

    def place(t, s):
        return jnp.where(t < span, s[CORE] * span + t, (1 - s[CORE]) * span + t - span)

    full = whole(seq, width)
    part = whole(seq, width // 2)
    outs = [
        (whole(seq, hidden // 2), shape((seq, hidden // 2), bf16)),
        (part, shape((seq, width // 2), bf16)),
        (part, shape((seq, width // 2), bf16)),
        (full, shape((seq, width), f32)),
        (whole(seq, half), shape((seq, half), bf16)),
        (whole(seq, half), shape((seq, half), bf16)),
        (whole(8, width), shape((8, width), f32)),
        (pl.BlockSpec((1, chunk), lambda t, s: (0, place(t, s))), shape((1, hidden), f32)),
    ]
    return launch(
        functools.partial(ff_bwd_kernel, layer), "ff_bwd", spot, hold,
        [(limits, smem())]
        + [
            (de, full),
            (df, full),
            (hat1, full),
            (rate1, whole(seq, 128)),
            (vec, at_layer(layer, *vec.shape[1:])),
            (gain, at_layer(layer, *gain.shape[1:])),
            (slope, pl.BlockSpec((seq, chunk), lambda t, s: (0, place(t, s)))),
            (w_up, pl.BlockSpec((None, width, chunk), lambda t, s: (layer, 0, place(t, s)))),
            (w_down, pl.BlockSpec((None, chunk, width), lambda t, s: (layer, place(t, s), 0))),
            (w_out, at_layer(layer, half, width)),
            (wo_oth[0], whole(half, width // 2)),
            (wo_oth[1], whole(half, width // 2)),
            (ctx_own, whole(seq, half)),
            (ctx_oth, whole(seq, half)),
        ],
        outs,
        scratch=[
            pltpu.VMEM((seq, width), bf16),
            pltpu.VMEM((seq, width), f32),
            pltpu.VMEM((seq, chunk), bf16),
        ],
        grid=(steps,),
        us=20.0
    )


def attn_bwd_half(q_ref, k_ref, v_ref, c_ref, lse_ref, dc_ref, seg_q, seg_k):
    query, key, value, grad = q_ref[...], k_ref[...], v_ref[...], dc_ref[...]
    key_ext = jnp.concatenate([key, seg_k], axis=1)
    key_t = key.astype(f32).T.astype(bf16)
    product_t = (grad.astype(f32) * c_ref[...]).T
    d_key = d_value = None
    d_query_t = []
    for head in range(2):
        scaled = query * head_mask(head, HEAD**-0.5)
        scores = dot(key_ext, jnp.concatenate([scaled, seg_q], axis=1), NT)
        probs = jnp.exp(scores - lse_ref[0, head : head + 1, :])
        grad_head = grad * head_mask(head, 1.0)
        d_probs = dot(value, grad_head, NT)
        delta = jnp.sum(product_t[head * HEAD : (head + 1) * HEAD], axis=0, keepdims=True)
        d_scores = (probs * (d_probs - delta)).astype(bf16)
        term_v = dot(probs.astype(bf16), grad_head)
        term_k = dot(d_scores, scaled)
        d_value = term_v if d_value is None else d_value + term_v
        d_key = term_k if d_key is None else d_key + term_k
        d_query_t.append(dot(key_t[head * HEAD : (head + 1) * HEAD], d_scores))
    d_query = jnp.concatenate(d_query_t, axis=0).T * HEAD**-0.5
    return d_query.astype(bf16), d_key.astype(bf16), d_value.astype(bf16)


def attn_bwd_kernel(
    layer, spot_ref, lim_ref, xt_ref, xb_ref, dy_ref, sq_ref, sk_ref,
    qo_ref, ko_ref, vo_ref, co_ref, lo_ref, dco_ref,
    qt_ref, kt_ref, vt_ref, ct_ref, lt_ref, dct_ref, wo_ref, wy_ref, wc_ref, *rest
):
    if layer:
        hat_ref, rate_ref, gain_ref, *rest = rest
    dqo_ref, dko_ref, dvo_ref, dqt_ref, dkt_ref, dvt_ref, bo_ref, bt_ref, *rest = rest
    acc_ref = rest[-1]
    step = pl.program_id(0)
    half_seq, width = xt_ref.shape
    share = width // 2
    rows = 64
    own = attn_bwd_half(qo_ref, ko_ref, vo_ref, co_ref, lo_ref, dco_ref, sq_ref[...], sk_ref[...])
    oth = attn_bwd_half(qt_ref, kt_ref, vt_ref, ct_ref, lt_ref, dct_ref, sq_ref[...], sk_ref[...])
    dqo_ref[...], dko_ref[...], dvo_ref[...] = own
    dqt_ref[...], dkt_ref[...], dvt_ref[...] = oth
    for out_ref, grads in ((bo_ref, own), (bt_ref, oth)):
        out_ref[0:1, :] = jnp.sum(grads[0].astype(f32), axis=0, keepdims=True)
        out_ref[1:2, :] = jnp.sum(grads[2].astype(f32), axis=0, keepdims=True)
        out_ref[2:8, :] = jnp.zeros((6, PAIR), f32)
    joined = [jnp.concatenate([own[k], oth[k]], axis=1) for k in range(3)]
    for piece, w_ref in enumerate((wy_ref, wc_ref)):
        which = jnp.where(spot_ref[CORE] == 0, piece, 1 - piece)
        at = pl.ds(pl.multiple_of(which * share, 128), share)
        total = None
        for k in range(3):
            term = dot(joined[k], jnp.concatenate([wo_ref[k, at, :], w_ref[k]], axis=1), NT)
            total = term if total is None else total + term

        @pl.when(step == 0)
        def _():
            acc_ref[:, at] = total

        @pl.when(step > 0)
        def _():
            acc_ref[:, at] += total

    @pl.when(step == pl.num_programs(0) - 1)
    def _():
        inv = 1.0 / lim_ref[layer, 0]
        sums = norm_sums(width)
        for part, x_ref in enumerate((xt_ref, xb_ref)):

            def body(i, carry, part=part, x_ref=x_ref):
                here = pl.ds(pl.multiple_of(i * rows, rows), rows)
                at = pl.ds(part * half_seq + pl.multiple_of(i * rows, rows), rows)
                bent = jnp.tanh(x_ref[here, :].astype(f32) * inv)
                grad = dy_ref[at, :] + acc_ref[at, :] * (1.0 - bent * bent)
                if layer:
                    return leave_norm(
                        grad, hat_ref[at, :], rate_ref[at, 0:1], gain_ref, at, rest[0], rest[1],
                        carry,
                    )
                rest[part][here, :] = grad.astype(rest[part].dtype)
                return carry

            sums = lax.fori_loop(0, half_seq // rows, body, sums)
        if layer:
            store_sums(sums, rest[2])


def attn_bwd(spot, hold, layer, limits, x, dy, seg_q, seg_k, own, oth, w_qkv, wq_oth, below=()):
    seq, width = dy.shape
    cols = own[0].shape[1]
    steps = cols // PAIR
    block = pl.BlockSpec((seq, PAIR), lambda t, s: (0, t))
    half_specs = [
        block,
        block,
        block,
        block,
        pl.BlockSpec((1, 8, seq), lambda t, s: (t, 0, 0)),
        block,
    ]
    return launch(
        functools.partial(attn_bwd_kernel, layer), "attn_bwd", spot, hold,
        [(limits, smem())]
        + halves(x, seq // 2, width)
        + [(dy, whole(seq, width)), (seg_q, whole(seq, PAIR)), (seg_k, whole(seq, PAIR))]
        + list(zip(own, half_specs))
        + list(zip(oth, half_specs))
        + list(zip((w_qkv,), weight_specs(layer, (w_qkv,))))
        + list(zip(wq_oth, weight_specs(layer, wq_oth)))
        + (
            [
                (below[0], whole(seq, width)),
                (below[1], whole(seq, 128)),
                (below[2], at_layer(layer - 1, *below[2].shape[1:])),
            ]
            if layer
            else []
        ),
        [(block, shape((seq, cols), bf16))] * 6
        + [(pl.BlockSpec((8, PAIR), lambda t, s: (0, t)), shape((8, cols), f32))] * 2
        + (
            norm_outs(seq, width)
            if layer
            else [
                (whole(seq // 2, width), shape((seq // 2, width), f32)),
                (whole(seq // 2, width), shape((seq // 2, width), bf16)),
            ]
        ),
        scratch=[pltpu.VMEM((seq, width), f32)],
        grid=(steps,),
        us=18.5
    )


FF_ORDERS = (
    (AXIS_X, SIDE, AXIS_Z0, AXIS_Z1),
    (SIDE, AXIS_Z0, AXIS_X, AXIS_Z1),
    (AXIS_Z0, AXIS_X, SIDE, AXIS_Z1),
)
FF_ROWS = (144, 128, 112)
ATT_ORDERS = (
    (AXIS_X, SIDE, AXIS_Z0, AXIS_Z1),
    (SIDE, AXIS_X, AXIS_Z0, AXIS_Z1),
)
ATT_ROWS = (96, 96)
PIECE = 48


def block_of(spot_ref, order, rel):
    bit = {axis: (rel >> (3 - k)) & 1 for k, axis in enumerate(order)}
    chip = 0
    for axis in (AXIS_Z1, AXIS_Z0, AXIS_X):
        own = spot_ref[axis]
        chip = chip * 2 + (1 - own if bit[axis] else own)
    return bit[SIDE], chip


def w_ff_kernel(
    spot_ref, um_ref, uo_ref, zm_ref, so_ref, gm_ref, go_ref, fm_ref, fo_ref, down_ref, *rest
):
    outs, ut_ref, half_ref, all_ref = rest[:-3], rest[-3], rest[-2], rest[-1]
    step = pl.program_id(0)
    sides, chips, tall, lanes = all_ref.shape
    seq, width = um_ref.shape
    thin = width // chips

    @pl.when(step == 0)
    def _():
        ut_ref[:, :seq] = um_ref[...].T
        ut_ref[:, seq:] = uo_ref[...].T
        mine = pl.ds(pl.multiple_of(spot_ref[CORE] * lanes, 128), lanes)
        half_ref[0] = fm_ref[:, mine]
        half_ref[1] = fo_ref[:, mine]

    theirs = (dot(fo_ref[...], down_ref[...], NT) * so_ref[...].astype(f32)).astype(bf16)
    grad_up = dot(ut_ref[:, :seq], zm_ref[...]) + dot(ut_ref[:, seq:], theirs)
    grad_up = grad_up.astype(bf16)
    for chip in range(chips):
        at = pl.ds(pl.multiple_of((step % 2) * thin, 16), thin)
        all_ref[step // 2, chip, at, :] = grad_up[chip * thin : (chip + 1) * thin]
    base = 2 * thin
    deep = tall - base
    per = gm_ref.shape[1] // (2 * deep)
    for part in range(per):
        cols = slice(part * 2 * deep, (part + 1) * 2 * deep)
        grad_down = dot(gm_ref[:, cols], half_ref[0], TN) + dot(go_ref[:, cols], half_ref[1], TN)
        grad_down = grad_down.astype(bf16)
        for side in range(2):
            all_ref[side, step * per + part, base:, :] = grad_down[side * deep : (side + 1) * deep]

    @pl.when(step == pl.num_programs(0) - 1)
    def _():
        start = 0
        for part, (order, count) in enumerate(zip(FF_ORDERS, FF_ROWS)):
            for rel in range(16):
                side, chip = block_of(spot_ref, order, rel)
                side = 1 - spot_ref[SIDE] if side else spot_ref[SIDE]
                value = all_ref[side, chip, start : start + count, :]
                if rel < 8:
                    outs[2 * part][rel] = value
                else:
                    outs[2 * part + 1][(rel - 8) * count : (rel - 7) * count, :] = value
            start += count


def w_ff(
    spot, hold, layer, cu_mine, cu_core, dz_mine, slope_core, g_mine, g_core, df_mine, df_core,
    w_down
):
    seq, width = df_mine.shape
    lanes, hidden = width // 2, g_mine.shape[1]
    steps = dz_mine.shape[1] // lanes
    tall = hidden // 8
    g_block = pl.BlockSpec((seq, hidden // steps), lambda t, s: (0, t))
    u_block = pl.BlockSpec((seq, width), lambda *_: (0, 1))
    outs = []
    for rows in FF_ROWS:
        outs.append((whole(8, rows, lanes), shape((8, rows, lanes), bf16)))
        outs.append((whole(8 * rows, lanes), shape((8 * rows, lanes), bf16)))
    return launch(
        w_ff_kernel, "w_ff", spot, hold,
        [
            (cu_mine, u_block),
            (cu_core, u_block),
            (dz_mine, pl.BlockSpec((seq, lanes), lambda t, s: (0, t))),
            (slope_core, pl.BlockSpec((seq, lanes), lambda t, s: (0, s[CORE] * steps + t))),
            (g_mine, g_block),
            (g_core, g_block),
            (df_mine, whole(seq, width)),
            (df_core, whole(seq, width)),
            (
                w_down,
                pl.BlockSpec(
                    (None, lanes, width), lambda t, s: (layer, s[CORE] * steps + t, 0)
                ),
            ),
        ],
        outs,
        scratch=[
            pltpu.VMEM((width, 2 * seq), bf16),
            pltpu.VMEM((2, seq, lanes), bf16),
            pltpu.VMEM((2, 8, tall, lanes), bf16),
        ],
        grid=(steps,),
        us=13.5,
    )


def w_att_kernel(
    spot_ref, a_ref, dqo_ref, dko_ref, dvo_ref, dqt_ref, dkt_ref, dvt_ref,
    cm_ref, cc_ref, dom_ref, doc_ref, keep_ref, out_ref, *rest
):
    send_refs, at_ref, spare_ref = rest[:-2], rest[-2], rest[-1]
    width = a_ref.shape[1]
    _, chips, tall, cols = keep_ref.shape
    core = spot_ref[CORE]
    piece = PIECE
    per = tall // piece
    at_ref[...] = a_ref[...].T
    sides = ((dqo_ref, dko_ref, dvo_ref), (dqt_ref, dkt_ref, dvt_ref))
    for side, grads in enumerate(sides):
        for which in range(3):
            result = dot(at_ref[...], grads[which][...]).astype(bf16)
            for j in range(width // piece):
                index = which * (width // piece) + j
                block, sub = index // per, index % per
                spare_ref[block % 2, block // 2, sub * piece : (sub + 1) * piece, :] = result[
                    j * piece : (j + 1) * piece
                ]
        keep_ref[side] = spare_ref[core]
        for k, send_ref in enumerate(send_refs):
            send_ref[side] = spare_ref[1 - core, :, k * piece : (k + 1) * piece, :]
    half = width // 2
    heads = half // HEAD
    for side in range(2):
        at = slice(side * half, (side + 1) * half)
        result = dot(cm_ref[:, at], dom_ref[...], TN) + dot(cc_ref[:, at], doc_ref[...], TN)
        for chip in range(chips):
            for pair in range(heads // 2):
                first = (2 * pair) * HEAD + 8 * chip
                second = first + HEAD
                out_ref[side, chip, pair * 16 : (pair + 1) * 16, :] = jnp.concatenate(
                    [result[first : first + 8], result[second : second + 8]], axis=0
                ).astype(bf16)


def w_att(spot, hold, act, d_own, d_oth, cu_mine, cu_core, do_mine, do_core):
    seq, width = act.shape
    cols = width // 2
    chips = 8
    tall = 3 * width // (2 * chips)
    outs = [
        shape((2, chips, tall, cols), bf16),
        shape((2, chips, cols // chips, cols), bf16),
        *[shape((2, chips, PIECE, cols), bf16)] * (tall // PIECE),
    ]
    cq_block = pl.BlockSpec((seq, width), lambda *_: (0, 0))
    return launch(
        w_att_kernel, "w_att", spot, hold,
        [(array, whole(*array.shape)) for array in (act, *d_own, *d_oth)]
        + [
            (cu_mine, cq_block),
            (cu_core, cq_block),
            (do_mine, whole(seq, cols)),
            (do_core, whole(seq, cols)),
        ],
        [(whole(*out.shape), out) for out in outs],
        scratch=[pltpu.VMEM((width, seq), bf16), pltpu.VMEM((2, chips, tall, cols), bf16)],
        us=8.0,
    )


class Part:
    def __init__(self, kind, order, kept):
        self.kind, self.order, self.kept = kind, order, kept
        self.stage = 0
        self.array = self.start = None
        self.final = None

    def arrives(self, array, start):
        self.array, self.start = array, start


def pack_small(spot_ref, small_refs, out_ref):
    for layer in range(len(small_refs) // 5):
        bo_ref, bt_ref, vec_ref, sums_ref, up_ref = small_refs[5 * layer : 5 * layer + 5]
        half = bo_ref.shape[1]
        width = 2 * half
        side = spot_ref[SIDE]
        mine = pl.ds(pl.multiple_of(side * half, 128), half)
        other = pl.ds(pl.multiple_of((1 - side) * half, 128), half)
        out_ref[layer, 0:2, mine] = bo_ref[0:2, :]
        out_ref[layer, 0:2, other] = bt_ref[0:2, :]
        out_ref[layer, 2:8, :] = vec_ref[0:6, :] + sums_ref[0:6, :]
        for k in range(up_ref.shape[1] // width):
            out_ref[layer, 8 + k : 9 + k, :] = up_ref[:, k * width : (k + 1) * width]


def exchange(spot, over_axis, parts, att=None, smalls=(), pair=None, carry=None):
    ins, outs, steps = [], [], []

    def take(array):
        for k, (known, _) in enumerate(ins):
            if known is array:
                return k
        ins.append((array, whole(*array.shape)))
        return len(ins) - 1

    def give(dims, dtype=bf16):
        outs.append((whole(*dims), shape(dims, dtype)))
        return len(outs) - 1

    lanes = (parts[0].kept if parts else att[0]).shape[-1]
    sends = {}

    def room(axis, rows):
        start = sends.get(axis, 0)
        sends[axis] = start + rows
        return start

    new_parts, places = [], []
    parts = sorted(parts, key=lambda part: (part.kind != "ff", part.kept.shape[0]))
    for part in parts:
        blocks, rows, _ = part.kept.shape
        source = take(part.kept), take(part.array), part.start
        if blocks > 1:
            axis = part.order[part.stage + 1]
            start = room(axis, blocks // 2 * rows)
            steps.append(("halve", source, give((blocks // 2, rows, lanes)), axis, start))
        elif part.kind == "ff":
            axis = SIDE
            start = room(axis, rows)
            steps.append(("end", source, give((rows, lanes), f32), axis, start))
        else:
            axis = None
            start = 0
            steps.append(("end", source, give((rows, lanes), f32), None, 0))
        places.append((part, axis, start))
    if att is not None:
        source = [take(array) for array in att]
        begin = 0
        for order, rows in zip(ATT_ORDERS, ATT_ROWS):
            start = room(order[0], 8 * rows)
            kept = give((8, rows, lanes))
            steps.append(("enter", source, kept, order[0], start, order, begin, rows))
            places.append((Part("att", order, None), order[0], start))
            begin += rows
    small_out = None
    if smalls:
        source = [take(array) for small in smalls for array in small]
        width = smalls[0][2].shape[1]
        small_out = give((len(smalls), 8 + smalls[0][4].shape[1] // width, width), f32)
        steps.append(("pack", source, small_out))
    if pair is not None:
        small_out = give(pair[0].shape, f32)
        steps.append(("sum", [take(array) for array in pair], small_out))
    if carry is not None:
        small_out = give(carry.shape, carry.dtype)
        steps.append(("copy", [take(carry)], small_out))
    send_at = {axis: give((rows, lanes)) for axis, rows in sends.items()}

    def body(spot_ref, *refs):
        in_refs, out_refs = refs[: len(ins)], refs[len(ins) :]
        for what, source, out, *more in steps:
            out_ref = out_refs[out]
            if what == "halve":
                axis, start = more
                kept, got = in_refs[source[0]], in_refs[source[1]]
                base = source[2]
                half, rows, _ = out_ref.shape
                send = out_refs[send_at[axis]]
                for j in range(half):
                    at = base + j * rows
                    out_ref[j] = kept[j] + got[at : at + rows, :]
                    at += half * rows
                    send[start + j * rows : start + (j + 1) * rows, :] = (
                        kept[half + j] + got[at : at + rows, :]
                    )
            elif what == "end":
                axis, start = more
                kept, got = in_refs[source[0]], in_refs[source[1]]
                base = source[2]
                rows = out_ref.shape[0]
                total = kept[0].astype(f32) + got[base : base + rows, :].astype(f32)
                out_ref[...] = total
                if axis is not None:
                    out_refs[send_at[axis]][start : start + rows, :] = total.astype(bf16)
            elif what == "enter":
                axis, start, order, begin, rows = more
                keep, outer, *got = (in_refs[k] for k in source)
                send = out_refs[send_at[axis]]
                for rel in range(16):
                    side, chip = block_of(spot_ref, order, rel)
                    for k in range(begin // PIECE, (begin + rows) // PIECE):
                        if k < len(got):
                            at = slice(k * PIECE, (k + 1) * PIECE)
                            value = keep[side, chip, at, :] + got[k][side, chip]
                        else:
                            value = outer[side, chip]
                        done = k * PIECE - begin
                        if rel < 8:
                            out_ref[rel, done : done + PIECE, :] = value
                        else:
                            at = start + (rel - 8) * rows + done
                            send[at : at + PIECE, :] = value
            elif what == "copy":
                out_ref[...] = in_refs[source[0]][...]
            elif what == "pack":
                pack_small(spot_ref, [in_refs[k] for k in source], out_ref)
            else:
                out_ref[...] = in_refs[source[0]][...] + in_refs[source[1]][...]

    results = launch(body, "exchange", spot, (), ins, outs, us=5.0)
    arrived = {axis: over_axis(results[k], axis) for axis, k in send_at.items()}
    kept_at = [step[2] for step in steps]
    for (part, axis, start), what, out in zip(places, [step[0] for step in steps], kept_at):
        if what == "end":
            part.final = results[out]
        else:
            part.kept = results[out]
        if what != "enter":
            part.stage += 1
        if axis is not None:
            part.arrives(arrived[axis], start)
        new_parts.append(part)
    return new_parts, (None if small_out is None else results[small_out])


def finish_kernel(spot_ref, a_ref, b_ref, c_ref, got_ref, keep_ref, send_ref, both_ref):
    core, side = spot_ref[CORE], spot_ref[SIDE]
    start = 0
    for ref in (a_ref, b_ref, c_ref):
        both_ref[side, start : start + ref.shape[0], :] = ref[...]
        start += ref.shape[0]
    both_ref[1 - side] = got_ref[...].astype(f32)
    half = both_ref.shape[1] // 2
    quarter = half // 4
    for out_ref, which in ((keep_ref, core), (send_ref, 1 - core)):
        for k in range(4):
            at = pl.ds(pl.multiple_of((k % 2) * 2 * quarter + which * quarter, 16), quarter)
            out_ref[k * quarter : (k + 1) * quarter, :] = both_ref[k // 2, at, :].astype(
                out_ref.dtype
            )
        out_ref[half:, :] = both_ref[which, half:, :].astype(out_ref.dtype)


def finish_ff(spot, parts):
    rows = sum(FF_ROWS)
    lanes = parts[0].final.shape[1]
    start = parts[0].start
    got = parts[0].array
    assert start % rows == 0
    return launch(
        finish_kernel, "finish_ff", spot, (),
        [(part.final, whole(*part.final.shape)) for part in parts]
        + [(got, pl.BlockSpec((rows, lanes), lambda *_: (start // rows, 0)))],
        [(whole(rows, lanes), shape((rows, lanes), f32)), (whole(rows, lanes), shape((rows, lanes), bf16))],
        scratch=[pltpu.VMEM((2, rows, lanes), f32)],
        us=3.0,
    )


def local(
    hidden_in, cotangent, segment_ids, clip_ranges, w_qkv, bias_qv, w_out, vector_bias, ln_gain,
    w_up, bias_up, w_down,
):
    layers = w_qkv.shape[0]
    row_count, half_seq, width = hidden_in.shape
    seq = segment_ids.shape[1]
    cols = w_qkv.shape[3]
    heads = cols // HEAD
    hidden = w_up.shape[2]
    dp_count = lax.axis_size("dp")
    assert lax.axis_size("mp") == 2 and row_count == 2 and seq == 2 * half_seq
    bits = dp_count.bit_length() - 1
    assert dp_count == 1 << bits and bits >= 1
    chips = dp_count // 2
    side = lax.axis_index("mp")
    place = lax.axis_index("dp")
    core = place % 2
    spot = Spot(
        jnp.stack(
            [core, side, (place >> 1) & 1, (place >> 2) & 1, (place >> 3) & 1]
        ).astype(jnp.int32)
    )

    def over_mp(value):
        return lax.ppermute(value, "mp", [(0, 1), (1, 0)])

    def over_bit(value, bit):
        return lax.ppermute(value, "dp", [(i, i ^ (1 << bit)) for i in range(dp_count)])

    def over_core(value):
        return over_bit(value, 0)

    def over_axis(value, axis):
        return over_mp(value) if axis == SIDE else over_bit(value, axis - AXIS_X + 1)

    def pick(value, index, axis):
        return lax.dynamic_index_in_dim(value, index, axis, keepdims=False)

    def ordered(index, mine, theirs, axis):
        first = jnp.where(index == 0, mine, theirs)
        second = jnp.where(index == 0, theirs, mine)
        return jnp.concatenate([first, second], axis=axis)

    x = (hidden_in, over_mp(pick(hidden_in, 1 - side, 0)))
    bias_oth = over_mp(bias_qv)
    limits = clip_ranges.astype(f32)
    seg_row = pick(segment_ids, side, 0).reshape(2, half_seq)
    seg_row = jnp.concatenate([pick(seg_row, side, 0), pick(seg_row, 1 - side, 0)])
    same = seg_row[:, None] == jnp.arange(PAIR, dtype=seg_row.dtype)[None, :]
    seg_q = jnp.where(same, BIG, 0.0).astype(bf16)
    seg_k = jnp.where(same, 0.0, 1.0).astype(bf16)

    arrived = [over_mp(piece) for piece in pick_weights(spot, (), 0, w_qkv, w_out)]
    act = enter(spot, limits, hidden_in, x[1])
    fetched, stored = [], []
    shared = ()
    for layer in range(layers):
        last = layer == layers - 1
        relays = []
        if layer:
            relays = relay_piece(arrived[0]) + relay_piece(arrived[1])
        if last:
            relays = relays + relay_row(cotangent)
        outs = attn_fwd(spot, (), layer, act, (w_qkv,), bias_qv, seg_q, seg_k, relays)
        own, copies = outs[:5], outs[5:]
        if last:
            cot = (cotangent, over_mp(copies[-1]))
        copy = copies[0] if layer else relay(spot, arrived[0])
        wq_oth = (arrived[0], over_core(copy))
        relays = [] if layer else relay_piece(arrived[1])
        if not last:
            relays = relays + relay_weights(layer + 1, w_qkv, w_out)
        outs = attn_fwd(spot, (), layer, act, wq_oth, bias_oth, seg_q, seg_k, relays)
        oth = outs[:5]
        wo_oth = (arrived[1], over_core(copies[1] if layer else outs[5]))
        fetched.append((wq_oth, wo_oth))
        if not last:
            arrived = [over_mp(piece) for piece in outs[-2:]]
        outs = ff_fwd(
            spot, shared, layer, last, limits, x, own[3], oth[3], w_out, wo_oth, vector_bias, ln_gain,
            w_up, bias_up, w_down, cot if last else None,
        )
        cu, hat1, rate1, g, slope = outs[:5]
        shared = over_core(cu), over_core(g), over_core(slope)
        norm = None
        if last:
            hidden_mine, hidden_send, *descent = outs[5:]
        else:
            norm = outs[5:7]
        stored.append((x, act, own, oth, cu, hat1, rate1, g, slope, norm, shared))
        if not last:
            x, act = (outs[7],), outs[8]
    hidden_recv = over_mp(hidden_send)

    fast = chips == 8 and width == 768 and hidden == 3072 and cols == 384

    smalls, groups = [], {}
    flying = []
    small = None
    df_core = over_core(descent[1])
    for layer in reversed(range(layers)):
        x, act, own, oth, cu, hat1, rate1, g, slope, norm, shared = stored[layer]
        wq_oth, wo_oth = fetched[layer]
        de, df, sums = descent
        dz_keep, do_keep, do_send, dy, dc_own, dc_oth, vec, d_bup = ff_bwd(
            spot, (), layer, limits, de, df, hat1, rate1, vector_bias, ln_gain, slope, w_up,
            w_down, w_out, wo_oth, own[3], oth[3],
        )
        if fast:
            do_core = over_core(do_send)
            if flying:
                flying, _ = exchange(spot, over_axis, flying, entering)
                groups["att", layer + 1] = flying[-len(ATT_ROWS) :]
            else:
                hidden_out = place_rows(spot, (), hidden_mine, hidden_recv, bf16)
            outs = w_ff(
                spot, (), layer, cu, shared[0], dz_keep, shared[2], g, shared[1], df, df_core,
                w_down,
            )
            parts_ff = []
            for k, order in enumerate(FF_ORDERS):
                parts_ff.append(Part("ff", order, outs[2 * k]))
                parts_ff[k].arrives(over_axis(outs[2 * k + 1], order[0]), 0)
            groups["ff", layer] = parts_ff
            ending = [part for part in flying if part.stage == 2]
            if ending:
                exchange(spot, over_axis, ending)
            flying = flying + parts_ff
        below = (*stored[layer - 1][9], ln_gain) if layer else ()
        outs = attn_bwd(
            spot, (), layer, limits, x, dy, seg_q, seg_k, (*own, dc_own), (*oth, dc_oth), w_qkv,
            wq_oth, below,
        )
        d_own, d_oth = outs[:3], outs[3:6]
        smalls.insert(0, (outs[6], outs[7], vec, sums, d_bup))
        descent = outs[8:]
        if fast:
            keep, out, *send = w_att(
                spot, (), act, d_own, d_oth, cu, shared[0], do_keep, do_core
            )
            entering = keep, out, *(over_core(piece) for piece in send)
            if layer:
                flying, df = exchange(spot, over_axis, flying, carry=descent[1])
                df_core = over_core(df)
            else:
                flying, small = exchange(spot, over_axis, flying, entering, smalls)
                groups["att", 0] = flying[-len(ATT_ROWS) :]
        else:
            dz = (dot(df, w_down[layer], NT) * slope.astype(f32)).astype(bf16)
            do = ordered(core, do_keep, do_send, 1)
            total = []
            for lhs, rhs in ((cu[:, width:], dz), (g, df)):
                grad = dot(lhs, rhs, TN).reshape(-1)
                grad = grad + over_mp(grad)
                total.append(lax.psum_scatter(grad, "dp", scatter_dimension=0, tiled=True))
            groups["ff", layer] = total
            sides = []
            for grads, part in ((d_own, cu[:, :cols]), (d_oth, cu[:, cols:width])):
                qkv = jnp.stack([dot(act, grad, TN) for grad in grads])
                qkv = qkv.reshape(3, width, heads, HEAD).transpose(2, 0, 1, 3)
                sides.append((qkv.reshape(heads, -1), dot(part, do, TN).reshape(heads, -1)))
            total = []
            for k in range(2):
                grad = sides[0][k] + over_mp(sides[1][k])
                total.append(lax.psum_scatter(grad, "dp", scatter_dimension=1, tiled=True))
            groups["att", layer] = total

    row_mine, row_send = descent
    if fast:
        axes = [AXIS_X, SIDE, AXIS_Z0, AXIS_Z1]
        pair = None
        while True:
            flying = [part for part in flying if part.final is None]
            if not flying:
                break
            flying, summed = exchange(spot, over_axis, flying, pair=pair)
            small = small if summed is None else summed
            pair = (small, over_axis(small, axes.pop(0))) if axes else None
        while pair:
            small = pair[0] + pair[1]
            pair = (small, over_axis(small, axes.pop(0))) if axes else None
        grad_input = place_rows(spot, (), row_mine, over_mp(row_send), f32)
        small = small + over_core(small)
        ups, downs, qkvs, outs = [], [], [], []
        for layer in range(layers):
            keep, send = finish_ff(spot, groups["ff", layer])
            both = ordered(core, keep[None], over_core(send).astype(f32)[None], 0)
            up = both[:, : width // 4].reshape(2, 4, -1, cols)
            ups.append(up.transpose(2, 0, 1, 3).reshape(-1))
            downs.append(both[:, width // 4 :].transpose(1, 0, 2).reshape(-1))
            rows = jnp.concatenate([part.final for part in groups["att", layer]], axis=0)
            share = 3 * width // dp_count
            qkv = rows[:share].reshape(share, heads, HEAD)
            qkvs.append(qkv.transpose(1, 0, 2).reshape(heads, -1))
            outs.append(rows[share:].reshape(heads, 2, 4, cols))
        outs = jnp.stack(outs)
        keep, sent = pick(outs, core, 2), pick(outs, 1 - core, 2).astype(bf16)
        outs = ordered(core, keep[:, :, :, None], over_core(sent).astype(f32)[:, :, :, None], 3)
        grads = (
            jnp.stack(qkvs), outs.reshape(layers, heads, -1), jnp.stack(ups), jnp.stack(downs)
        )
    else:
        hidden_out = place_rows(spot, (), hidden_mine, hidden_recv, bf16)
        grad_input = place_rows(spot, (), row_mine, over_mp(row_send), f32)
        small = jnp.stack(
            [
                jnp.concatenate(
                    [ordered(side, bo[:2], bt[:2], 1), (vec + sums)[:6], up.reshape(-1, width)],
                    axis=0,
                )
                for bo, bt, vec, sums, up in smalls
            ]
        )
        small = lax.psum(small, ("dp", "mp"))
        grads = [
            jnp.stack([groups[kind, layer][k] for layer in range(layers)])
            for kind, k in (("att", 0), ("att", 1), ("ff", 0), ("ff", 1))
        ]
    grad_bias_qv = lax.dynamic_slice_in_dim(small[:, :2], side * cols, cols, 2)
    return (
        hidden_out,
        grad_input,
        grads[0],
        grad_bias_qv,
        grads[1],
        small[:, 2:6],
        small[:, 6:8],
        grads[2],
        small[:, 8:].reshape(layers, hidden),
        grads[3],
    )


def solution(mesh):
    return jax.shard_map(
        local,
        mesh=mesh,
        in_specs=(
            P("dp", "mp", None),
            P("dp", "mp", None),
            P("dp", None),
            P(),
            P(None, None, None, "mp"),
            P(None, None, "mp"),
            P(None, "mp", None),
            P(),
            P(),
            P(),
            P(),
            P(),
        ),
        out_specs=(
            P("dp", "mp", None),
            P("dp", "mp", None),
            P(None, "mp", "dp"),
            P(None, None, "mp"),
            P(None, "mp", "dp"),
            P(),
            P(),
            P(None, "dp"),
            P(),
            P(None, "dp"),
        ),
        check_vma=False,
    )
```

time: 580 us -> 461 us (0.79)
  local copies, waits for them, and re-layouts: 131 us -> 33.4 us
  Pallas kernels: 171 us -> 262 us
  waiting for transfers between devices: 178 us -> 103 us
  other arithmetic: 42.3 us -> 8.05 us
    pallas_call x14 -> x29, Pallas kernels: 171 us -> 262 us  [launch(): pl.pallas_call(kernel, grid_spec=pltpu.PrefetchScalarGridSpec(num_scalar_...]
    ppermute x14 -> x17, waiting for transfers between devices: 84.9 us -> 40 us  [over_mp(): return lax.ppermute(value, 'mp', [(0, 1), (1, 0)])]
    unnamed x280 -> x114, local copies, waits for them, and re-layouts: 62.6 us -> 22.7 us
    ppermute x42 -> x43, waiting for transfers between devices: 93.1 us -> 63.5 us  [over_bit(): lax.ppermute(value, 'dp', [(i, i ^ 1 << bit) for i in range(dp_count)])]
    squeeze x7 -> x0, local copies, waits for them, and re-layouts: 18.1 us -> none  [the longest x1 8.33 us: local(): w_up[layer]]
    convert_element_type x13 -> x1, other arithmetic: 13.6 us -> 0.83 us  [local(): seg_k = jnp.where(same, 0.0, 1.0).astype(bf16)]
    slice x12 -> x4, local copies, waits for them, and re-layouts: 13 us -> 1.22 us  [the longest x2 0.89 us: local(): outs.append(rows[share:].reshape(heads, 2, 4, cols))]
    squeeze x11 -> x1, local copies, waits for them, and re-layouts: 10.6 us -> 1.03 us  [pick(): return lax.dynamic_index_in_dim(value, index, axis, keepdims=False)]
  transfers between devices with their start and end apart: 56 -> 60, of which waited for: 20 -> 18; matrix products, arithmetic and copies ran while one was open for 18% -> 3% of each run, Pallas kernels for 12% -> 46%
where the time goes in v2:
time: 461 us; the launch traced here: 452 us
  Pallas kernels  262 us (57%)
  waiting for transfers between devices  103 us (22%)
  starting transfers between devices  43.5 us (9%)
  local copies, waits for them, and re-layouts  33.4 us (7%)
  other arithmetic  8.05 us (2%)
    pallas_call x29, Pallas kernels, launch(): pl.pallas_call(kernel, grid_spec=pltpu.PrefetchScalarGridSpec(num_scalar_...  262 us
    ppermute x43, waiting for transfers between devices, over_bit(): lax.ppermute(value, 'dp', [(i, i ^ 1 << bit) for i in range(dp_count)])  63.5 us
    ppermute x17, waiting for transfers between devices, over_mp(): return lax.ppermute(value, 'mp', [(0, 1), (1, 0)])  40 us
    ppermute x43, starting transfers between devices, over_bit(): lax.ppermute(value, 'dp', [(i, i ^ 1 << bit) for i in range(dp_count)])  23.7 us
    unnamed x114, local copies, waits for them, and re-layouts  22.7 us
    ppermute x17, starting transfers between devices, over_mp(): return lax.ppermute(value, 'mp', [(0, 1), (1, 0)])  19.8 us
  transfers between devices with their start and end apart: 60, of which 18 were waited for; matrix products, arithmetic and copies ran while one was open for 3% of the time, Pallas kernels for 46%

profile of v2, /device:TPU:0, one launch (start us, length us, event | category | flops | bytes accessed | tf_op | source)
XLA Modules:
  0.0 451.8 jit_solution(10140151490373637903)
XLA Ops:
  1.7 3.0 collective-permute-start
  5.4 3.1 pick_weights.1
  10.0 4.7 %collective-permute-done.refs_2_ = bf16[256,768]{1,0:T(8,128)(2,1)S(1)} collective-permute-done((bf16[256,768]{1,0:T(8,128)(2,1)S(1)}, bf16[256,768]{1,0:T(8,128)(2,1)S(1)}, u32[]{:S(2)}, u32[]{:S(2)}) %collective-permute-start) | collective-permute-done | bytes 393248 | tf_op jit(solution)/shard_map/ppermute | solution.py:1134
  15.4 3.0 enter.1.refs_0_
  18.4 8.0 %attn_fwd.4 = (bf16[512,384]{1,0:T(8,128)(2,1)}, bf16[512,384]{1,0:T(8,128)(2,1)}, bf16[512,384]{1,0:T(8,128)(2,1)}, f32[512,384]{1,0:T(8,128)}, f32[3,8,512]{2,1,0:T(8,128)}) custom-call(s32[5]{0:T(128)} %stack.35.spot_ref, bf16[512,768]{1,0:T(8,128)(2,1)} %enter.1.refs_0_, bf16[2,3,768,384]{3,2,1,0:T(8,128)(2,1)} %refs_18_.3, f32[2,2,384]{2,1,0:T(2,128)} %refs_2_.3, ...), custom_call_target="tpu_custom_call" | custom-call | flops 8000000000 | bytes 8000000 | tf_op jit(solution)/shard_map/attn_fwd/pallas_call | solution.py:58
  26.4 6.4 %collective-permute-done.1.refs_0_.refs_1_.refs_19_ = bf16[3,384,384]{2,1,0:T(8,128)(2,1)S(1)} collective-permute-done((bf16[3,384,384]{2,1,0:T(8,128)(2,1)}, bf16[3,384,384]{2,1,0:T(8,128)(2,1)S(1)}, u32[]{:S(2)}, u32[]{:S(2)}) %collective-permute-start.1) | collective-permute-done | bytes 884768 | tf_op jit(solution)/shard_map/ppermute | solution.py:1134
  33.7 3.7 relay.1.refs_9_
  37.4 1.7 collective-permute-start.4
  39.5 7.5 %collective-permute-done.3.refs_3_ = f32[2,2,384]{2,1,0:T(2,128)S(1)} collective-permute-done((f32[2,2,384]{2,1,0:T(2,128)S(1)}, f32[2,2,384]{2,1,0:T(2,128)S(1)}, u32[]{:S(2)}, u32[]{:S(2)}) %collective-permute-start.3) | collective-permute-done | bytes 6176 | tf_op jit(solution)/shard_map/ppermute | solution.py:1134
  48.7 9.0 %attn_fwd.5 = (bf16[512,384]{1,0:T(8,128)(2,1)}, bf16[512,384]{1,0:T(8,128)(2,1)}, bf16[512,384]{1,0:T(8,128)(2,1)}, f32[512,384]{1,0:T(8,128)}, f32[3,8,512]{2,...) custom-call(s32[5]{0:T(128)} %stack.35.spot_ref, ...), custom_call_target="tpu_custom_call" | custom-call | flops 8000000000 | bytes 8000000 | tf_op jit(solution)/shard_map/attn_fwd/pallas_call | solution.py:58
  57.7 1.8 collective-permute-start.6
  60.2 21.3 %ff_fwd.2 = (bf16[512,1536]{1,0:T(8,128)(2,1)}, f32[512,768]{1,0:T(8,128)}, f32[512,128]{1,0:T(8,128)}, bf16[512,3072]{1,0:T(8,128)(2,1)}, bf16[512,3072]{1,0:T(...) custom-call(s32[5]{0:T(128)} %stack.35.spot_ref, ...), custom_call_target="tpu_custom_call" | custom-call | flops 20999999488 | bytes 21000000 | tf_op jit(solution)/shard_map/ff_fwd/pallas_call | solution.py:58
  82.1 1.7 collective-permute-start.7
  83.8 7.6 %collective-permute-done.7.refs_6_.refs_11_ = bf16[384,384]{1,0:T(8,128)(2,1)S(1)} collective-permute-done((bf16[384,384]{1,0:T(8,128)(2,1)}, bf16[384,384]{1,0:T(8,128)(2,1)S(1)}, u32[]{:S(2)}, u32[]{:S(2)}) %collective-permute-start.7) | collective-permute-done | bytes 294944 | tf_op jit(solution)/shard_map/ppermute | solution.py:1134
  93.1 8.5 %attn_fwd.6 = (bf16[512,384]{1,0:T(8,128)(2,1)}, bf16[512,384]{1,0:T(8,128)(2,1)}, bf16[512,384]{1,0:T(8,128)(2,1)}, f32[512,384]{1,0:T(8,128)}, f32[3,8,512]{2,...) custom-call(s32[5]{0:T(128)} %stack.35.spot_ref, ...), custom_call_target="tpu_custom_call" | custom-call | flops 8000000000 | bytes 8000000 | tf_op jit(solution)/shard_map/attn_fwd/pallas_call | solution.py:58
  102.2 2.5 collective-permute-done.8.refs_2_.refs_20_
  104.7 1.7 collective-permute-start.10
  106.4 8.5 %attn_fwd.7 = (bf16[512,384]{1,0:T(8,128)(2,1)}, bf16[512,384]{1,0:T(8,128)(2,1)}, bf16[512,384]{1,0:T(8,128)(2,1)}, f32[512,384]{1,0:T(8,128)}, f32[3,8,512]{2,1,0:T(8,128)}) custom-call(s32[5]{0:T(128)} %stack.35.spot_ref, bf16[512,768]{1,0:T(8,128)(2,1)} %get-tuple-element.194.refs_0_, bf16[3,384,384]{2,1,0:T(8,128)(2,1)} %copy-done.12, ...), custom_call_target="tpu_custom_call" | custom-call | flops 8000000000 | bytes 8000000 | tf_op jit(solution)/shard_map/attn_fwd/pallas_call | solution.py:58
  116.2 1.7 copy-done.6
  117.9 22.3 %ff_fwd.3 = (bf16[512,1536]{1,0:T(8,128)(2,1)}, f32[512,768]{1,0:T(8,128)}, f32[512,128]{1,0:T(8,128)}, bf16[512,3072]{1,0:T(8,128)(2,1)}, bf16[512,3072]{1,0:T(...) custom-call(s32[5]{0:T(128)} %stack.35.spot_ref, ...), custom_call_target="tpu_custom_call" | custom-call | flops 20999999488 | bytes 21000000 | tf_op jit(solution)/shard_map/ff_fwd/pallas_call | solution.py:58
  140.9 1.7 collective-permute-start.14
  143.1 17.9 %ff_bwd.2 = (bf16[512,1536]{1,0:T(8,128)(2,1)}, bf16[512,384]{1,0:T(8,128)(2,1)}, bf16[512,384]{1,0:T(8,128)(2,1)}, f32[512,768]{1,0:T(8,128)}, bf16[512,384]{1,...) custom-call(s32[5]{0:T(128)} %stack.35.spot_ref, ...), custom_call_target="tpu_custom_call" | custom-call | flops 20000000000 | bytes 20000000 | tf_op jit(solution)/shard_map/ff_bwd/pallas_call | solution.py:58
  161.1 2.7 place_rows.2.refs_9_
  165.7 16.3 %w_ff.2 = (bf16[8,144,384]{2,1,0:T(8,128)(2,1)}, bf16[1152,384]{1,0:T(8,128)(2,1)}, bf16[8,128,384]{2,1,0:T(8,128)(2,1)}, bf16[1024,384]{1,0:T(8,128)(2,1)}, bf1...) custom-call(s32[5]{0:T(128)} %stack.35.spot_ref, bf16[512,1536]{1,0:T(8,128)(2,1)} %get-tuple-element.214.refs_15_.refs_0_.refs_7_, ...), custom_call_target="tpu_custom_call" | custom-call | flops 13500000256 | bytes 13500000 | tf_op jit(solution)/shard_map/w_ff/pallas_call | solution.py:58
  182.0 1.5 collective-permute-start.19
  184.0 1.6 collective-permute-start.21
  185.6 21.1 %attn_bwd.2 = (bf16[512,384]{1,0:T(8,128)(2,1)}, bf16[512,384]{1,0:T(8,128)(2,1)}, bf16[512,384]{1,0:T(8,128)(2,1)}, bf16[512,384]{1,0:T(8,128)(2,1)}, bf16[512,...) custom-call(s32[5]{0:T(128)} %stack.35.spot_ref, ...), custom_call_target="tpu_custom_call" | custom-call | flops 18499999744 | bytes 18500000 | tf_op jit(solution)/shard_map/attn_bwd/pallas_call | solution.py:58
  206.7 8.2 %w_att.2 = (bf16[2,8,144,384]{3,2,1,0:T(8,128)(2,1)}, bf16[2,8,48,384]{3,2,1,0:T(8,128)(2,1)}, bf16[2,8,48,384]{3,2,1,0:T(8,128)(2,1)}, bf16[2,8,48,384]{3,2,1,0:T(8,128)(2,1)}, bf16[2,8,48,384]{3,2,1,0:T(8,128)(2,1)}) custom-call(s32[5]{0:T(128)} %stack.35.spot_ref, bf16[512,768]{1,0:T(8,128)(2,1)} %get-tuple-element.194.refs_0_, ...), custom_call_target="tpu_custom_call" | custom-call | flops 8000000000 | bytes 8000000 | tf_op jit(solution)/shard_map/w_att/pallas_call | solution.py:58
  216.8 5.0 %exchange.8 = (bf16[4,144,384]{2,1,0:T(8,128)(2,1)}, bf16[4,128,384]{2,1,0:T(8,128)(2,1)}, bf16[4,112,384]{2,1,0:T(8,128)(2,1)}, bf16[512,768]{1,0:T(8,128)(2,1)...) custom-call(s32[5]{0:T(128)} %stack.35.spot_ref, ...), custom_call_target="tpu_custom_call" | custom-call | flops 5000000000 | bytes 5000000 | tf_op jit(solution)/shard_map/exchange/pallas_call | solution.py:58
  221.8 1.5 collective-permute-start.23
  224.3 18.0 %ff_bwd.3 = (bf16[512,1536]{1,0:T(8,128)(2,1)}, bf16[512,384]{1,0:T(8,128)(2,1)}, bf16[512,384]{1,0:T(8,128)(2,1)}, f32[512,768]{1,0:T(8,128)}, bf16[512,384]{1,...) custom-call(s32[5]{0:T(128)} %stack.35.spot_ref, ...), custom_call_target="tpu_custom_call" | custom-call | flops 20000000000 | bytes 20000000 | tf_op jit(solution)/shard_map/ff_bwd/pallas_call | solution.py:58
  243.8 5.9 %exchange.9 = (bf16[2,144,384]{2,1,0:T(8,128)(2,1)}, bf16[2,128,384]{2,1,0:T(8,128)(2,1)}, bf16[2,112,384]{2,1,0:T(8,128)(2,1)}, bf16[8,96,384]{2,1,0:T(8,128)(2...) custom-call(s32[5]{0:T(128)} %stack.35.spot_ref, ...), custom_call_target="tpu_custom_call" | custom-call | flops 5000000000 | bytes 5000000 | tf_op jit(solution)/shard_map/exchange/pallas_call | solution.py:58
  249.7 1.6 collective-permute-start.29
  251.3 1.5 collective-permute-start.30
  254.2 16.7 %w_ff.3 = (bf16[8,144,384]{2,1,0:T(8,128)(2,1)}, bf16[1152,384]{1,0:T(8,128)(2,1)}, bf16[8,128,384]{2,1,0:T(8,128)(2,1)}, bf16[1024,384]{1,0:T(8,128)(2,1)}, bf1...) custom-call(s32[5]{0:T(128)} %stack.35.spot_ref, bf16[512,1536]{1,0:T(8,128)(2,1)} %get-tuple-element.197.refs_8_.refs_0_.refs_7_, ...), custom_call_target="tpu_custom_call" | custom-call | flops 13500000256 | bytes 13500000 | tf_op jit(solution)/shard_map/w_ff/pallas_call | solution.py:58
  272.1 1.5 collective-permute-start.36
  275.0 3.2 exchange.10
  278.2 2.6 collective-permute-start.34
  280.8 18.5 %attn_bwd.3 = (bf16[512,384]{1,0:T(8,128)(2,1)}, bf16[512,384]{1,0:T(8,128)(2,1)}, bf16[512,384]{1,0:T(8,128)(2,1)}, bf16[512,384]{1,0:T(8,128)(2,1)}, bf16[512,...) custom-call(s32[5]{0:T(128)} %stack.35.spot_ref, ...), custom_call_target="tpu_custom_call" | custom-call | flops 18499999744 | bytes 18500000 | tf_op jit(solution)/shard_map/attn_bwd/pallas_call | solution.py:58
  299.3 8.2 %w_att.3 = (bf16[2,8,144,384]{3,2,1,0:T(8,128)(2,1)}, bf16[2,8,48,384]{3,2,1,0:T(8,128)(2,1)}, bf16[2,8,48,384]{3,2,1,0:T(8,128)(2,1)}, bf16[2,8,48,384]{3,2,1,0:T(8,128)(2,1)}, bf16[2,8,48,384]{3,2,1,0:T(8,128)(2,1)}) custom-call(s32[5]{0:T(128)} %stack.35.spot_ref, bf16[512,768]{1,0:T(8,128)(2,1)} %enter.1.refs_0_, ...), custom_call_target="tpu_custom_call" | custom-call | flops 8000000000 | bytes 8000000 | tf_op jit(solution)/shard_map/w_att/pallas_call | solution.py:58
  308.1 1.6 collective-permute-done.39.refs_16_
  309.7 1.7 collective-permute-done.40.refs_17_
  312.2 9.0 %exchange.11 = (f32[144,384]{1,0:T(8,128)}, f32[128,384]{1,0:T(8,128)}, f32[112,384]{1,0:T(8,128)}, bf16[4,144,384]{2,1,0:T(8,128)(2,1)}, bf16[4,128,384]{2,1,0:...) custom-call(s32[5]{0:T(128)} %stack.35.spot_ref, ...), custom_call_target="tpu_custom_call" | custom-call | flops 5000000000 | bytes 5000000 | tf_op jit(solution)/shard_map/exchange/pallas_call | solution.py:58
  323.2 1.6 collective-permute-start.43
  324.8 9.2 %collective-permute-done.43.refs_3_ = bf16[512,384]{1,0:T(8,128)(2,1)S(1)} collective-permute-done((bf16[512,384]{1,0:T(8,128)(2,1)}, bf16[512,384]{1,0:T(8,128)(2,1)S(1)}, u32[]{:S(2)}, u32[]{:S(2)}) %collective-permute-start.43) | collective-permute-done | bytes 393248 | tf_op jit(solution)/shard_map/ppermute | solution.py:1137
  334.1 16.7 %collective-permute-done.44.refs_5_ = bf16[1600,384]{1,0:T(8,128)(2,1)S(1)} collective-permute-done((bf16[1600,384]{1,0:T(8,128)(2,1)}, bf16[1600,384]{1,0:T(8,128)(2,1)S(1)}, u32[]{:S(2)}, u32[]{:S(2)}) %collective-permute-start.44) | collective-permute-done | bytes 1228832 | tf_op jit(solution)/shard_map/ppermute | solution.py:1137
  350.8 8.2 %collective-permute-done.42.refs_1_.refs_3_ = bf16[2112,384]{1,0:T(8,128)(2,1)S(1)} collective-permute-done((bf16[2112,384]{1,0:T(8,128)(2,1)}, bf16[2112,384]{1,0:T(8,128)(2,1)S(1)}, u32[]{:S(2)}, u32[]{:S(2)}) %collective-permute-start.42) | collective-permute-done | bytes 1622048 | tf_op jit(solution)/shard_map/ppermute | solution.py:1134
  360.1 5.2 %exchange.12 = (bf16[2,144,384]{2,1,0:T(8,128)(2,1)}, bf16[2,128,384]{2,1,0:T(8,128)(2,1)}, bf16[2,112,384]{2,1,0:T(8,128)(2,1)}, bf16[2,96,384]{2,1,0:T(8,128)(...) custom-call(s32[5]{0:T(128)} %stack.35.spot_ref, ...), custom_call_target="tpu_custom_call" | custom-call | flops 5000000000 | bytes 5000000 | tf_op jit(solution)/shard_map/exchange/pallas_call | solution.py:58
  365.3 1.6 collective-permute-start.45
  366.9 1.5 collective-permute-start.46
  369.4 11.9 %collective-permute-done.48.refs_11_ = f32[2,12,768]{2,1,0:T(8,128)S(1)} collective-permute-done((f32[2,12,768]{2,1,0:T(8,128)S(1)}, f32[2,12,768]{2,1,0:T(8,128)S(1)}, u32[]{:S(2)}, u32[]{:S(2)}) %collective-permute-start.48) | collective-permute-done | bytes 73760 | tf_op jit(solution)/shard_map/ppermute | solution.py:1137
  382.5 3.7 exchange.13
  387.3 4.4 collective-permute-done.51.refs_10_
  391.7 9.1 %collective-permute-done.50.refs_7_ = bf16[384,384]{1,0:T(8,128)(2,1)S(1)} collective-permute-done((bf16[384,384]{1,0:T(8,128)(2,1)}, bf16[384,384]{1,0:T(8,128)(2,1)S(1)}, u32[]{:S(2)}, u32[]{:S(2)}) %collective-permute-start.50) | collective-permute-done | bytes 294944 | tf_op jit(solution)/shard_map/ppermute | solution.py:1137
  400.9 5.9 %collective-permute-done.49.refs_1_ = bf16[576,384]{1,0:T(8,128)(2,1)S(1)} collective-permute-done((bf16[576,384]{1,0:T(8,128)(2,1)}, bf16[576,384]{1,0:T(8,128)(2,1)S(1)}, u32[]{:S(2)}, u32[]{:S(2)}) %collective-permute-start.49) | collective-permute-done | bytes 442400 | tf_op jit(solution)/shard_map/ppermute | solution.py:1137
  407.6 3.3 exchange.14
  414.8 1.6 collective-permute-start.57
  416.4 3.0 collective-permute-done.53.refs_4_
  420.1 2.5 exchange.15
  426.5 3.1 place_rows.3.refs_4_
  430.7 1.5 collective-permute-done.54
  433.0 3.0 finish_ff.2
  436.0 3.1 finish_ff.3
  448.4 3.2 pad_maximum_fusion
  (243 shorter events, 51.8 us)
Async XLA Ops:
  1.7 13.0 %collective-permute-start = (bf16[256,768]{1,0:T(8,128)(2,1)S(1)}, bf16[256,768]{1,0:T(8,128)(2,1)S(1)}, u32[]{:S(2)}, u32[]{:S(2)}) collective-permute-start(bf16[256,768]{1,0:T(8,128)(2,1)S(1)} %dynamic-slice_bitcast_fusion), channel_id=1, source_target_pairs={{0,1},{1,0},{2,3},{3,2},{4,5},{5,4},{6,7},{7,6},{8,9},{9,8},{10,11... | collective-permute-start | bytes 1179656 | tf_op jit(solution)/shard_map/ppermute | solution.py:1134
  8.5 24.3 %collective-permute-start.1 = (bf16[3,384,384]{2,1,0:T(8,128)(2,1)}, bf16[3,384,384]{2,1,0:T(8,128)(2,1)S(1)}, u32[]{:S(2)}, u32[]{:S(2)}) collective-permute-start(bf16[3,384,384]{2,1,0:T(8,128)(2,1)} %get-tuple-element.186.refs_3_), channel_id=1, source_target_pairs={{0,1},{1,0},{2,3},{3,2},{4,5},{5,4},{6,7},{7,6},{8,9},{9,8},{10,11... | collective-permute-start | bytes 2654216 | tf_op jit(solution)/shard_map/ppermute | solution.py:1134
  37.4 9.6 %collective-permute-start.2 = (bf16[3,384,384]{2,1,0:T(8,128)(2,1)}, bf16[3,384,384]{2,1,0:T(8,128)(2,1)S(1)}, u32[]{:S(2)}, u32[]{:S(2)}) collective-permute-start(bf16[3,384,384]{2,1,0:T(8,128)(2,1)} %relay.1.refs_9_), channel_id=1, source_target_pairs={{0,2},{2,0},{4,6},{6,4},{8,10},{10,8},{12,14},{14,12},{16,18},{18,... | collective-permute-start | bytes 2654216 | tf_op jit(solution)/shard_map/ppermute | solution.py:1137
  37.4 9.6 %collective-permute-start.4 = (bf16[384,384]{1,0:T(8,128)(2,1)S(1)}, bf16[384,384]{1,0:T(8,128)(2,1)S(1)}, u32[]{:S(2)}, u32[]{:S(2)}) collective-permute-start(bf16[384,384]{1,0:T(8,128)(2,1)S(1)} %copy-done.45), channel_id=1, source_target_pairs={{0,1},{1,0},{2,3},{3,2},{4,5},{5,4},{6,7},{7,6},{8,9},{9,8},{10,11... | collective-permute-start | bytes 884744 | tf_op jit(solution)/shard_map/ppermute | solution.py:1134
  39.2 7.8 %collective-permute-start.3 = (f32[2,2,384]{2,1,0:T(2,128)S(1)}, f32[2,2,384]{2,1,0:T(2,128)S(1)}, u32[]{:S(2)}, u32[]{:S(2)}) collective-permute-start(f32[2,2,384]{2,1,0:T(2,128)S(1)} %copy-done.53), channel_id=1, source_target_pairs={{0,1},{1,0},{2,3},{3,2},{4,5},{5,4},{6,7},{7,6},{8,9},{9,8},{10,11... | collective-permute-start | bytes 18440 | tf_op jit(solution)/shard_map/ppermute | solution.py:1134
  57.6 1.9 collective-permute-start.5
  57.7 33.7 %collective-permute-start.6 = (bf16[3,384,384]{2,1,0:T(8,128)(2,1)}, bf16[3,384,384]{2,1,0:T(8,128)(2,1)S(1)}, u32[]{:S(2)}, u32[]{:S(2)}) collective-permute-start(bf16[3,384,384]{2,1,0:T(8,128)(2,1)} %get-tuple-element.195), channel_id=1, source_target_pairs={{0,1},{1,0},{2,3},{3,2},{4,5},{5,4},{6,7},{7,6},{8,9},{9,8},{10,11... | collective-permute-start | bytes 2654216 | tf_op jit(solution)/shard_map/ppermute | solution.py:1134
  81.5 34.7 %collective-permute-start.12 = (bf16[512,3072]{1,0:T(8,128)(2,1)}, bf16[512,3072]{1,0:T(8,128)(2,1)S(1)}, u32[]{:S(2)}, u32[]{:S(2)}) collective-permute-start(bf16[512,3072]{1,0:T(8,128)(2,1)} %get-tuple-element.204.refs_4_), channel_id=1, source_target_pairs={{0,2},{2,0},{4,6},{6,4},{8,10},{10,8},{12,14},{14,12},{16,18},{18,... | collective-permute-start | bytes 9437192 | tf_op jit(solution)/shard_map/ppermute | solution.py:1137
  81.8 34.4 %collective-permute-start.13 = (bf16[512,3072]{1,0:T(8,128)(2,1)}, bf16[512,3072]{1,0:T(8,128)(2,1)}, u32[]{:S(2)}, u32[]{:S(2)}) collective-permute-start(bf16[512,3072]{1,0:T(8,128)(2,1)} %get-tuple-element.205.refs_7_), channel_id=1, source_target_pairs={{0,2},{2,0},{4,6},{6,4},{8,10},{10,8},{12,14},{14,12},{16,18},{18,... | collective-permute-start | bytes 9437192 | tf_op jit(solution)/shard_map/ppermute | solution.py:1137
  82.1 9.3 %collective-permute-start.7 = (bf16[384,384]{1,0:T(8,128)(2,1)}, bf16[384,384]{1,0:T(8,128)(2,1)S(1)}, u32[]{:S(2)}, u32[]{:S(2)}) collective-permute-start(bf16[384,384]{1,0:T(8,128)(2,1)} %get-tuple-element.196), channel_id=1, source_target_pairs={{0,1},{1,0},{2,3},{3,2},{4,5},{5,4},{6,7},{7,6},{8,9},{9,8},{10,11... | collective-permute-start | bytes 884744 | tf_op jit(solution)/shard_map/ppermute | solution.py:1134
  101.6 3.2 collective-permute-start.8
  101.6 14.6 %collective-permute-start.11 = (bf16[512,1536]{1,0:T(8,128)(2,1)}, bf16[512,1536]{1,0:T(8,128)(2,1)}, u32[]{:S(2)}, u32[]{:S(2)}) collective-permute-start(bf16[512,1536]{1,0:T(8,128)(2,1)} %get-tuple-element.197.refs_8_.refs_0_.refs_7_), channel_id=1, source_target_pairs={{0,2},{2,0},{4,6},{6,4},{8,10},{10,8},{12,14},{14,12},{16,18},{18,... | collective-permute-start | bytes 4718600 | tf_op jit(solution)/shard_map/ppermute | solution.py:1137
  102.1 12.9 %collective-permute-start.9 = (bf16[384,384]{1,0:T(8,128)(2,1)}, bf16[384,384]{1,0:T(8,128)(2,1)}, u32[]{:S(2)}, u32[]{:S(2)}) collective-permute-start(bf16[384,384]{1,0:T(8,128)(2,1)} %get-tuple-element.202), channel_id=1, source_target_pairs={{0,2},{2,0},{4,6},{6,4},{8,10},{10,8},{12,14},{14,12},{16,18},{18,... | collective-permute-start | bytes 884744 | tf_op jit(solution)/shard_map/ppermute | solution.py:1137
  104.7 11.5 %collective-permute-start.10 = (bf16[256,768]{1,0:T(8,128)(2,1)}, bf16[256,768]{1,0:T(8,128)(2,1)}, u32[]{:S(2)}, u32[]{:S(2)}) collective-permute-start(bf16[256,768]{1,0:T(8,128)(2,1)} %get-tuple-element.203), channel_id=1, source_target_pairs={{0,1},{1,0},{2,3},{3,2},{4,5},{5,4},{6,7},{7,6},{8,9},{9,8},{10,11... | collective-permute-start | bytes 1179656 | tf_op jit(solution)/shard_map/ppermute | solution.py:1134
  140.3 23.5 %collective-permute-start.16 = (bf16[512,3072]{1,0:T(8,128)(2,1)}, bf16[512,3072]{1,0:T(8,128)(2,1)S(1)}, u32[]{:S(2)}, u32[]{:S(2)}) collective-permute-start(bf16[512,3072]{1,0:T(8,128)(2,1)} %get-tuple-element.213.refs_7_), channel_id=1, source_target_pairs={{0,2},{2,0},{4,6},{6,4},{8,10},{10,8},{12,14},{14,12},{16,18},{18,... | collective-permute-start | bytes 9437192 | tf_op jit(solution)/shard_map/ppermute | solution.py:1137
  140.4 23.4 %collective-permute-start.17 = (bf16[512,3072]{1,0:T(8,128)(2,1)}, bf16[512,3072]{1,0:T(8,128)(2,1)}, u32[]{:S(2)}, u32[]{:S(2)}) collective-permute-start(bf16[512,3072]{1,0:T(8,128)(2,1)} %get-tuple-element.227.refs_4_), channel_id=1, source_target_pairs={{0,2},{2,0},{4,6},{6,4},{8,10},{10,8},{12,14},{14,12},{16,18},{18,... | collective-permute-start | bytes 9437192 | tf_op jit(solution)/shard_map/ppermute | solution.py:1137
  140.9 20.1 %collective-permute-start.14 = (bf16[256,768]{1,0:T(8,128)(2,1)}, bf16[256,768]{1,0:T(8,128)(2,1)}, u32[]{:S(2)}, u32[]{:S(2)}) collective-permute-start(bf16[256,768]{1,0:T(8,128)(2,1)} %get-tuple-element.208), channel_id=1, source_target_pairs={{0,1},{1,0},{2,3},{3,2},{4,5},{5,4},{6,7},{7,6},{8,9},{9,8},{10,11... | collective-permute-start | bytes 1179656 | tf_op jit(solution)/shard_map/ppermute | solution.py:1134
  142.6 21.2 %collective-permute-start.15 = (bf16[512,1536]{1,0:T(8,128)(2,1)}, bf16[512,1536]{1,0:T(8,128)(2,1)}, u32[]{:S(2)}, u32[]{:S(2)}) collective-permute-start(bf16[512,1536]{1,0:T(8,128)(2,1)} %get-tuple-element.214.refs_15_.refs_0_.refs_7_), channel_id=1, source_target_pairs={{0,2},{2,0},{4,6},{6,4},{8,10},{10,8},{12,14},{14,12},{16,18},{18,... | collective-permute-start | bytes 4718600 | tf_op jit(solution)/shard_map/ppermute | solution.py:1137
  142.6 21.2 %collective-permute-start.18 = (bf16[512,768]{1,0:T(8,128)(2,1)}, bf16[512,768]{1,0:T(8,128)(2,1)S(1)}, u32[]{:S(2)}, u32[]{:S(2)}) collective-permute-start(bf16[512,768]{1,0:T(8,128)(2,1)} %get-tuple-element.210.refs_2_.refs_6_), channel_id=1, source_target_pairs={{0,2},{2,0},{4,6},{6,4},{8,10},{10,8},{12,14},{14,12},{16,18},{18,... | collective-permute-start | bytes 2359304 | tf_op jit(solution)/shard_map/ppermute | solution.py:1137
  161.0 45.7 %collective-permute-start.22 = (bf16[512,384]{1,0:T(8,128)(2,1)}, bf16[512,384]{1,0:T(8,128)(2,1)}, u32[]{:S(2)}, u32[]{:S(2)}) collective-permute-start(bf16[512,384]{1,0:T(8,128)(2,1)} %get-tuple-element.245), channel_id=1, source_target_pairs={{0,2},{2,0},{4,6},{6,4},{8,10},{10,8},{12,14},{14,12},{16,18},{18,... | collective-permute-start | bytes 1179656 | tf_op jit(solution)/shard_map/ppermute | solution.py:1137
  182.0 33.4 %collective-permute-start.19 = (bf16[1152,384]{1,0:T(8,128)(2,1)}, bf16[1152,384]{1,0:T(8,128)(2,1)S(1)}, u32[]{:S(2)}, u32[]{:S(2)}) collective-permute-start(bf16[1152,384]{1,0:T(8,128)(2,1)} %get-tuple-element.233), channel_id=1, source_target_pairs={{0,4},{2,6},{4,0},{6,2},{8,12},{10,14},{12,8},{14,10},{16,20},{18,... | collective-permute-start | bytes 2654216 | tf_op jit(solution)/shard_map/ppermute | solution.py:1137
  183.5 32.0 %collective-permute-start.20 = (bf16[1024,384]{1,0:T(8,128)(2,1)}, bf16[1024,384]{1,0:T(8,128)(2,1)S(1)}, u32[]{:S(2)}, u32[]{:S(2)}) collective-permute-start(bf16[1024,384]{1,0:T(8,128)(2,1)} %get-tuple-element.235), channel_id=1, source_target_pairs={{0,1},{1,0},{2,3},{3,2},{4,5},{5,4},{6,7},{7,6},{8,9},{9,8},{10,11... | collective-permute-start | bytes 2359304 | tf_op jit(solution)/shard_map/ppermute | solution.py:1134
  184.0 31.4 %collective-permute-start.21 = (bf16[896,384]{1,0:T(8,128)(2,1)}, bf16[896,384]{1,0:T(8,128)(2,1)S(1)}, u32[]{:S(2)}, u32[]{:S(2)}) collective-permute-start(bf16[896,384]{1,0:T(8,128)(2,1)} %get-tuple-element.237), channel_id=1, source_target_pairs={{0,8},{2,10},{4,12},{6,14},{8,0},{10,2},{12,4},{14,6},{16,24},{18,... | collective-permute-start | bytes 2064392 | tf_op jit(solution)/shard_map/ppermute | solution.py:1137
  214.9 8.9 %collective-permute-start.26 = (bf16[2,8,48,384]{3,2,1,0:T(8,128)(2,1)}, bf16[2,8,48,384]{3,2,1,0:T(8,128)(2,1)S(1)}, u32[]{:S(2)}, u32[]{:S(2)}) collective-permute-start(bf16[2,8,48,384]{3,2,1,0:T(8,128)(2,1)} %get-tuple-element.263), channel_id=1, source_target_pairs={{0,2},{2,0},{4,6},{6,4},{8,10},{10,8},{12,14},{14,12},{16,18},{18,... | collective-permute-start | bytes 1769480 | tf_op jit(solution)/shard_map/ppermute | solution.py:1137
  214.9 9.4 %collective-permute-start.27 = (bf16[2,8,48,384]{3,2,1,0:T(8,128)(2,1)}, bf16[2,8,48,384]{3,2,1,0:T(8,128)(2,1)S(1)}, u32[]{:S(2)}, u32[]{:S(2)}) collective-permute-start(bf16[2,8,48,384]{3,2,1,0:T(8,128)(2,1)} %get-tuple-element.264), channel_id=1, source_target_pairs={{0,2},{2,0},{4,6},{6,4},{8,10},{10,8},{12,14},{14,12},{16,18},{18,... | collective-permute-start | bytes 1769480 | tf_op jit(solution)/shard_map/ppermute | solution.py:1137
  215.4 26.9 %collective-permute-start.28 = (bf16[2,8,48,384]{3,2,1,0:T(8,128)(2,1)}, bf16[2,8,48,384]{3,2,1,0:T(8,128)(2,1)}, u32[]{:S(2)}, u32[]{:S(2)}) collective-permute-start(bf16[2,8,48,384]{3,2,1,0:T(8,128)(2,1)} %get-tuple-element.265), channel_id=1, source_target_pairs={{0,2},{2,0},{4,6},{6,4},{8,10},{10,8},{12,14},{14,12},{16,18},{18,... | collective-permute-start | bytes 1769480 | tf_op jit(solution)/shard_map/ppermute | solution.py:1137
  221.8 21.0 %collective-permute-start.23 = (bf16[576,384]{1,0:T(8,128)(2,1)}, bf16[576,384]{1,0:T(8,128)(2,1)S(1)}, u32[]{:S(2)}, u32[]{:S(2)}) collective-permute-start(bf16[576,384]{1,0:T(8,128)(2,1)} %get-tuple-element.257), channel_id=1, source_target_pairs={{0,1},{1,0},{2,3},{3,2},{4,5},{5,4},{6,7},{7,6},{8,9},{9,8},{10,11... | collective-permute-start | bytes 1327112 | tf_op jit(solution)/shard_map/ppermute | solution.py:1134
  223.3 19.5 %collective-permute-start.24 = (bf16[512,384]{1,0:T(8,128)(2,1)}, bf16[512,384]{1,0:T(8,128)(2,1)S(1)}, u32[]{:S(2)}, u32[]{:S(2)}) collective-permute-start(bf16[512,384]{1,0:T(8,128)(2,1)} %get-tuple-element.259), channel_id=1, source_target_pairs={{0,8},{2,10},{4,12},{6,14},{8,0},{10,2},{12,4},{14,6},{16,24},{18,... | collective-permute-start | bytes 1179656 | tf_op jit(solution)/shard_map/ppermute | solution.py:1137
  223.7 18.5 %copy-start.24 = (bf16[2,8,48,384]{3,2,1,0:T(8,128)(2,1)}, bf16[2,8,48,384]{3,2,1,0:T(8,128)(2,1)S(1)}, u32[]{:S(2)}) copy-start(bf16[2,8,48,384]{3,2,1,0:T(8,128)(2,1)S(1)} %collective-permute-done.26.refs_8_) | copy-start | bytes 1769476
  223.7 19.0 %collective-permute-start.25 = (bf16[448,384]{1,0:T(8,128)(2,1)}, bf16[448,384]{1,0:T(8,128)(2,1)S(1)}, u32[]{:S(2)}, u32[]{:S(2)}) collective-permute-start(bf16[448,384]{1,0:T(8,128)(2,1)} %get-tuple-element.261), channel_id=1, source_target_pairs={{0,4},{2,6},{4,0},{6,2},{8,12},{10,14},{12,8},{14,10},{16,20},{18,... | collective-permute-start | bytes 1032200 | tf_op jit(solution)/shard_map/ppermute | solution.py:1137
  224.3 18.0 %copy-start.25 = (bf16[2,8,48,384]{3,2,1,0:T(8,128)(2,1)}, bf16[2,8,48,384]{3,2,1,0:T(8,128)(2,1)S(1)}, u32[]{:S(2)}) copy-start(bf16[2,8,48,384]{3,2,1,0:T(8,128)(2,1)S(1)} %collective-permute-done.27.refs_9_) | copy-start | bytes 1769476
  224.3 29.0 %collective-permute-start.32 = (bf16[512,768]{1,0:T(8,128)(2,1)}, bf16[512,768]{1,0:T(8,128)(2,1)S(1)}, u32[]{:S(2)}, u32[]{:S(2)}) collective-permute-start(bf16[512,768]{1,0:T(8,128)(2,1)} %get-tuple-element.273), channel_id=1, source_target_pairs={{0,2},{2,0},{4,6},{6,4},{8,10},{10,8},{12,14},{14,12},{16,18},{18,... | collective-permute-start | bytes 2359304 | tf_op jit(solution)/shard_map/ppermute | solution.py:1137
  242.3 57.0 %collective-permute-start.38 = (bf16[512,384]{1,0:T(8,128)(2,1)}, bf16[512,384]{1,0:T(8,128)(2,1)}, u32[]{:S(2)}, u32[]{:S(2)}) collective-permute-start(bf16[512,384]{1,0:T(8,128)(2,1)} %get-tuple-element.295), channel_id=1, source_target_pairs={{0,2},{2,0},{4,6},{6,4},{8,10},{10,8},{12,14},{14,12},{16,18},{18,... | collective-permute-start | bytes 1179656 | tf_op jit(solution)/shard_map/ppermute | solution.py:1137
  249.7 21.7 %collective-permute-start.29 = (bf16[288,384]{1,0:T(8,128)(2,1)}, bf16[288,384]{1,0:T(8,128)(2,1)S(1)}, u32[]{:S(2)}, u32[]{:S(2)}) collective-permute-start(bf16[288,384]{1,0:T(8,128)(2,1)} %get-tuple-element.268), channel_id=1, source_target_pairs={{0,8},{2,10},{4,12},{6,14},{8,0},{10,2},{12,4},{14,6},{16,24},{18,... | collective-permute-start | bytes 663560 | tf_op jit(solution)/shard_map/ppermute | solution.py:1137
  251.3 22.8 %collective-permute-start.30 = (bf16[1024,384]{1,0:T(8,128)(2,1)}, bf16[1024,384]{1,0:T(8,128)(2,1)S(1)}, u32[]{:S(2)}, u32[]{:S(2)}) collective-permute-start(bf16[1024,384]{1,0:T(8,128)(2,1)} %get-tuple-element.270), channel_id=1, source_target_pairs={{0,4},{2,6},{4,0},{6,2},{8,12},{10,14},{12,8},{14,10},{16,20},{18,... | collective-permute-start | bytes 2359304 | tf_op jit(solution)/shard_map/ppermute | solution.py:1137
  252.8 20.9 %collective-permute-start.31 = (bf16[992,384]{1,0:T(8,128)(2,1)}, bf16[992,384]{1,0:T(8,128)(2,1)S(1)}, u32[]{:S(2)}, u32[]{:S(2)}) collective-permute-start(bf16[992,384]{1,0:T(8,128)(2,1)} %get-tuple-element.272), channel_id=1, source_target_pairs={{0,1},{1,0},{2,3},{3,2},{4,5},{5,4},{6,7},{7,6},{8,9},{9,8},{10,11... | collective-permute-start | bytes 2285576 | tf_op jit(solution)/shard_map/ppermute | solution.py:1134
  270.9 37.2 %collective-permute-start.35 = (bf16[1152,384]{1,0:T(8,128)(2,1)}, bf16[1152,384]{1,0:T(8,128)(2,1)S(1)}, u32[]{:S(2)}, u32[]{:S(2)}) collective-permute-start(bf16[1152,384]{1,0:T(8,128)(2,1)} %get-tuple-element.281), channel_id=1, source_target_pairs={{0,4},{2,6},{4,0},{6,2},{8,12},{10,14},{12,8},{14,10},{16,20},{18,... | collective-permute-start | bytes 2654216 | tf_op jit(solution)/shard_map/ppermute | solution.py:1137
  272.1 36.0 %collective-permute-start.36 = (bf16[1024,384]{1,0:T(8,128)(2,1)}, bf16[1024,384]{1,0:T(8,128)(2,1)S(1)}, u32[]{:S(2)}, u32[]{:S(2)}) collective-permute-start(bf16[1024,384]{1,0:T(8,128)(2,1)} %get-tuple-element.283), channel_id=1, source_target_pairs={{0,1},{1,0},{2,3},{3,2},{4,5},{5,4},{6,7},{7,6},{8,9},{9,8},{10,11... | collective-permute-start | bytes 2359304 | tf_op jit(solution)/shard_map/ppermute | solution.py:1134
  273.6 33.8 %collective-permute-start.37 = (bf16[896,384]{1,0:T(8,128)(2,1)}, bf16[896,384]{1,0:T(8,128)(2,1)S(1)}, u32[]{:S(2)}, u32[]{:S(2)}) collective-permute-start(bf16[896,384]{1,0:T(8,128)(2,1)} %get-tuple-element.285), channel_id=1, source_target_pairs={{0,8},{2,10},{4,12},{6,14},{8,0},{10,2},{12,4},{14,6},{16,24},{18,... | collective-permute-start | bytes 2064392 | tf_op jit(solution)/shard_map/ppermute | solution.py:1137
  278.2 29.8 %collective-permute-start.34 = (bf16[384,384]{1,0:T(8,128)(2,1)}, bf16[384,384]{1,0:T(8,128)(2,1)}, u32[]{:S(2)}, u32[]{:S(2)}) collective-permute-start(bf16[384,384]{1,0:T(8,128)(2,1)} %get-tuple-element.278), channel_id=1, source_target_pairs={{0,16},{2,18},{4,20},{6,22},{8,24},{10,26},{12,28},{14,30},{16,0},... | collective-permute-start | bytes 884744 | tf_op jit(solution)/shard_map/ppermute | solution.py:1137
  307.5 2.2 collective-permute-start.39
  307.5 3.9 collective-permute-start.40
  308.0 3.5 collective-permute-start.41
  321.2 37.8 %collective-permute-start.42 = (bf16[2112,384]{1,0:T(8,128)(2,1)}, bf16[2112,384]{1,0:T(8,128)(2,1)S(1)}, u32[]{:S(2)}, u32[]{:S(2)}) collective-permute-start(bf16[2112,384]{1,0:T(8,128)(2,1)} %get-tuple-element.312), channel_id=1, source_target_pairs={{0,1},{1,0},{2,3},{3,2},{4,5},{5,4},{6,7},{7,6},{8,9},{9,8},{10,11... | collective-permute-start | bytes 4866056 | tf_op jit(solution)/shard_map/ppermute | solution.py:1134
  321.8 29.0 %collective-permute-start.44 = (bf16[1600,384]{1,0:T(8,128)(2,1)}, bf16[1600,384]{1,0:T(8,128)(2,1)S(1)}, u32[]{:S(2)}, u32[]{:S(2)}) collective-permute-start(bf16[1600,384]{1,0:T(8,128)(2,1)} %get-tuple-element.316), channel_id=1, source_target_pairs={{0,4},{2,6},{4,0},{6,2},{8,12},{10,14},{12,8},{14,10},{16,20},{18,... | collective-permute-start | bytes 3686408 | tf_op jit(solution)/shard_map/ppermute | solution.py:1137
  323.2 10.8 %collective-permute-start.43 = (bf16[512,384]{1,0:T(8,128)(2,1)}, bf16[512,384]{1,0:T(8,128)(2,1)S(1)}, u32[]{:S(2)}, u32[]{:S(2)}) collective-permute-start(bf16[512,384]{1,0:T(8,128)(2,1)} %get-tuple-element.314), channel_id=1, source_target_pairs={{0,8},{2,10},{4,12},{6,14},{8,0},{10,2},{12,4},{14,6},{16,24},{18,... | collective-permute-start | bytes 1179656 | tf_op jit(solution)/shard_map/ppermute | solution.py:1137
  334.1 24.9 %copy-start.37 = (bf16[512,384]{1,0:T(8,128)(2,1)}, bf16[512,384]{1,0:T(8,128)(2,1)S(1)}, u32[]{:S(2)}) copy-start(bf16[512,384]{1,0:T(8,128)(2,1)S(1)} %collective-permute-done.43.refs_3_) | copy-start | bytes 1179652
  365.3 16.1 %collective-permute-start.45 = (bf16[672,384]{1,0:T(8,128)(2,1)}, bf16[672,384]{1,0:T(8,128)(2,1)S(1)}, u32[]{:S(2)}, u32[]{:S(2)}) collective-permute-start(bf16[672,384]{1,0:T(8,128)(2,1)} %get-tuple-element.323), channel_id=1, source_target_pairs={{0,8},{2,10},{4,12},{6,14},{8,0},{10,2},{12,4},{14,6},{16,24},{18,... | collective-permute-start | bytes 1548296 | tf_op jit(solution)/shard_map/ppermute | solution.py:1137
  366.9 14.5 %collective-permute-start.46 = (bf16[640,384]{1,0:T(8,128)(2,1)}, bf16[640,384]{1,0:T(8,128)(2,1)S(1)}, u32[]{:S(2)}, u32[]{:S(2)}) collective-permute-start(bf16[640,384]{1,0:T(8,128)(2,1)} %get-tuple-element.325), channel_id=1, source_target_pairs={{0,4},{2,6},{4,0},{6,2},{8,12},{10,14},{12,8},{14,10},{16,20},{18,... | collective-permute-start | bytes 1474568 | tf_op jit(solution)/shard_map/ppermute | solution.py:1137
  368.4 13.0 %collective-permute-start.47 = (bf16[608,384]{1,0:T(8,128)(2,1)}, bf16[608,384]{1,0:T(8,128)(2,1)S(1)}, u32[]{:S(2)}, u32[]{:S(2)}) collective-permute-start(bf16[608,384]{1,0:T(8,128)(2,1)} %get-tuple-element.327), channel_id=1, source_target_pairs={{0,1},{1,0},{2,3},{3,2},{4,5},{5,4},{6,7},{7,6},{8,9},{9,8},{10,11... | collective-permute-start | bytes 1400840 | tf_op jit(solution)/shard_map/ppermute | solution.py:1134
  368.9 12.5 %collective-permute-start.48 = (f32[2,12,768]{2,1,0:T(8,128)S(1)}, f32[2,12,768]{2,1,0:T(8,128)S(1)}, u32[]{:S(2)}, u32[]{:S(2)}) collective-permute-start(f32[2,12,768]{2,1,0:T(8,128)S(1)} %copy-done.49), channel_id=1, source_target_pairs={{0,4},{2,6},{4,0},{6,2},{8,12},{10,14},{12,8},{14,10},{16,20},{18,... | collective-permute-start | bytes 221192 | tf_op jit(solution)/shard_map/ppermute | solution.py:1137
  386.2 20.6 %collective-permute-start.49 = (bf16[576,384]{1,0:T(8,128)(2,1)}, bf16[576,384]{1,0:T(8,128)(2,1)S(1)}, u32[]{:S(2)}, u32[]{:S(2)}) collective-permute-start(bf16[576,384]{1,0:T(8,128)(2,1)} %get-tuple-element.334), channel_id=1, source_target_pairs={{0,16},{2,18},{4,20},{6,22},{8,24},{10,26},{12,28},{14,30},{16,0},... | collective-permute-start | bytes 1327112 | tf_op jit(solution)/shard_map/ppermute | solution.py:1137
  386.5 14.4 %collective-permute-start.50 = (bf16[384,384]{1,0:T(8,128)(2,1)}, bf16[384,384]{1,0:T(8,128)(2,1)S(1)}, u32[]{:S(2)}, u32[]{:S(2)}) collective-permute-start(bf16[384,384]{1,0:T(8,128)(2,1)} %get-tuple-element.340), channel_id=1, source_target_pairs={{0,8},{2,10},{4,12},{6,14},{8,0},{10,2},{12,4},{14,6},{16,24},{18,... | collective-permute-start | bytes 884744 | tf_op jit(solution)/shard_map/ppermute | solution.py:1137
  386.9 4.8 %collective-permute-start.51 = (f32[2,12,768]{2,1,0:T(8,128)}, f32[2,12,768]{2,1,0:T(8,128)S(1)}, u32[]{:S(2)}, u32[]{:S(2)}) collective-permute-start(f32[2,12,768]{2,1,0:T(8,128)} %get-tuple-element.342.refs_9_), channel_id=1, source_target_pairs={{0,1},{1,0},{2,3},{3,2},{4,5},{5,4},{6,7},{7,6},{8,9},{9,8},{10,11... | collective-permute-start | bytes 221192 | tf_op jit(solution)/shard_map/ppermute | solution.py:1134
  391.7 15.0 %copy-start.51 = (f32[2,12,768]{2,1,0:T(8,128)}, f32[2,12,768]{2,1,0:T(8,128)S(1)}, u32[]{:S(2)}) copy-start(f32[2,12,768]{2,1,0:T(8,128)S(1)} %collective-permute-done.51.refs_10_) | copy-start | bytes 221188
  410.9 8.5 %collective-permute-start.52 = (bf16[192,384]{1,0:T(8,128)(2,1)}, bf16[192,384]{1,0:T(8,128)(2,1)S(1)}, u32[]{:S(2)}, u32[]{:S(2)}) collective-permute-start(bf16[192,384]{1,0:T(8,128)(2,1)} %get-tuple-element.344), channel_id=1, source_target_pairs={{0,16},{2,18},{4,20},{6,22},{8,24},{10,26},{12,28},{14,30},{16,0},... | collective-permute-start | bytes 442376 | tf_op jit(solution)/shard_map/ppermute | solution.py:1137
  411.0 14.8 %collective-permute-start.33 = (bf16[256,768]{1,0:T(8,128)(2,1)S(1)}, bf16[256,768]{1,0:T(8,128)(2,1)S(1)}, u32[]{:S(2)}, u32[]{:S(2)}) collective-permute-start(bf16[256,768]{1,0:T(8,128)(2,1)S(1)} %copy-done.34), channel_id=1, source_target_pairs={{0,1},{1,0},{2,3},{3,2},{4,5},{5,4},{6,7},{7,6},{8,9},{9,8},{10,11... | collective-permute-start | bytes 1179656 | tf_op jit(solution)/shard_map/ppermute | solution.py:1134
  411.6 7.8 %collective-permute-start.53 = (f32[2,12,768]{2,1,0:T(8,128)}, f32[2,12,768]{2,1,0:T(8,128)S(1)}, u32[]{:S(2)}, u32[]{:S(2)}) collective-permute-start(f32[2,12,768]{2,1,0:T(8,128)} %get-tuple-element.346.refs_3_), channel_id=1, source_target_pairs={{0,8},{2,10},{4,12},{6,14},{8,0},{10,2},{12,4},{14,6},{16,24},{18,... | collective-permute-start | bytes 221192 | tf_op jit(solution)/shard_map/ppermute | solution.py:1137
  414.8 17.5 %collective-permute-start.57 = (bf16[384,384]{1,0:T(8,128)(2,1)S(1)}, bf16[384,384]{1,0:T(8,128)(2,1)S(1)}, u32[]{:S(2)}, u32[]{:S(2)}) collective-permute-start(bf16[384,384]{1,0:T(8,128)(2,1)S(1)} %copy-done.41), channel_id=1, source_target_pairs={{0,1},{1,0},{2,3},{3,2},{4,5},{5,4},{6,7},{7,6},{8,9},{9,8},{10,11... | collective-permute-start | bytes 884744 | tf_op jit(solution)/shard_map/ppermute | solution.py:1134
  425.6 6.6 %collective-permute-start.54 = (f32[2,12,768]{2,1,0:T(8,128)S(1)}, f32[2,12,768]{2,1,0:T(8,128)S(1)}, u32[]{:S(2)}, u32[]{:S(2)}) collective-permute-start(f32[2,12,768]{2,1,0:T(8,128)S(1)} %copy-done.4), channel_id=1, source_target_pairs={{0,16},{2,18},{4,20},{6,22},{8,24},{10,26},{12,28},{14,30},{16,0},... | collective-permute-start | bytes 221192 | tf_op jit(solution)/shard_map/ppermute | solution.py:1137
  425.7 4.0 collective-permute-start.56
  432.2 7.4 %collective-permute-start.55 = (f32[2,12,768]{2,1,0:T(8,128)S(1)}, f32[2,12,768]{2,1,0:T(8,128)S(1)}, u32[]{:S(2)}, u32[]{:S(2)}) collective-permute-start(f32[2,12,768]{2,1,0:T(8,128)S(1)} %add.36), channel_id=1, source_target_pairs={{0,2},{2,0},{4,6},{6,4},{8,10},{10,8},{12,14},{14,12},{16,18},{18,... | collective-permute-start | bytes 221192 | tf_op jit(solution)/shard_map/ppermute | solution.py:1137
  439.1 3.0 collective-permute-start.59
  439.6 4.7 %collective-permute-start.58 = (bf16[384,384]{1,0:T(8,128)(2,1)S(1)}, bf16[384,384]{1,0:T(8,128)(2,1)S(1)}, u32[]{:S(2)}, u32[]{:S(2)}) collective-permute-start(bf16[384,384]{1,0:T(8,128)(2,1)S(1)} %copy-done.44), channel_id=1, source_target_pairs={{0,2},{2,0},{4,6},{6,4},{8,10},{10,8},{12,14},{14,12},{16,18},{18,... | collective-permute-start | bytes 884744 | tf_op jit(solution)/shard_map/ppermute | solution.py:1137
  (51 other events, 105.2 us)
